TPU v7x, 32 devices: a whole 2x2x4 slice. The times are simulated.
32 devices in a mesh: gx: 4 (over y, core), gy: 8 (over z, x).
Axes of the slice: x: 2, y: 2, z: 4, core: 2. Of those that a mesh axis runs over, the one named last changes fastest.
Arguments:
- adjoint_rhs: float32 [8, 8, 768, 128], P('gx', 'gy'), may hold values from -6 to 6
- local_inverse: bfloat16 [8, 8, 1024, 768], P('gx', 'gy')
- local_operator: bfloat16 [8, 8, 1024, 768], P('gx', 'gy')
- spill_rows: int32 [8, 8, 4, 64], P('gx', 'gy'), may hold values from 0 to 767, as said below
- coarse_basis: bfloat16 [8, 8, 64, 768], P('gx', 'gy'), may hold values from -3 to 3
- coarse_ids: int32 [8, 8, 64], P('gx', 'gy'), may hold values from 0 to 1023
- coarse_inverse: bfloat16 [1024, 1024], P(('gx', 'gy')), may hold values from -0.0008544922 to 0.0008544922
Outputs:
- adjoint_solution: float32 [8, 8, 768, 128], P('gx', 'gy')
- residual: float32 [8, 8, 768, 128], P('gx', 'gy')
Inputs may be any that keep to these rules, and one draw needn't show every extreme that they name: Each list of spill_rows holds 64 distinct rows. `coarse_ids`: A coarse function may be listed more than once for a subdomain.
All inputs are finite; a program needn't handle non-finite values.
Results may differ from a plain program's by a relative error of at most 0.0041.
Values may be sent and summed in bfloat16 or wider, within the bound.
No kernel may reach another device: no remote copies, remote signals or barrier semaphores. Data moves between devices by JAX's collectives and lax.ppermute only.
A program may use at most 64 MiB of HBM per device.

v0:
```python
import jax
import jax.numpy as jnp
from jax import lax
from jax.sharding import PartitionSpec as P


def with_halo(block, sides, width):
    for axis, dim in sides:
        count = lax.axis_size(axis)
        forward = [(i, i + 1) for i in range(count - 1)]
        backward = [(target, source) for source, target in forward]
        low = lax.ppermute(
            lax.slice_in_dim(block, block.shape[dim] - width, None, axis=dim), axis, forward
        )
        high = lax.ppermute(lax.slice_in_dim(block, 0, width, axis=dim), axis, backward)
        block = jnp.concatenate([low, block, high], axis=dim)
    return block


def add_rows(owned_rows, indices, values):
    return owned_rows.at[indices].add(values)


def spread(extended, indices):
    sub_count = extended.shape[0]
    group_rows = indices.shape[1] // 4
    owned_count = extended.shape[1] - 4 * group_rows
    owned_rows = extended[:, :owned_count]
    groups = extended[:, owned_count:].reshape(sub_count, 4, group_rows, extended.shape[2])
    outward = jnp.stack([groups[0, 0], groups[sub_count - 1, 1]])
    across = with_halo(outward, (("gx", 0),), 1)
    from_west = jnp.concatenate([across[0][None], groups[:-1, 1]], 0)
    from_east = jnp.concatenate([groups[1:, 0], across[3][None]], 0)
    vertical = jnp.stack([groups[:, 2], groups[:, 3]])
    beside = with_halo(vertical, (("gy", 0),), 1)
    received = jnp.stack([from_west, from_east, beside[0], beside[3]], 1).reshape(
        sub_count, 4 * group_rows, extended.shape[2]
    )
    return jax.vmap(add_rows)(owned_rows, indices, received)


def body(
    adjoint_rhs, local_inverse, local_operator, spill_rows, coarse_basis, coarse_ids, coarse_inverse
):
    highest = lax.Precision.HIGHEST
    contract_first = (((0,), (0,)), ((), ()))
    residual = adjoint_rhs[:, 0]
    inverses = local_inverse[:, 0]
    operators = local_operator[:, 0]
    indices = spill_rows[:, 0].reshape(spill_rows.shape[0], -1)
    basis_rows = coarse_basis[:, 0].astype(jnp.float32)
    sub_count = coarse_ids.shape[0]
    functions = coarse_ids.shape[2]
    coarse_order = coarse_inverse.shape[1]
    flat_ids = coarse_ids[:, 0].reshape(-1)
    one_hot = (flat_ids[None, :] == jnp.arange(coarse_order, dtype=jnp.int32)[:, None]).astype(
        jnp.float32
    )
    whole_inverse = lax.all_gather(coarse_inverse, ("gx", "gy"), axis=0, tiled=True)
    terms = jnp.einsum("skn,snr->skr", basis_rows, residual, precision=highest)
    local_sums = jnp.dot(
        one_hot, terms.reshape(sub_count * functions, terms.shape[2]), precision=highest
    )
    totals = lax.psum(local_sums, ("gx", "gy"))
    coarse_sol = lax.dot_general(
        whole_inverse,
        totals.astype(jnp.bfloat16),
        contract_first,
        preferred_element_type=jnp.float32,
    )
    local_sol = jnp.einsum(
        "sln,snr->slr", inverses, residual.astype(jnp.bfloat16), preferred_element_type=jnp.float32
    )
    picked = jnp.dot(one_hot.T, coarse_sol, precision=highest).reshape(
        sub_count, functions, coarse_sol.shape[1]
    )
    coarse_part = jnp.einsum("skn,skr->snr", basis_rows, picked, precision=highest)
    correction = spread(local_sol, indices) + coarse_part
    image = jnp.einsum(
        "sln,snr->slr",
        operators,
        correction.astype(jnp.bfloat16),
        preferred_element_type=jnp.float32,
    )
    residual = residual - spread(image, indices)
    return (correction[:, None], residual[:, None])


def solution(mesh):
    in_specs = (
        P("gx", "gy", None, None),
        P("gx", "gy", None, None),
        P("gx", "gy", None, None),
        P("gx", "gy", None, None),
        P("gx", "gy", None, None),
        P("gx", "gy", None),
        P(("gx", "gy"), None),
    )
    out_specs = (P("gx", "gy", None, None), P("gx", "gy", None, None))
    return jax.shard_map(body, mesh=mesh, in_specs=in_specs, out_specs=out_specs, check_vma=False)
```

profile of v0, /device:TPU:6, one launch (start us, length us, event | category | flops | bytes accessed | tf_op | source)
XLA Modules:
  0.0 223.9 jit_solution(3410227485739052414)
XLA Ops:
  7.3 0.7 all-gather.2.cloned.1.call-update
  7.9 1.1 copy-done
  9.1 2.1 fusion.2
  11.2 1.0 copy-done.1
  12.8 1.9 collective-permute-start
  14.7 3.6 %collective-permute-start.1 = (f32[1,64,128]{2,1,0:T(8,128)}, f32[1,64,128]{2,1,0:T(8,128)}, u32[]{:S(2)}, u32[]{:S(2)}) collective-permute-start(f32[1,64,128]{2,1,0:T(8,128)} %get-tuple-element.13), channel_id=1, source_target_pairs={{8,0},{16,8},{24,16},{9,1},{17,9},{25,17},{10,2},{18,10},{26,18},{... | collective-permute-start | bytes 98312 | tf_op jit(solution)/shard_map/ppermute | solution.py:15
  18.4 3.5 %collective-permute-start.2 = (f32[1,2,64,128]{3,2,1,0:T(8,128)S(1)}, f32[1,2,64,128]{3,2,1,0:T(8,128)}, u32[]{:S(2)}, u32[]{:S(2)}) collective-permute-start(f32[1,2,64,128]{3,2,1,0:T(8,128)S(1)} %get-tuple-element.16), channel_id=1, source_target_pairs={{0,1},{1,2},{2,3},{3,4},{4,5},{5,6},{6,7},{8,9},{9,10},{10,11},{11... | collective-permute-start | bytes 196616 | tf_op jit(solution)/shard_map/ppermute | solution.py:12
  21.8 3.0 %collective-permute-start.3 = (f32[1,2,64,128]{3,2,1,0:T(8,128)S(1)}, f32[1,2,64,128]{3,2,1,0:T(8,128)}, u32[]{:S(2)}, u32[]{:S(2)}) collective-permute-start(f32[1,2,64,128]{3,2,1,0:T(8,128)S(1)} %get-tuple-element.17), channel_id=1, source_target_pairs={{1,0},{2,1},{3,2},{4,3},{5,4},{6,5},{7,6},{9,8},{10,9},{11,10},{12... | collective-permute-start | bytes 196616 | tf_op jit(solution)/shard_map/ppermute | solution.py:15
  25.4 0.7 reduce.3
  26.2 1.5 fusion.8
  27.8 1.2 fusion.12
  28.9 45.1 %all-reduce.1 = bf16[1024,128]{1,0:T(8,128)(2,1)} all-reduce(f32[1024,128]{1,0:T(8,128)} %fusion.12), channel_id=1, replica_groups=mesh['gx'=4,'gy'=8] {'gx','gy'}, use_global_device_ids=true, to_apply=%region_0.0 | all-reduce | flops 131072 | bytes 786432 | tf_op jit(solution)/shard_map/psum | solution.py:64
  74.0 0.8 maximum_bitcast_fusion
  74.8 0.8 maximum_bitcast_fusion.1
  75.6 0.9 pad_maximum_fusion
  76.5 2.2 fusion.28
  79.3 1.4 fusion.7
  80.7 54.2 %scatter_fusion = f32[2,768,128]{2,1,0:T(8,128)} fusion(f32[2,768,128]{2,1,0:T(8,128)} %fusion.7, s32[512]{0:T(512)S(1)} %bitcast.98, f32[512,128]{1,0:T(8,128)S(1)} %bitcast.101), kind=kCustom, calls=%fused_computation | custom fusion | flops 65536 | bytes 790528 | tf_op jit(solution)/shard_map/vmap()/scatter-add | solution.py:21
  134.9 3.3 %fusion.4 = f32[2,1024,128]{1,2,0:T(8,128)S(1)} fusion(bf16[2,1,1024,768]{3,2,1,0:T(8,128)(2,1)} %param.9, f32[2,768,128]{2,1,0:T(8,128)} %scatter_fusion), kind=kOutput, calls=%fused_computation.6 | convolution fusion | flops 402849792 | bytes 4980736 | tf_op jit(solution)/shard_map/sln,snr->slr/dot_general | solution.py:79
  138.2 1.0 copy-done.3
  139.2 0.7 slice.77
  139.9 1.1 copy.28
  141.6 1.9 collective-permute-start.4
  144.2 2.1 slice.76
  146.3 2.3 %copy.31 = f32[2,768,128]{2,1,0:T(8,128)} copy(f32[2,768,128]{1,2,0:T(8,128)} %slice.76) | data formatting | bytes 1572864 | tf_op jit(solution)/shard_map/slice | solution.py:28
  148.6 3.6 %collective-permute-start.5 = (f32[1,64,128]{2,1,0:T(8,128)S(1)}, f32[1,64,128]{2,1,0:T(8,128)S(1)}, u32[]{:S(2)}, u32[]{:S(2)}) collective-permute-start(f32[1,64,128]{2,1,0:T(8,128)S(1)} %copy-done.7), channel_id=1, source_target_pairs={{8,0},{16,8},{24,16},{9,1},{17,9},{25,17},{10,2},{18,10},{26,18},{... | collective-permute-start | bytes 98312 | tf_op jit(solution)/shard_map/ppermute | solution.py:15
  152.2 4.2 %collective-permute-start.6 = (f32[1,2,64,128]{3,2,1,0:T(8,128)S(1)}, f32[1,2,64,128]{3,2,1,0:T(8,128)S(1)}, u32[]{:S(2)}, u32[]{:S(2)}) collective-permute-start(f32[1,2,64,128]{3,2,1,0:T(8,128)S(1)} %copy-done.6), channel_id=1, source_target_pairs={{0,1},{1,2},{2,3},{3,4},{4,5},{5,6},{6,7},{8,9},{9,10},{10,11},{11... | collective-permute-start | bytes 196616 | tf_op jit(solution)/shard_map/ppermute | solution.py:12
  156.4 1.9 collective-permute-start.7
  158.4 0.8 maximum_bitcast_fusion.2
  159.2 4.3 %collective-permute-done.7 = f32[1,2,64,128]{3,2,1,0:T(8,128)S(1)} collective-permute-done((f32[1,2,64,128]{3,2,1,0:T(8,128)S(1)}, f32[1,2,64,128]{3,2,1,0:T(8,128)S(1)}, u32[]{:S(2)}, u32[]{:S(2)}) %collective-permute-start.7) | collective-permute-done | bytes 65568 | tf_op jit(solution)/shard_map/ppermute | solution.py:15
  163.5 51.2 %scatter_fusion.1 = f32[2,768,128]{2,1,0:T(8,128)} fusion(f32[2,768,128]{2,1,0:T(8,128)} %copy.31, s32[512]{0:T(512)S(1)} %bitcast.99, f32[512,128]{1,0:T(8,128)S(1)} %bitcast.102), kind=kCustom, calls=%fused_computation.1 | custom fusion | flops 65536 | bytes 790528 | tf_op jit(solution)/shard_map/vmap()/scatter-add | solution.py:21
  214.8 2.3 %fusion.10 = f32[2,1,768,128]{3,2,1,0:T(8,128)} fusion(f32[2,768,128]{2,1,0:T(8,128)} %scatter_fusion.1, f32[2,1,768,128]{3,2,1,0:T(8,128)} %param.7), kind=kLoop, calls=%fused_computation.13 | loop fusion | flops 196608 | bytes 2359296
  (41 shorter events, 3.3 us)
Async XLA Ops:
  7.2 1.9 copy-start
  7.2 18.2 %copy-start.9 = (s32[2,1,64]{2,1,0:T(1,128)S(1)}, s32[2,1,64]{2,1,0:T(1,128)}, u32[]{:S(2)}) copy-start(s32[2,1,64]{2,1,0:T(1,128)} %param.12) | copy-start | bytes 1540
  7.2 18.9 %copy-start.8 = (s32[2,1,4,64]{3,2,1,0:T(4,128)S(1)}, s32[2,1,4,64]{3,2,1,0:T(4,128)}, u32[]{:S(2)}) copy-start(s32[2,1,4,64]{3,2,1,0:T(4,128)} %param.10) | copy-start | bytes 6148
  7.2 19.0 %copy-start.4 = (bf16[2,1,64,768]{3,2,1,0:T(8,128)(2,1)S(1)}, bf16[2,1,64,768]{3,2,1,0:T(8,128)(2,1)}, u32[]{:S(2)}) copy-start(bf16[2,1,64,768]{3,2,1,0:T(8,128)(2,1)} %param.11) | copy-start | bytes 589828
  7.2 69.3 %all-gather.2.cloned.1.call-start = ((), (), s32[]{:S(2)}) async-start(), calls=%async_computation | async-start | bytes 2162688 | tf_op jit(solution)/shard_map/all_gather | solution.py:59
  11.2 1.0 copy-start.1
  12.8 61.2 %collective-permute-start = (f32[1,64,128]{2,1,0:T(8,128)}, f32[1,64,128]{2,1,0:T(8,128)}, u32[]{:S(2)}, u32[]{:S(2)}) collective-permute-start(f32[1,64,128]{2,1,0:T(8,128)} %get-tuple-element.12), channel_id=1, source_target_pairs={{0,8},{8,16},{16,24},{1,9},{9,17},{17,25},{2,10},{10,18},{18,26},{... | collective-permute-start | bytes 98312 | tf_op jit(solution)/shard_map/ppermute | solution.py:12
  14.7 60.1 %collective-permute-start.1 = (f32[1,64,128]{2,1,0:T(8,128)}, f32[1,64,128]{2,1,0:T(8,128)}, u32[]{:S(2)}, u32[]{:S(2)}) collective-permute-start(f32[1,64,128]{2,1,0:T(8,128)} %get-tuple-element.13), channel_id=1, source_target_pairs={{8,0},{16,8},{24,16},{9,1},{17,9},{25,17},{10,2},{18,10},{26,18},{... | collective-permute-start | bytes 98312 | tf_op jit(solution)/shard_map/ppermute | solution.py:15
  18.4 57.2 %collective-permute-start.2 = (f32[1,2,64,128]{3,2,1,0:T(8,128)S(1)}, f32[1,2,64,128]{3,2,1,0:T(8,128)}, u32[]{:S(2)}, u32[]{:S(2)}) collective-permute-start(f32[1,2,64,128]{3,2,1,0:T(8,128)S(1)} %get-tuple-element.16), channel_id=1, source_target_pairs={{0,1},{1,2},{2,3},{3,4},{4,5},{5,6},{6,7},{8,9},{9,10},{10,11},{11... | collective-permute-start | bytes 196616 | tf_op jit(solution)/shard_map/ppermute | solution.py:12
  21.8 53.7 %collective-permute-start.3 = (f32[1,2,64,128]{3,2,1,0:T(8,128)S(1)}, f32[1,2,64,128]{3,2,1,0:T(8,128)}, u32[]{:S(2)}, u32[]{:S(2)}) collective-permute-start(f32[1,2,64,128]{3,2,1,0:T(8,128)S(1)} %get-tuple-element.17), channel_id=1, source_target_pairs={{1,0},{2,1},{3,2},{4,3},{5,4},{6,5},{7,6},{9,8},{10,9},{11,10},{12... | collective-permute-start | bytes 196616 | tf_op jit(solution)/shard_map/ppermute | solution.py:15
  76.5 2.8 %copy-start.2 = (f32[2,1024,128]{2,1,0:T(8,128)S(1)}, f32[2,1024,128]{2,1,0:T(8,128)}, u32[]{:S(2)}) copy-start(f32[2,1024,128]{2,1,0:T(8,128)} %copy-done.1) | copy-start | bytes 3145732
  76.5 2.8 %copy-start.5 = (bf16[2,1,64,768]{3,2,1,0:T(8,128)(2,1)S(1)}, bf16[2,1,64,768]{3,2,1,0:T(8,128)(2,1)}, u32[]{:S(2)}) copy-start(bf16[2,1,64,768]{3,2,1,0:T(8,128)(2,1)} %param.11) | copy-start | bytes 589828
  138.2 1.0 copy-start.3
  141.6 16.8 %collective-permute-start.4 = (f32[1,64,128]{2,1,0:T(8,128)}, f32[1,64,128]{2,1,0:T(8,128)}, u32[]{:S(2)}, u32[]{:S(2)}) collective-permute-start(f32[1,64,128]{2,1,0:T(8,128)} %get-tuple-element.6), channel_id=1, source_target_pairs={{0,8},{8,16},{16,24},{1,9},{9,17},{17,25},{2,10},{10,18},{18,26},{... | collective-permute-start | bytes 98312 | tf_op jit(solution)/shard_map/ppermute | solution.py:12
  144.2 4.4 %copy-start.7 = (f32[1,64,128]{2,1,0:T(8,128)S(1)}, f32[1,64,128]{2,1,0:T(8,128)}, u32[]{:S(2)}) copy-start(f32[1,64,128]{2,1,0:T(8,128)} %get-tuple-element.7) | copy-start | bytes 98308
  144.2 8.0 %copy-start.6 = (f32[1,2,64,128]{3,2,1,0:T(8,128)S(1)}, f32[1,2,64,128]{3,2,1,0:T(8,128)}, u32[]{:S(2)}) copy-start(f32[1,2,64,128]{3,2,1,0:T(8,128)} %get-tuple-element.10) | copy-start | bytes 196612
  148.6 10.6 %collective-permute-start.5 = (f32[1,64,128]{2,1,0:T(8,128)S(1)}, f32[1,64,128]{2,1,0:T(8,128)S(1)}, u32[]{:S(2)}, u32[]{:S(2)}) collective-permute-start(f32[1,64,128]{2,1,0:T(8,128)S(1)} %copy-done.7), channel_id=1, source_target_pairs={{8,0},{16,8},{24,16},{9,1},{17,9},{25,17},{10,2},{18,10},{26,18},{... | collective-permute-start | bytes 98312 | tf_op jit(solution)/shard_map/ppermute | solution.py:15
  152.2 6.9 %collective-permute-start.6 = (f32[1,2,64,128]{3,2,1,0:T(8,128)S(1)}, f32[1,2,64,128]{3,2,1,0:T(8,128)S(1)}, u32[]{:S(2)}, u32[]{:S(2)}) collective-permute-start(f32[1,2,64,128]{3,2,1,0:T(8,128)S(1)} %copy-done.6), channel_id=1, source_target_pairs={{0,1},{1,2},{2,3},{3,4},{4,5},{5,6},{6,7},{8,9},{9,10},{10,11},{11... | collective-permute-start | bytes 196616 | tf_op jit(solution)/shard_map/ppermute | solution.py:12
  156.4 7.1 %collective-permute-start.7 = (f32[1,2,64,128]{3,2,1,0:T(8,128)S(1)}, f32[1,2,64,128]{3,2,1,0:T(8,128)S(1)}, u32[]{:S(2)}, u32[]{:S(2)}) collective-permute-start(f32[1,2,64,128]{3,2,1,0:T(8,128)S(1)} %get-tuple-element.11), channel_id=1, source_target_pairs={{1,0},{2,1},{3,2},{4,3},{5,4},{6,5},{7,6},{9,8},{10,9},{11,10},{12... | collective-permute-start | bytes 196616 | tf_op jit(solution)/shard_map/ppermute | solution.py:15
Sparse Core Ops, SparseCore 0:
  11.0 57.1 all-gather.1
where the time goes:
time: 227 us; the launch traced here: 224 us
  other arithmetic  112 us (49%)
  blocking collectives  45.1 us (20%)
  starting transfers between devices  23.7 us (10%)
  between operations  14.3 us (6%)
  matrix products  12.3 us (5%)
  local copies, waits for them, and re-layouts  11.9 us (5%)
  waiting for transfers between devices  5.05 us (2%)
    scatter-add x2, other arithmetic, add_rows(): return owned_rows.at[indices].add(values)  105 us
    psum x1, blocking collectives, body(): totals = lax.psum(local_sums, ('gx', 'gy'))  45.1 us
    ppermute x4, starting transfers between devices, with_halo(): lax.ppermute(lax.slice_in_dim(block, 0, width, axis=dim), axis, backward)  12.2 us
    ppermute x4, starting transfers between devices, with_halo(): lax.ppermute(lax.slice_in_dim(block, block.shape[dim] - width, None, axis...  11.5 us
  transfers between devices with their start and end apart: 9, of which 1 were waited for; matrix products, arithmetic and copies ran while one was open for 7% of the time, Pallas kernels for 0%

commit v1 on v0

v1 whole, which is shorter than its diff:
```python
import functools
import jax
import jax.numpy as jnp
from jax import lax
from jax.experimental import pallas as pl
from jax.experimental.pallas import tpu as pltpu
from jax.sharding import PartitionSpec as P

F32 = jnp.float32
BF16 = jnp.bfloat16
CONTRACT_FIRST = (((0,), (0,)), ((), ()))
VMEM = pl.BlockSpec(memory_space=pltpu.VMEM)
PARAMS = pltpu.CompilerParams(vmem_limit_bytes=24 * 1024 * 1024)


def bits_of(count):
    return count.bit_length() - 1


def mask_of(step):
    return (1 << step) - 1


def swap(value, axis, mask):
    count = lax.axis_size(axis)
    return lax.ppermute(value, axis, [(i, i ^ mask) for i in range(count)])


def relative_block(block, device, steps):
    left = block ^ device
    place = left * 0
    for step in range(steps, 0, -1):
        bit = (left >> (step - 1)) & 1
        place = place | (bit << (steps - step))
        left = left ^ (bit * mask_of(step))
    return place


def halves(value):
    high = value.astype(BF16)
    low = (value - high.astype(F32)).astype(BF16)
    return jnp.concatenate([high, low], axis=1)


def joined(value):
    width = value.shape[1] // 2
    return value[:, :width] + value[:, width:]


def mm(left, right):
    return jnp.dot(left, right, preferred_element_type=F32)


def terms_kernel(steps, rhs_ref, basis_ref, ids_ref, keep_ref, send_ref):
    device = lax.axis_index("gx")
    subs, _, functions, _ = basis_ref.shape
    half, width = keep_ref.shape
    order = 2 * half
    block = order >> steps
    total = None
    for s in range(subs):
        terms = joined(mm(basis_ref[s, 0], halves(rhs_ref[s, 0])))
        ids = ids_ref[s]
        place = relative_block(ids // block, device, steps) * block + ids % block
        rows = lax.broadcasted_iota(jnp.int32, (order, functions), 0)
        pick = (rows == place).astype(BF16)
        part = joined(mm(pick, halves(terms)))
        total = part if total is None else total + part
    keep_ref[...] = total[:half]
    send_ref[:half] = total[half:].astype(BF16)
    ids = jnp.concatenate([ids_ref[s] for s in range(subs)], axis=1)
    row = lax.broadcasted_iota(jnp.int32, (16, ids.shape[1]), 0)
    coded = jnp.where(row == 0, ids // 256, jnp.where(row == 1, ids % 256, 0))
    send_ref[half:] = coded.astype(F32).astype(BF16)


def halve_kernel(keep_ref, got_ref, own_ids_ref, next_ref, send_ref):
    rows = keep_ref.shape[0]
    half = rows // 2
    total = keep_ref[...] + got_ref[:rows].astype(F32)
    next_ref[...] = total[:half]
    send_ref[:half] = total[half:].astype(BF16)
    known = own_ids_ref.shape[0]
    send_ref[half : half + known] = own_ids_ref[...]
    send_ref[half + known :] = got_ref[rows:]


def sum_kernel(keep_ref, got_ref, halo_ref, next_ref, send_ref):
    rows = keep_ref.shape[0]
    total = keep_ref[...] + got_ref[:rows].astype(F32)
    next_ref[...] = total
    send_ref[:rows] = total.astype(BF16)
    send_ref[rows:] = halo_ref[...]


def solve_kernel(own_rows, inverse_ref, rhs_ref, own_ref, margin_ref):
    value = mm(inverse_ref[0, 0], rhs_ref[0, 0].astype(BF16))
    own_ref[0] = value[:own_rows]
    margin_ref[0] = value[own_rows:].astype(BF16)


def pick_kernel(masks, steps, near_ref, far_ref, *rest):
    id_refs, out_ref, scratch = rest[:-2], rest[-2], rest[-1]
    device = lax.axis_index("gy")
    half, order = near_ref.shape
    width = scratch.shape[1]
    rows = 2 * half
    per_device = rows >> steps
    place = lax.broadcasted_iota(jnp.int32, (rows, rows), 1)
    target = lax.broadcasted_iota(jnp.int32, (rows, rows), 0)
    piece = place // per_device
    source = piece * 0 + device
    for bit, mask in enumerate(masks):
        source = source ^ (((piece >> bit) & 1) * mask)
    arrange = (source * per_device + place % per_device == target).astype(BF16)
    names = lax.broadcasted_iota(jnp.int32, (order, width), 0)
    near = near_ref[...]
    far = far_ref[...]
    for q, ref in enumerate(id_refs):
        code = ref[...].astype(F32)
        ids = (code[0:1] * 256.0 + code[1:2]).astype(jnp.int32)
        pick = (names == ids).astype(BF16)
        scratch[:half] = mm(near, pick).astype(BF16)
        scratch[half:] = mm(far, pick).astype(BF16)
        value = mm(arrange, scratch[...])
        out_ref[q * width : (q + 1) * width] = value.T.astype(BF16)


def coarse_kernel(rows, picked_ref, keep_ref, halo_ref, *rest):
    got_refs, next_ref, send_ref = rest[:-2], rest[-2], rest[-1]
    total = keep_ref[...]
    for ref in got_refs:
        total = total + ref[:rows].astype(F32)
    low = total.astype(BF16)
    half = next_ref.shape[0]
    value = mm(picked_ref[...], low)
    next_ref[...] = value[:half]
    send_ref[:half] = value[half:].astype(BF16)
    send_ref[half:] = halo_ref[...]


def halve_halo_kernel(keep_ref, got_ref, halo_ref, next_ref, send_ref):
    rows = keep_ref.shape[0]
    half = rows // 2
    total = keep_ref[...] + got_ref[:rows].astype(F32)
    next_ref[...] = total[:half]
    send_ref[:half] = total[half:].astype(BF16)
    send_ref[half:] = halo_ref[...]


def spread_pick(rows, spill):
    iota = lax.broadcasted_iota(jnp.int32, (rows, spill.shape[1]), 0)
    return (iota == spill).astype(BF16)


def received(subs, sub, width, groups, pair_x, other_x, pair_y, other_y, even_x, even_y):
    west = groups(sub - 1, 1) if sub > 0 else jnp.where(even_x, other_x, pair_x)
    east = groups(sub + 1, 0) if sub < subs - 1 else jnp.where(even_x, pair_x, other_x)
    rows = slice(sub * width, (sub + 1) * width)
    south = jnp.where(even_y, other_y[rows], pair_y[rows])
    north = jnp.where(even_y, pair_y[rows], other_y[rows])
    return jnp.concatenate([west, east, south, north], axis=0)


def other_neighbour(axis):
    device = lax.axis_index(axis)
    even = device % 2 == 0
    other = jnp.where(even, device - 1, device + 1)
    return device, even, other


def correction_kernel(
    counts, width, own_ref, margin_ref, spill_ref, basis_ref, operator_ref, keep_ref, *rest
):
    gx_first, gx_later, gy_first, gy_later = counts
    refs = list(rest)
    pair_x_ref = refs.pop(0)
    last_refs = [refs.pop(0) for _ in range(gx_later)]
    pair_y_ref = refs.pop(0)
    later_y = [refs.pop(0) for _ in range(gy_later)]
    out_ref, low_ref, image_ref, send_xp, send_xo, send_yp, send_yo = refs
    subs, rows, columns = own_ref.shape
    functions = basis_ref.shape[2]
    picked = keep_ref[...]
    count = picked.shape[0]
    final_ref = last_refs[-1] if last_refs else pair_x_ref
    picked = picked + final_ref[:count].astype(F32)
    _, even_x, _ = other_neighbour("gx")
    _, even_y, _ = other_neighbour("gy")
    top = pair_x_ref.shape[0] - width
    pair_x = pair_x_ref[top:]
    other_x = None
    device_x, _, other_dev = other_neighbour("gx")
    for step, ref in enumerate(last_refs, 2):
        here = (device_x ^ mask_of(step)) == other_dev
        part = jnp.where(here, ref[ref.shape[0] - width :], jnp.zeros((width, columns), BF16))
        other_x = part if other_x is None else other_x + part
    if other_x is None:
        other_x = jnp.zeros((width, columns), BF16)
    size = subs * width
    pair_y = pair_y_ref[pair_y_ref.shape[0] - size :]
    other_y = jnp.zeros((size, columns), BF16)
    device_y, _, other_dev = other_neighbour("gy")
    for step, ref in enumerate(later_y, 2):
        here = (device_y ^ mask_of(step)) == other_dev
        other_y = other_y + jnp.where(
            here, ref[ref.shape[0] - size :], jnp.zeros((size, columns), BF16)
        )

    def groups(sub, side):
        return margin_ref[sub, side * width : (side + 1) * width]

    for s in range(subs):
        values = received(
            subs, s, width, groups, pair_x, other_x, pair_y, other_y, even_x, even_y
        )
        coarse = lax.dot_general(
            basis_ref[s, 0],
            halves(picked[s * functions : (s + 1) * functions]),
            CONTRACT_FIRST,
            preferred_element_type=F32,
        )
        value = own_ref[s] + mm(spread_pick(rows, spill_ref[s]), values) + joined(coarse)
        out_ref[s, 0] = value
        low = value.astype(BF16)
        low_ref[s] = low
        image_ref[s] = mm(operator_ref[s, 0], low).astype(BF16)

    def side(sub, number):
        return image_ref[sub, number * width : (number + 1) * width]

    west, east = side(0, 0), side(subs - 1, 1)
    send_xp[...] = jnp.where(even_x, east, west)
    send_xo[...] = jnp.where(even_x, west, east)
    for s in range(subs):
        south, north = side(s, 2), side(s, 3)
        send_yp[s * width : (s + 1) * width] = jnp.where(even_y, north, south)
        send_yo[s * width : (s + 1) * width] = jnp.where(even_y, south, north)


def image_kernel(operator_ref, low_ref, rhs_ref, out_ref):
    for s in range(low_ref.shape[0]):
        out_ref[s] = rhs_ref[s, 0] - mm(operator_ref[s, 0], low_ref[s])


def residual_kernel(
    width, part_ref, image_ref, spill_ref, xp_ref, xo_ref, yp_ref, yo_ref, out_ref
):
    subs, rows, _ = part_ref.shape
    _, even_x, _ = other_neighbour("gx")
    _, even_y, _ = other_neighbour("gy")

    def groups(sub, side):
        return image_ref[sub, side * width : (side + 1) * width]

    for s in range(subs):
        values = received(
            subs, s, width, groups, xp_ref[...], xo_ref[...], yp_ref[...], yo_ref[...],
            even_x, even_y,
        )
        out_ref[s, 0] = part_ref[s] - mm(spread_pick(rows, spill_ref[s]), values)


def call(kernel, shapes, *args, scratch=(), name=None):
    return pl.pallas_call(
        kernel,
        out_shape=[jax.ShapeDtypeStruct(shape, dtype) for shape, dtype in shapes],
        in_specs=[VMEM] * len(args),
        out_specs=[VMEM] * len(shapes),
        scratch_shapes=list(scratch),
        compiler_params=PARAMS,
        name=name,
    )(*args)


def body(
    adjoint_rhs, local_inverse, local_operator, spill_rows, coarse_basis, coarse_ids, coarse_inverse
):
    subs, _, rows, width = adjoint_rhs.shape
    extended = local_inverse.shape[2]
    margin = spill_rows.shape[3]
    functions = coarse_ids.shape[2]
    order = coarse_inverse.shape[1]
    count_x, count_y = lax.axis_size("gx"), lax.axis_size("gy")
    steps_x, steps_y = bits_of(count_x), bits_of(count_y)
    listed = subs * functions
    spill = spill_rows.reshape(subs, 1, 4 * margin)

    keep, send = call(
        functools.partial(terms_kernel, steps_x),
        [((order // 2, width), F32), ((order // 2 + 16, listed), BF16)],
        adjoint_rhs, coarse_basis, coarse_ids, name="coarse_terms",
    )
    ids_known = [send[order // 2 :]]
    got = swap(send, "gx", mask_of(1))

    own, margins = pl.pallas_call(
        functools.partial(solve_kernel, rows),
        grid=(subs,),
        out_shape=[
            jax.ShapeDtypeStruct((subs, rows, width), F32),
            jax.ShapeDtypeStruct((subs, 4 * margin, width), BF16),
        ],
        in_specs=[
            pl.BlockSpec((1, 1, extended, rows), lambda s: (s, 0, 0, 0)),
            pl.BlockSpec((1, 1, rows, width), lambda s: (s, 0, 0, 0)),
        ],
        out_specs=[
            pl.BlockSpec((1, rows, width), lambda s: (s, 0, 0)),
            pl.BlockSpec((1, 4 * margin, width), lambda s: (s, 0, 0)),
        ],
        compiler_params=PARAMS,
        name="local_solve",
    )(local_inverse, adjoint_rhs)

    even_x = lax.axis_index("gx") % 2 == 0
    even_y = lax.axis_index("gy") % 2 == 0
    groups = margins.reshape(subs, 4, margin, width)
    west, east = groups[0, 0], groups[subs - 1, 1]
    south = groups[:, 2].reshape(subs * margin, width)
    north = groups[:, 3].reshape(subs * margin, width)
    halo_xp, halo_xo = jnp.where(even_x, east, west), jnp.where(even_x, west, east)
    halo_yp, halo_yo = jnp.where(even_y, north, south), jnp.where(even_y, south, north)

    size = order // 2
    for step in range(2, steps_x + 1):
        own_ids = jnp.concatenate(ids_known, 0)
        known = own_ids.shape[0]
        half = size // 2
        keep, send = call(
            halve_kernel,
            [((half, width), F32), ((half + 2 * known, listed), BF16)],
            keep, got, own_ids, name="coarse_halve",
        )
        ids_known = ids_known + [
            got[size + 16 * i : size + 16 * (i + 1)] for i in range(len(ids_known))
        ]
        got = swap(send, "gx", mask_of(step))
        size = half
    ids_known = ids_known + [
        got[size + 16 * i : size + 16 * (i + 1)] for i in range(len(ids_known))
    ]
    ordered = []
    for q in range(count_x):
        p = sum(((q >> (steps_x - k)) & 1) << (k - 1) for k in range(1, steps_x + 1))
        ordered.append(ids_known[p])

    gather_masks = [1 << (steps_y - 1 - i) for i in range(steps_y)]
    near, far = coarse_inverse, None
    for i, mask in enumerate(gather_masks):
        far = swap(near, "gy", mask)
        if i < steps_y - 1:
            near = jnp.concatenate([near, far], 0)
    (picked,) = call(
        functools.partial(pick_kernel, gather_masks, steps_y),
        [((count_x * listed, size), BF16)],
        near, far, *ordered,
        scratch=[pltpu.VMEM((size, listed), BF16)],
        name="inverse_pick",
    )

    halo_rows = subs * margin
    keep, send = call(
        sum_kernel,
        [((size, width), F32), ((size + halo_rows, width), BF16)],
        keep, got, halo_yp, name="coarse_sum_x",
    )
    got = swap(send, "gy", mask_of(1))
    pair_y = got
    later_y = []
    pending = [got]
    step = 2
    while step <= steps_y:
        keep, send = call(
            sum_kernel,
            [((size, width), F32), ((size + halo_rows, width), BF16)],
            keep, pending[0], halo_yo, name="coarse_sum_y",
        )
        if step < steps_y:
            first = swap(send, "gy", mask_of(step))
            second = swap(send, "gy", mask_of(step + 1))
            third = swap(send[:size], "gy", mask_of(step) ^ mask_of(step + 1))
            later_y += [first, second]
            pending = [first, second, third]
            step += 2
        else:
            first = swap(send, "gy", mask_of(step))
            later_y += [first]
            pending = [first]
            step += 1
        if step <= steps_y:
            while len(pending) > 1:
                extra = pending.pop()
                keep = keep + extra[:size].astype(F32)

    half = count_x * listed // 2
    keep, send = call(
        functools.partial(coarse_kernel, size),
        [((half, width), F32), ((half + margin, width), BF16)],
        picked, keep, halo_xp, *pending, name="coarse_solve",
    )
    pair_x = swap(send, "gx", mask_of(1))
    got = pair_x
    later_x = []
    for step in range(2, steps_x + 1):
        half = half // 2
        keep, send = call(
            halve_halo_kernel,
            [((half, width), F32), ((half + margin, width), BF16)],
            keep, got, halo_xo, name="picked_halve",
        )
        got = swap(send, "gx", mask_of(step))
        later_x.append(got)

    full = lambda shape: pl.BlockSpec(shape, lambda i: (0,) * len(shape))
    inputs = [own, margins, spill, coarse_basis, local_operator, keep, pair_x, *later_x, pair_y, *later_y]
    in_specs = [full(x.shape) for x in inputs]
    in_specs[4] = pl.BlockSpec(
        (subs, 1, extended - rows, rows), lambda i: (0, 0, rows // (extended - rows), 0)
    )
    shapes = [
        ((subs, 1, rows, width), F32),
        ((subs, rows, width), BF16),
        ((subs, 4 * margin, width), BF16),
        ((margin, width), BF16),
        ((margin, width), BF16),
        ((subs * margin, width), BF16),
        ((subs * margin, width), BF16),
    ]
    correction, low, image, send_xp, send_xo, send_yp, send_yo = pl.pallas_call(
        functools.partial(correction_kernel, (1, len(later_x), 1, len(later_y)), margin),
        grid=(1,),
        out_shape=[jax.ShapeDtypeStruct(*s) for s in shapes],
        in_specs=in_specs,
        out_specs=[full(s[0]) for s in shapes],
        compiler_params=PARAMS,
        name="correction",
    )(*inputs)

    def other(value, axis):
        count = lax.axis_size(axis)
        pairs = [(i, i + 1) for i in range(1, count - 1, 2)]
        return lax.ppermute(value, axis, pairs + [(j, i) for i, j in pairs])

    got_xo = other(send_xo, "gx")
    got_yp = swap(send_yp, "gy", 1)
    got_yo = other(send_yo, "gy")
    got_xp = swap(send_xp, "gx", 1)

    (part,) = pl.pallas_call(
        image_kernel,
        grid=(1,),
        out_shape=[jax.ShapeDtypeStruct((subs, rows, width), F32)],
        in_specs=[
            full((subs, 1, rows, rows)),
            full((subs, rows, width)),
            full((subs, 1, rows, width)),
        ],
        out_specs=[full((subs, rows, width))],
        compiler_params=PARAMS,
        name="image_own",
    )(local_operator, low, adjoint_rhs)
    (residual,) = call(
        functools.partial(residual_kernel, margin),
        [((subs, 1, rows, width), F32)],
        part, image, spill, got_xp, got_xo, got_yp, got_yo, name="residual",
    )
    return correction, residual


def solution(mesh):
    in_specs = (
        P("gx", "gy", None, None),
        P("gx", "gy", None, None),
        P("gx", "gy", None, None),
        P("gx", "gy", None, None),
        P("gx", "gy", None, None),
        P("gx", "gy", None),
        P(("gx", "gy"), None),
    )
    out_specs = (P("gx", "gy", None, None), P("gx", "gy", None, None))
    return jax.shard_map(body, mesh=mesh, in_specs=in_specs, out_specs=out_specs, check_vma=False)
```

time: 227 us -> 71.4 us (0.31)
  the two profiles are of different devices: /device:TPU:6 before, /device:TPU:9 now
where the time goes in v1:
time: 71.4 us; the launch traced here: 70.6 us
  local copies, waits for them, and re-layouts  22 us (31%)
  starting transfers between devices  21.2 us (30%)
  waiting for transfers between devices  14.4 us (20%)
  Pallas kernels  10.6 us (15%)
  other arithmetic  1.53 us (2%)
  between operations  0.79 us (1%)
    unnamed x48, local copies, waits for them, and re-layouts  17.7 us
    ppermute x13, starting transfers between devices, swap(): return lax.ppermute(value, axis, [(i, i ^ mask) for i in range(count)])  15.8 us
    ppermute x13, waiting for transfers between devices, swap(): return lax.ppermute(value, axis, [(i, i ^ mask) for i in range(count)])  12.4 us
    pallas_call x8, Pallas kernels, call(): pl.pallas_call(kernel, out_shape=[jax.ShapeDtypeStruct(shape, dtype) for...  6.14 us
    ppermute x2, starting transfers between devices, other(): return lax.ppermute(value, axis, pairs + [(j, i) for i, j in pairs])  5.42 us
    pallas_call x1, Pallas kernels, body(): pl.pallas_call(functools.partial(correction_kernel, (1, len(later_x), 1,...  2.52 us
    ppermute x2, waiting for transfers between devices, other(): return lax.ppermute(value, axis, pairs + [(j, i) for i, j in pairs])  2.01 us
    concatenate x1, local copies, waits for them, and re-layouts, body(): near = jnp.concatenate([near, far], 0)  1.57 us
  transfers between devices with their start and end apart: 15, of which 5 were waited for; matrix products, arithmetic and copies ran while one was open for 11% of the time, Pallas kernels for 8%

profile of v1, /device:TPU:9, one launch (start us, length us, event | category | flops | bytes accessed | tf_op | source)
XLA Modules:
  0.0 70.6 jit_solution(4432354037497705704)
XLA Ops:
  0.6 2.4 %collective-permute-start = (bf16[32,1024]{1,0:T(8,128)(2,1)}, bf16[32,1024]{1,0:T(8,128)(2,1)}, u32[]{:S(2)}, u32[]{:S(2)}) collective-permute-start(bf16[32,1024]{1,0:T(8,128)(2,1)} %param.13), channel_id=1, source_target_pairs={{0,4},{1,5},{2,6},{3,7},{4,0},{5,1},{6,2},{7,3},{8,12},{9,13},{10,... | collective-permute-start | bytes 196616 | tf_op jit(solution)/shard_map/ppermute | solution.py:26
  3.0 1.1 %copy-done.1 = f32[2,1,768,128]{3,2,1,0:T(8,128)S(1)} copy-done((f32[2,1,768,128]{3,2,1,0:T(8,128)S(1)}, f32[2,1,768,128]{3,2,1,0:T(8,128)}, u32[]{:S(2)}) %copy-start.1) | copy-done | bytes 786456
  5.7 1.4 %coarse_terms.1 = (f32[512,128]{1,0:T(8,128)S(1)}, bf16[528,128]{1,0:T(8,128)(2,1)}) custom-call(f32[2,1,768,128]{3,2,1,0:T(8,128)S(1)} %copy-done.1, bf16[2,1,64,768]{3,2,1,0:T(8,128)(2,1)S(1)} %copy-done.5, s32[2,1,64]{2,1,0:T(1,128)S(1)} %copy-done.21), custom_call_target="tpu_custom_call" | custom-call | tf_op jit(solution)/shard_map/coarse_terms/pallas_call | solution.py:265
  7.9 1.0 %collective-permute-start.3 = (bf16[528,128]{1,0:T(8,128)(2,1)}, bf16[528,128]{1,0:T(8,128)(2,1)}, u32[]{:S(2)}, u32[]{:S(2)}) collective-permute-start(bf16[528,128]{1,0:T(8,128)(2,1)} %get-tuple-element.25), channel_id=1, source_target_pairs={{0,8},{8,0},{16,24},{24,16},{1,9},{9,1},{17,25},{25,17},{2,10},{10... | collective-permute-start | bytes 405512 | tf_op jit(solution)/shard_map/ppermute | solution.py:26
  8.8 1.1 %copy-done.2 = f32[2,1,768,128]{3,2,1,0:T(8,128)S(1)} copy-done((f32[2,1,768,128]{3,2,1,0:T(8,128)S(1)}, f32[2,1,768,128]{3,2,1,0:T(8,128)}, u32[]{:S(2)}) %copy-start.2) | copy-done | bytes 786456
  10.0 1.9 %copy-done.4 = bf16[2,1,1024,768]{3,2,1,0:T(8,128)(2,1)S(1)} copy-done((bf16[2,1,1024,768]{3,2,1,0:T(8,128)(2,1)S(1)}, bf16[2,1,1024,768]{3,2,1,0:T(8,128)(2,1)}, u32[]{:S(2)}) %copy-start.4) | copy-done | bytes 3145752
  11.9 1.2 %local_solve.1 = (f32[2,768,128]{2,1,0:T(8,128)S(1)}, bf16[2,256,128]{2,1,0:T(8,128)(2,1)S(1)}) custom-call(bf16[2,1,1024,768]{3,2,1,0:T(8,128)(2,1)S(1)} %copy-done.4, f32[2,1,768,128]{3,2,1,0:T(8,128)S(1)} %copy-done.2), custom_call_target="tpu_custom_call" | custom-call | tf_op jit(solution)/shard_map/local_solve/pallas_call | solution.py:297
  13.9 1.5 %pad_maximum_fusion = bf16[64,1024]{1,0:T(8,128)(2,1)} fusion(bf16[32,1024]{1,0:T(8,128)(2,1)} %collective-permute-done, bf16[32,1024]{1,0:T(8,128)(2,1)S(1)} %copy-done.22), kind=kLoop, calls=%fused_computation | loop fusion | flops 262144 | bytes 262144 | tf_op jit(solution)/shard_map/concatenate | solution.py:353
  16.9 1.5 %constant_dynamic-update-slice_fusion.1 = bf16[128,1024]{1,0:T(8,128)(2,1)} fusion(bf16[128,1024]{1,0:T(8,128)(2,1)} %constant_dynamic-update-slice_fusion.2, bf16[32,1024]{1,0:T(8,128)(2,1)} %collective-permute-done), kind=kLoop, calls=%fused_computation.6 | loop fusion | bytes 131072
  18.4 0.9 %copy-done.17 = f32[512,128]{1,0:T(8,128)S(1)} copy-done((f32[512,128]{1,0:T(8,128)S(1)}, f32[512,128]{1,0:T(8,128)}, u32[]{:S(2)}) %copy-start.17) | copy-done | bytes 262168
  19.4 0.9 %coarse_halve.1 = (f32[256,128]{1,0:T(8,128)S(1)}, bf16[288,128]{1,0:T(8,128)(2,1)S(1)}) custom-call(f32[512,128]{1,0:T(8,128)S(1)} %copy-done.17, bf16[528,128]{1,0:T(8,128)(2,1)} %collective-permute-done.3.got_ref, bf16[16,128]{1,0:T(8,128)(2,1)S(1)} %slice.27.own_ids_ref.rest_0_), custom_call_target="tpu_custom_call" | custom-call | tf_op jit(solution)/shard_map/coarse_halve/pallas_call | solution.py:265
  20.3 1.5 %collective-permute-start.4 = (bf16[288,128]{1,0:T(8,128)(2,1)S(1)}, bf16[288,128]{1,0:T(8,128)(2,1)S(1)}, u32[]{:S(2)}, u32[]{:S(2)}) collective-permute-start(bf16[288,128]{1,0:T(8,128)(2,1)S(1)} %get-tuple-element.27), channel_id=1, source_target_pairs={{0,24},{8,16},{16,8},{24,0},{1,25},{9,17},{17,9},{25,1},{2,26},{10... | collective-permute-start | bytes 221192 | tf_op jit(solution)/shard_map/ppermute | solution.py:26
  21.8 1.6 %constant_dynamic-update-slice_fusion.near_ref = bf16[128,1024]{1,0:T(8,128)(2,1)} fusion(bf16[128,1024]{1,0:T(8,128)(2,1)} %constant_dynamic-update-slice_fusion.1, bf16[64,1024]{1,0:T(8,128)(2,1)} %collective-permute-done.1), kind=kLoop, calls=%fused_computation.5 | loop fusion | bytes 262144 | tf_op jit(solution)/shard_map/concatenate | solution.py:353
  23.4 1.2 %collective-permute-start.2 = (bf16[128,1024]{1,0:T(8,128)(2,1)}, bf16[128,1024]{1,0:T(8,128)(2,1)S(1)}, u32[]{:S(2)}, u32[]{:S(2)}) collective-permute-start(bf16[128,1024]{1,0:T(8,128)(2,1)} %constant_dynamic-update-slice_fusion.near_ref), channel_id=1, source_target_pairs={{0,1},{1,0},{2,3},{3,2},{4,5},{5,4},{6,7},{7,6},{8,9},{9,8},{10,11... | collective-permute-start | bytes 786440 | tf_op jit(solution)/shard_map/ppermute | solution.py:26
  24.6 1.2 %collective-permute-start.5 = (bf16[384,128]{1,0:T(8,128)(2,1)S(1)}, bf16[384,128]{1,0:T(8,128)(2,1)S(1)}, u32[]{:S(2)}, u32[]{:S(2)}) collective-permute-start(bf16[384,128]{1,0:T(8,128)(2,1)S(1)} %get-tuple-element.30), channel_id=1, source_target_pairs={{0,1},{1,0},{2,3},{3,2},{4,5},{5,4},{6,7},{7,6},{8,9},{9,8},{10,11... | collective-permute-start | bytes 294920 | tf_op jit(solution)/shard_map/ppermute | solution.py:26
  26.5 6.8 %collective-permute-done.5.got_ref.rest_2_ = bf16[384,128]{1,0:T(8,128)(2,1)S(1)} collective-permute-done((bf16[384,128]{1,0:T(8,128)(2,1)S(1)}, bf16[384,128]{1,0:T(8,128)(2,1)S(1)}, u32[]{:S(2)}, u32[]{:S(2)}) %collective-permute-start.5) | collective-permute-done | bytes 98336 | tf_op jit(solution)/shard_map/ppermute | solution.py:26
  33.4 1.2 %collective-permute-start.7 = (bf16[384,128]{1,0:T(8,128)(2,1)S(1)}, bf16[384,128]{1,0:T(8,128)(2,1)S(1)}, u32[]{:S(2)}, u32[]{:S(2)}) collective-permute-start(bf16[384,128]{1,0:T(8,128)(2,1)S(1)} %get-tuple-element.32), channel_id=1, source_target_pairs={{0,7},{1,6},{2,5},{3,4},{4,3},{5,2},{6,1},{7,0},{8,15},{9,14},{10,... | collective-permute-start | bytes 294920 | tf_op jit(solution)/shard_map/ppermute | solution.py:26
  34.6 1.2 %collective-permute-start.6 = (bf16[384,128]{1,0:T(8,128)(2,1)S(1)}, bf16[384,128]{1,0:T(8,128)(2,1)S(1)}, u32[]{:S(2)}, u32[]{:S(2)}) collective-permute-start(bf16[384,128]{1,0:T(8,128)(2,1)S(1)} %get-tuple-element.32), channel_id=1, source_target_pairs={{0,3},{1,2},{2,1},{3,0},{4,7},{5,6},{6,5},{7,4},{8,11},{9,10},{10,... | collective-permute-start | bytes 294920 | tf_op jit(solution)/shard_map/ppermute | solution.py:26
  35.8 2.0 %collective-permute-start.8 = (bf16[256,128]{1,0:T(8,128)(2,1)S(1)}, bf16[256,128]{1,0:T(8,128)(2,1)S(1)}, u32[]{:S(2)}, u32[]{:S(2)}) collective-permute-start(bf16[256,128]{1,0:T(8,128)(2,1)S(1)} %slice.35), channel_id=1, source_target_pairs={{0,4},{1,5},{2,6},{3,7},{4,0},{5,1},{6,2},{7,3},{8,12},{9,13},{10,... | collective-permute-start | bytes 196616 | tf_op jit(solution)/shard_map/ppermute | solution.py:26
  37.8 0.9 %copy-done.9 = bf16[128,1024]{1,0:T(8,128)(2,1)S(1)} copy-done((bf16[128,1024]{1,0:T(8,128)(2,1)S(1)}, bf16[128,1024]{1,0:T(8,128)(2,1)}, u32[]{:S(2)}) %copy-start.9) | copy-done | bytes 262168
  38.7 1.6 %inverse_pick.1.picked_ref = bf16[512,256]{1,0:T(8,128)(2,1)S(1)} custom-call(bf16[128,1024]{1,0:T(8,128)(2,1)S(1)} %copy-done.9, bf16[128,1024]{1,0:T(8,128)(2,1)S(1)} %collective-permute-done.2.far_ref, bf16[16,128]{1,0:T(8,128)(2,1)S(1)} %slice.27.own_ids_ref.rest_0_, bf16[16,128]{1,0:T(8,128)(2,1)S(1)} %get-tuple-element.49.rest_1_, ...), custom_call_target="tpu_custom_call" | custom-call | tf_op jit(solution)/shard_map/inverse_pick/pallas_call | solution.py:265
  40.4 2.5 %collective-permute-done.8.rest_2_ = bf16[256,128]{1,0:T(8,128)(2,1)S(1)} collective-permute-done((bf16[256,128]{1,0:T(8,128)(2,1)S(1)}, bf16[256,128]{1,0:T(8,128)(2,1)S(1)}, u32[]{:S(2)}, u32[]{:S(2)}) %collective-permute-start.8) | collective-permute-done | bytes 65568 | tf_op jit(solution)/shard_map/ppermute | solution.py:26
  43.5 2.2 %collective-permute-start.9 = (bf16[320,128]{1,0:T(8,128)(2,1)S(1)}, bf16[320,128]{1,0:T(8,128)(2,1)S(1)}, u32[]{:S(2)}, u32[]{:S(2)}) collective-permute-start(bf16[320,128]{1,0:T(8,128)(2,1)S(1)} %get-tuple-element.34), channel_id=1, source_target_pairs={{0,8},{8,0},{16,24},{24,16},{1,9},{9,1},{17,25},{25,17},{2,10},{10... | collective-permute-start | bytes 245768 | tf_op jit(solution)/shard_map/ppermute | solution.py:26
  48.5 1.3 %reshape.18.spill_ref = s32[2,1,256]{2,1,0:T(1,128)} reshape(s32[2,1,4,64]{3,2,1,0:T(4,128)} %param.10) | data formatting | bytes 4096 | tf_op jit(solution)/shard_map/reshape | solution.py:287
  49.8 2.1 %collective-permute-done.10.rest_1_ = bf16[192,128]{1,0:T(8,128)(2,1)} collective-permute-done((bf16[192,128]{1,0:T(8,128)(2,1)}, bf16[192,128]{1,0:T(8,128)(2,1)}, u32[]{:S(2)}, u32[]{:S(2)}) %collective-permute-start.10) | collective-permute-done | bytes 49184 | tf_op jit(solution)/shard_map/ppermute | solution.py:26
  52.0 1.1 %copy-done.8 = f32[2,768,128]{2,1,0:T(8,128)S(1)} copy-done((f32[2,768,128]{2,1,0:T(8,128)S(1)}, f32[2,768,128]{2,1,0:T(8,128)}, u32[]{:S(2)}) %copy-start.8) | copy-done | bytes 786456
  57.3 2.5 %correction.1 = (f32[2,1,768,128]{3,2,1,0:T(8,128)}, bf16[2,768,128]{2,1,0:T(8,128)(2,1)S(1)}, bf16[2,256,128]{2,1,0:T(8,128)(2,1)S(1)}, bf16[64,128]{1,0:T(8,12...) custom-call(f32[2,768,128]{2,1,0:T(8,128)S(1)} %copy-done.8, ...), custom_call_target="tpu_custom_call" | custom-call | tf_op jit(solution)/shard_map/correction/pallas_call | solution.py:430
  60.1 3.2 %collective-permute-start.14 = (bf16[128,128]{1,0:T(8,128)(2,1)S(1)}, bf16[128,128]{1,0:T(8,128)(2,1)S(1)}, u32[]{:S(2)}, u32[]{:S(2)}) collective-permute-start(bf16[128,128]{1,0:T(8,128)(2,1)S(1)} %get-tuple-element.43), channel_id=1, source_target_pairs={{1,2},{3,4},{5,6},{2,1},{4,3},{6,5},{9,10},{11,12},{13,14},{10,9},... | collective-permute-start | bytes 98312 | tf_op jit(solution)/shard_map/ppermute | solution.py:443
  63.3 1.0 %collective-permute-start.11 = (bf16[64,128]{1,0:T(8,128)(2,1)S(1)}, bf16[64,128]{1,0:T(8,128)(2,1)S(1)}, u32[]{:S(2)}, u32[]{:S(2)}) collective-permute-start(bf16[64,128]{1,0:T(8,128)(2,1)S(1)} %get-tuple-element.40), channel_id=1, source_target_pairs={{0,8},{8,0},{16,24},{24,16},{1,9},{9,1},{17,25},{25,17},{2,10},{10... | collective-permute-start | bytes 49160 | tf_op jit(solution)/shard_map/ppermute | solution.py:26
  64.2 2.2 %collective-permute-start.12 = (bf16[64,128]{1,0:T(8,128)(2,1)S(1)}, bf16[64,128]{1,0:T(8,128)(2,1)S(1)}, u32[]{:S(2)}, u32[]{:S(2)}) collective-permute-start(bf16[64,128]{1,0:T(8,128)(2,1)S(1)} %get-tuple-element.41), channel_id=1, source_target_pairs={{8,16},{16,8},{9,17},{17,9},{10,18},{18,10},{11,19},{19,11},{12,20... | collective-permute-start | bytes 49160 | tf_op jit(solution)/shard_map/ppermute | solution.py:443
  67.3 2.0 %collective-permute-done.12.xo_ref = bf16[64,128]{1,0:T(8,128)(2,1)S(1)} collective-permute-done((bf16[64,128]{1,0:T(8,128)(2,1)S(1)}, bf16[64,128]{1,0:T(8,128)(2,1)S(1)}, u32[]{:S(2)}, u32[]{:S(2)}) %collective-permute-start.12) | collective-permute-done | bytes 16416 | tf_op jit(solution)/shard_map/ppermute | solution.py:443
  69.3 1.3 %residual.1 = f32[2,1,768,128]{3,2,1,0:T(8,128)} custom-call(f32[2,768,128]{2,1,0:T(8,128)S(1)} %image_own.1.part_ref, bf16[2,256,128]{2,1,0:T(8,128)(2,1)S(1)} %get-tuple-element.39.image_ref, s32[2,1,256]{2,1,0:T(1,128)S(1)} %copy-done.20, bf16[64,128]{1,0:T(8,128)(2,1)S(1)} %collective-permute-done.11.xp_ref, ...), custom_call_target="tpu_custom_call" | custom-call | tf_op jit(solution)/shard_map/residual/pallas_call | solution.py:265
  (66 shorter events, 14.1 us)
Async XLA Ops:
  0.6 13.3 %collective-permute-start = (bf16[32,1024]{1,0:T(8,128)(2,1)}, bf16[32,1024]{1,0:T(8,128)(2,1)}, u32[]{:S(2)}, u32[]{:S(2)}) collective-permute-start(bf16[32,1024]{1,0:T(8,128)(2,1)} %param.13), channel_id=1, source_target_pairs={{0,4},{1,5},{2,6},{3,7},{4,0},{5,1},{6,2},{7,3},{8,12},{9,13},{10,... | collective-permute-start | bytes 196616 | tf_op jit(solution)/shard_map/ppermute | solution.py:26
  3.0 1.1 %copy-start.1 = (f32[2,1,768,128]{3,2,1,0:T(8,128)S(1)}, f32[2,1,768,128]{3,2,1,0:T(8,128)}, u32[]{:S(2)}) copy-start(f32[2,1,768,128]{3,2,1,0:T(8,128)} %rhs_ref.5) | copy-start | bytes 2359300
  4.1 0.9 %copy-start.5 = (bf16[2,1,64,768]{3,2,1,0:T(8,128)(2,1)S(1)}, bf16[2,1,64,768]{3,2,1,0:T(8,128)(2,1)}, u32[]{:S(2)}) copy-start(bf16[2,1,64,768]{3,2,1,0:T(8,128)(2,1)} %basis_ref.3) | copy-start | bytes 589828
  7.9 10.5 %collective-permute-start.3 = (bf16[528,128]{1,0:T(8,128)(2,1)}, bf16[528,128]{1,0:T(8,128)(2,1)}, u32[]{:S(2)}, u32[]{:S(2)}) collective-permute-start(bf16[528,128]{1,0:T(8,128)(2,1)} %get-tuple-element.25), channel_id=1, source_target_pairs={{0,8},{8,0},{16,24},{24,16},{1,9},{9,1},{17,25},{25,17},{2,10},{10... | collective-permute-start | bytes 405512 | tf_op jit(solution)/shard_map/ppermute | solution.py:26
  8.8 1.1 %copy-start.2 = (f32[2,1,768,128]{3,2,1,0:T(8,128)S(1)}, f32[2,1,768,128]{3,2,1,0:T(8,128)}, u32[]{:S(2)}) copy-start(f32[2,1,768,128]{3,2,1,0:T(8,128)} %rhs_ref.5) | copy-start | bytes 2359300
  10.0 1.9 %copy-start.4 = (bf16[2,1,1024,768]{3,2,1,0:T(8,128)(2,1)S(1)}, bf16[2,1,1024,768]{3,2,1,0:T(8,128)(2,1)}, u32[]{:S(2)}) copy-start(bf16[2,1,1024,768]{3,2,1,0:T(8,128)(2,1)} %inverse_ref.1) | copy-start | bytes 9437188
  11.8 2.1 %copy-start.22 = (bf16[32,1024]{1,0:T(8,128)(2,1)S(1)}, bf16[32,1024]{1,0:T(8,128)(2,1)}, u32[]{:S(2)}) copy-start(bf16[32,1024]{1,0:T(8,128)(2,1)} %param.13) | copy-start | bytes 196612
  11.9 40.1 %copy-start = (bf16[2,1,1024,768]{3,2,1,0:T(8,128)(2,1)S(1)}, bf16[2,1,1024,768]{3,2,1,0:T(8,128)(2,1)}, u32[]{:S(2)}) copy-start(bf16[2,1,1024,768]{3,2,1,0:T(8,128)(2,1)} %operator_ref.3) | copy-start | bytes 9437188
  11.9 40.1 %copy-start.6 = (bf16[2,1,64,768]{3,2,1,0:T(8,128)(2,1)S(1)}, bf16[2,1,64,768]{3,2,1,0:T(8,128)(2,1)}, u32[]{:S(2)}) copy-start(bf16[2,1,64,768]{3,2,1,0:T(8,128)(2,1)} %basis_ref.3) | copy-start | bytes 589828
  13.0 0.9 %copy-start.7 = (f32[2,768,128]{2,1,0:T(8,128)}, f32[2,768,128]{2,1,0:T(8,128)S(1)}, u32[]{:S(2)}) copy-start(f32[2,768,128]{2,1,0:T(8,128)S(1)} %get-tuple-element.23.own_ref) | copy-start | bytes 2359300
  15.5 6.3 %collective-permute-start.1 = (bf16[64,1024]{1,0:T(8,128)(2,1)}, bf16[64,1024]{1,0:T(8,128)(2,1)}, u32[]{:S(2)}, u32[]{:S(2)}) collective-permute-start(bf16[64,1024]{1,0:T(8,128)(2,1)} %pad_maximum_fusion), channel_id=1, source_target_pairs={{0,2},{1,3},{2,0},{3,1},{4,6},{5,7},{6,4},{7,5},{8,10},{9,11},{10,... | collective-permute-start | bytes 393224 | tf_op jit(solution)/shard_map/ppermute | solution.py:26
  18.4 1.0 %copy-start.17 = (f32[512,128]{1,0:T(8,128)S(1)}, f32[512,128]{1,0:T(8,128)}, u32[]{:S(2)}) copy-start(f32[512,128]{1,0:T(8,128)} %copy-done.16) | copy-start | bytes 786436
  20.3 4.3 %collective-permute-start.4 = (bf16[288,128]{1,0:T(8,128)(2,1)S(1)}, bf16[288,128]{1,0:T(8,128)(2,1)S(1)}, u32[]{:S(2)}, u32[]{:S(2)}) collective-permute-start(bf16[288,128]{1,0:T(8,128)(2,1)S(1)} %get-tuple-element.27), channel_id=1, source_target_pairs={{0,24},{8,16},{16,8},{24,0},{1,25},{9,17},{17,9},{25,1},{2,26},{10... | collective-permute-start | bytes 221192 | tf_op jit(solution)/shard_map/ppermute | solution.py:26
  23.4 14.4 %collective-permute-start.2 = (bf16[128,1024]{1,0:T(8,128)(2,1)}, bf16[128,1024]{1,0:T(8,128)(2,1)S(1)}, u32[]{:S(2)}, u32[]{:S(2)}) collective-permute-start(bf16[128,1024]{1,0:T(8,128)(2,1)} %constant_dynamic-update-slice_fusion.near_ref), channel_id=1, source_target_pairs={{0,1},{1,0},{2,3},{3,2},{4,5},{5,4},{6,7},{7,6},{8,9},{9,8},{10,11... | collective-permute-start | bytes 786440 | tf_op jit(solution)/shard_map/ppermute | solution.py:26
  24.6 8.8 %collective-permute-start.5 = (bf16[384,128]{1,0:T(8,128)(2,1)S(1)}, bf16[384,128]{1,0:T(8,128)(2,1)S(1)}, u32[]{:S(2)}, u32[]{:S(2)}) collective-permute-start(bf16[384,128]{1,0:T(8,128)(2,1)S(1)} %get-tuple-element.30), channel_id=1, source_target_pairs={{0,1},{1,0},{2,3},{3,2},{4,5},{5,4},{6,7},{7,6},{8,9},{9,8},{10,11... | collective-permute-start | bytes 294920 | tf_op jit(solution)/shard_map/ppermute | solution.py:26
  33.3 4.4 %copy-start.10 = (bf16[384,128]{1,0:T(8,128)(2,1)}, bf16[384,128]{1,0:T(8,128)(2,1)S(1)}, u32[]{:S(2)}) copy-start(bf16[384,128]{1,0:T(8,128)(2,1)S(1)} %collective-permute-done.5.got_ref.rest_2_) | copy-start | bytes 294916
  33.4 9.5 %collective-permute-start.7 = (bf16[384,128]{1,0:T(8,128)(2,1)S(1)}, bf16[384,128]{1,0:T(8,128)(2,1)S(1)}, u32[]{:S(2)}, u32[]{:S(2)}) collective-permute-start(bf16[384,128]{1,0:T(8,128)(2,1)S(1)} %get-tuple-element.32), channel_id=1, source_target_pairs={{0,7},{1,6},{2,5},{3,4},{4,3},{5,2},{6,1},{7,0},{8,15},{9,14},{10,... | collective-permute-start | bytes 294920 | tf_op jit(solution)/shard_map/ppermute | solution.py:26
  34.6 8.3 %collective-permute-start.6 = (bf16[384,128]{1,0:T(8,128)(2,1)S(1)}, bf16[384,128]{1,0:T(8,128)(2,1)S(1)}, u32[]{:S(2)}, u32[]{:S(2)}) collective-permute-start(bf16[384,128]{1,0:T(8,128)(2,1)S(1)} %get-tuple-element.32), channel_id=1, source_target_pairs={{0,3},{1,2},{2,1},{3,0},{4,7},{5,6},{6,5},{7,4},{8,11},{9,10},{10,... | collective-permute-start | bytes 294920 | tf_op jit(solution)/shard_map/ppermute | solution.py:26
  35.8 7.1 %collective-permute-start.8 = (bf16[256,128]{1,0:T(8,128)(2,1)S(1)}, bf16[256,128]{1,0:T(8,128)(2,1)S(1)}, u32[]{:S(2)}, u32[]{:S(2)}) collective-permute-start(bf16[256,128]{1,0:T(8,128)(2,1)S(1)} %slice.35), channel_id=1, source_target_pairs={{0,4},{1,5},{2,6},{3,7},{4,0},{5,1},{6,2},{7,3},{8,12},{9,13},{10,... | collective-permute-start | bytes 196616 | tf_op jit(solution)/shard_map/ppermute | solution.py:26
  37.8 1.0 %copy-start.9 = (bf16[128,1024]{1,0:T(8,128)(2,1)S(1)}, bf16[128,1024]{1,0:T(8,128)(2,1)}, u32[]{:S(2)}) copy-start(bf16[128,1024]{1,0:T(8,128)(2,1)} %constant_dynamic-update-slice_fusion.near_ref) | copy-start | bytes 786436
  43.5 3.1 %collective-permute-start.9 = (bf16[320,128]{1,0:T(8,128)(2,1)S(1)}, bf16[320,128]{1,0:T(8,128)(2,1)S(1)}, u32[]{:S(2)}, u32[]{:S(2)}) collective-permute-start(bf16[320,128]{1,0:T(8,128)(2,1)S(1)} %get-tuple-element.34), channel_id=1, source_target_pairs={{0,8},{8,0},{16,24},{24,16},{1,9},{9,1},{17,25},{25,17},{2,10},{10... | collective-permute-start | bytes 245768 | tf_op jit(solution)/shard_map/ppermute | solution.py:26
  47.9 4.0 %collective-permute-start.10 = (bf16[192,128]{1,0:T(8,128)(2,1)}, bf16[192,128]{1,0:T(8,128)(2,1)}, u32[]{:S(2)}, u32[]{:S(2)}) collective-permute-start(bf16[192,128]{1,0:T(8,128)(2,1)} %get-tuple-element.36), channel_id=1, source_target_pairs={{0,24},{8,16},{16,8},{24,0},{1,25},{9,17},{17,9},{25,1},{2,26},{10... | collective-permute-start | bytes 147464 | tf_op jit(solution)/shard_map/ppermute | solution.py:26
  49.8 16.7 %copy-start.3 = (f32[2,1,768,128]{3,2,1,0:T(8,128)S(1)}, f32[2,1,768,128]{3,2,1,0:T(8,128)}, u32[]{:S(2)}) copy-start(f32[2,1,768,128]{3,2,1,0:T(8,128)} %rhs_ref.5) | copy-start | bytes 2359300
  52.0 1.1 %copy-start.8 = (f32[2,768,128]{2,1,0:T(8,128)S(1)}, f32[2,768,128]{2,1,0:T(8,128)}, u32[]{:S(2)}) copy-start(f32[2,768,128]{2,1,0:T(8,128)} %copy-done.7) | copy-start | bytes 2359300
  53.1 0.9 %copy-start.11 = (bf16[384,128]{1,0:T(8,128)(2,1)S(1)}, bf16[384,128]{1,0:T(8,128)(2,1)}, u32[]{:S(2)}) copy-start(bf16[384,128]{1,0:T(8,128)(2,1)} %copy-done.10) | copy-start | bytes 294916
  54.0 0.9 %copy-start.13 = (bf16[384,128]{1,0:T(8,128)(2,1)S(1)}, bf16[384,128]{1,0:T(8,128)(2,1)}, u32[]{:S(2)}) copy-start(bf16[384,128]{1,0:T(8,128)(2,1)} %copy-done.12) | copy-start | bytes 294916
  54.9 0.9 %copy-start.15 = (bf16[384,128]{1,0:T(8,128)(2,1)S(1)}, bf16[384,128]{1,0:T(8,128)(2,1)}, u32[]{:S(2)}) copy-start(bf16[384,128]{1,0:T(8,128)(2,1)} %copy-done.14) | copy-start | bytes 294916
  55.8 0.8 %copy-start.19 = (f32[128,128]{1,0:T(8,128)S(1)}, f32[128,128]{1,0:T(8,128)}, u32[]{:S(2)}) copy-start(f32[128,128]{1,0:T(8,128)} %copy-done.18) | copy-start | bytes 196612
  59.8 9.5 %collective-permute-start.13 = (bf16[128,128]{1,0:T(8,128)(2,1)S(1)}, bf16[128,128]{1,0:T(8,128)(2,1)S(1)}, u32[]{:S(2)}, u32[]{:S(2)}) collective-permute-start(bf16[128,128]{1,0:T(8,128)(2,1)S(1)} %get-tuple-element.42), channel_id=1, source_target_pairs={{0,1},{1,0},{2,3},{3,2},{4,5},{5,4},{6,7},{7,6},{8,9},{9,8},{10,11... | collective-permute-start | bytes 98312 | tf_op jit(solution)/shard_map/ppermute | solution.py:26
  60.1 9.2 %collective-permute-start.14 = (bf16[128,128]{1,0:T(8,128)(2,1)S(1)}, bf16[128,128]{1,0:T(8,128)(2,1)S(1)}, u32[]{:S(2)}, u32[]{:S(2)}) collective-permute-start(bf16[128,128]{1,0:T(8,128)(2,1)S(1)} %get-tuple-element.43), channel_id=1, source_target_pairs={{1,2},{3,4},{5,6},{2,1},{4,3},{6,5},{9,10},{11,12},{13,14},{10,9},... | collective-permute-start | bytes 98312 | tf_op jit(solution)/shard_map/ppermute | solution.py:443
  63.3 4.0 %collective-permute-start.11 = (bf16[64,128]{1,0:T(8,128)(2,1)S(1)}, bf16[64,128]{1,0:T(8,128)(2,1)S(1)}, u32[]{:S(2)}, u32[]{:S(2)}) collective-permute-start(bf16[64,128]{1,0:T(8,128)(2,1)S(1)} %get-tuple-element.40), channel_id=1, source_target_pairs={{0,8},{8,0},{16,24},{24,16},{1,9},{9,1},{17,25},{25,17},{2,10},{10... | collective-permute-start | bytes 49160 | tf_op jit(solution)/shard_map/ppermute | solution.py:26
  64.2 5.0 %collective-permute-start.12 = (bf16[64,128]{1,0:T(8,128)(2,1)S(1)}, bf16[64,128]{1,0:T(8,128)(2,1)S(1)}, u32[]{:S(2)}, u32[]{:S(2)}) collective-permute-start(bf16[64,128]{1,0:T(8,128)(2,1)S(1)} %get-tuple-element.41), channel_id=1, source_target_pairs={{8,16},{16,8},{9,17},{17,9},{10,18},{18,10},{11,19},{19,11},{12,20... | collective-permute-start | bytes 49160 | tf_op jit(solution)/shard_map/ppermute | solution.py:443
  (6 other events, 4.0 us)

commit v2 on v0

v2 whole, which is shorter than its diff:
```python
import functools
import jax
import jax.numpy as jnp
from jax import lax
from jax.experimental import pallas as pl
from jax.experimental.pallas import tpu as pltpu
from jax.sharding import PartitionSpec as P

F32 = jnp.float32
BF16 = jnp.bfloat16
CONTRACT_FIRST = (((0,), (0,)), ((), ()))


def bits_of(count):
    return count.bit_length() - 1


def mask_of(step):
    return (1 << step) - 1


def mirror(bit):
    return (2 << bit) - 2


def swap(value, axis, mask):
    count = lax.axis_size(axis)
    return lax.ppermute(value, axis, [(i, i ^ mask) for i in range(count)])


def other(value, axis, closed=False):
    count = lax.axis_size(axis)
    pairs = [(i, i + 1) for i in range(1, count - 1, 2)] + [(0, count - 1)] * closed
    return lax.ppermute(value, axis, pairs + [(j, i) for i, j in pairs])


def relative_block(block, device, steps):
    left = block ^ device
    place = left * 0
    for step in range(steps, 0, -1):
        bit = (left >> (step - 1)) & 1
        place = place | (bit << (steps - step))
        left = left ^ (bit * mask_of(step))
    return place


def halves(value):
    high = value.astype(BF16)
    low = (value - high.astype(F32)).astype(BF16)
    return jnp.concatenate([high, low], axis=1)


def joined(value):
    width = value.shape[1] // 2
    return value[:, :width] + value[:, width:]


def mm(left, right):
    return jnp.dot(left, right, preferred_element_type=F32)


def copies_of(pairs, semaphores):
    copies = [
        pltpu.make_async_copy(source, target, semaphores.at[i])
        for i, (source, target) in enumerate(pairs)
    ]
    for copy in copies:
        copy.start()
    return copies


def terms_kernel(
    steps, rhs_hbm, basis_hbm, ids_hbm, keep_ref, send_ref, low_ref, rhs_ref, basis_ref, ids_ref, sems
):
    device = lax.axis_index("gx")
    subs, functions, _ = basis_ref.shape
    pairs = [(ids_hbm, ids_ref)]
    for s in range(subs):
        pairs += [(basis_hbm.at[s, 0], basis_ref.at[s]), (rhs_hbm.at[s, 0], rhs_ref.at[s])]
    copies = copies_of(pairs, sems)
    half, width = keep_ref.shape
    order = 2 * half
    block = order >> steps
    copies[0].wait()
    ids = jnp.concatenate([ids_ref[s] for s in range(subs)], axis=1)
    row = lax.broadcasted_iota(jnp.int32, (16, ids.shape[1]), 0)
    coded = jnp.where(row == 0, ids // 256, jnp.where(row == 1, ids % 256, 0))
    send_ref[half:] = coded.astype(F32).astype(BF16)
    place = relative_block(ids // block, device, steps) * block + ids % block
    rows = lax.broadcasted_iota(jnp.int32, (order, ids.shape[1]), 0)
    pick = (rows == place).astype(BF16)
    terms = []
    for s in range(subs):
        copies[1 + 2 * s].wait()
        copies[2 + 2 * s].wait()
        value = rhs_ref[s]
        high = value.astype(BF16)
        low = (value - high.astype(F32)).astype(BF16)
        low_ref[s] = high
        terms.append(joined(mm(basis_ref[s], jnp.concatenate([high, low], axis=1))))
    total = joined(mm(pick, halves(jnp.concatenate(terms, axis=0))))
    keep_ref[...] = total[:half]
    send_ref[:half] = total[half:].astype(BF16)


def halve_kernel(known, keep_ref, got_ref, sent_ref, next_ref, send_ref):
    rows = keep_ref.shape[0]
    half = rows // 2
    total = keep_ref[...] + got_ref[:rows].astype(F32)
    next_ref[...] = total[:half]
    send_ref[:half] = total[half:].astype(BF16)
    send_ref[half : half + known] = sent_ref[rows:]
    send_ref[half + known :] = got_ref[rows:]


def join_kernel(near_ref, far_ref, token_ref, out_ref):
    rows = near_ref.shape[0]
    out_ref[:rows] = near_ref[...]
    out_ref[rows:] = far_ref[...]


def sum_kernel(keep_ref, got_ref, *rest):
    halo_refs, next_ref, send_ref = rest[:-2], rest[-2], rest[-1]
    rows = keep_ref.shape[0]
    total = keep_ref[...] + got_ref[:rows].astype(F32)
    next_ref[...] = total
    send_ref[:rows] = total.astype(BF16)
    at = rows
    for ref in halo_refs:
        send_ref[at : at + ref.shape[0]] = ref[...]
        at += ref.shape[0]


def forward_kernel(keep_ref, got_ref, next_ref, send_ref):
    rows = keep_ref.shape[0]
    total = keep_ref[...] + got_ref[:rows].astype(F32)
    next_ref[...] = total
    send_ref[:rows] = total.astype(BF16)
    start = got_ref.shape[0] - (send_ref.shape[0] - rows)
    send_ref[rows:] = got_ref[start:]


def outward(width, groups, subs, send_xp, send_xo, send_yp, send_yo):
    even_x = lax.axis_index("gx") % 2 == 0
    even_y = lax.axis_index("gy") % 2 == 0
    west, east = groups(0, 0), groups(subs - 1, 1)
    send_xp[...] = jnp.where(even_x, east, west)
    send_xo[...] = jnp.where(even_x, west, east)
    for s in range(subs):
        south, north = groups(s, 2), groups(s, 3)
        send_yp[s * width : (s + 1) * width] = jnp.where(even_y, north, south)
        send_yo[s * width : (s + 1) * width] = jnp.where(even_y, south, north)


def solve_kernel(width, inverse_ref, rhs_ref, token_ref, own_ref, margin_ref, *sends):
    subs, rows, _ = own_ref.shape
    for s in range(subs):
        value = mm(inverse_ref[s, 0], rhs_ref[s])
        own_ref[s] = value[:rows]
        margin_ref[s] = value[rows:].astype(BF16)

    def groups(sub, number):
        return margin_ref[sub, number * width : (number + 1) * width]

    outward(width, groups, subs, *sends)


def pick_kernel(places, rows_ref, token_ref, *rest):
    id_refs, out_ref = rest[:-1], rest[-1]
    order = rows_ref.shape[1]
    width = id_refs[0].shape[1]
    names = lax.broadcasted_iota(jnp.int32, (order, width), 0)
    rows = rows_ref[...]
    for q, (holder, start) in enumerate(places):
        code = id_refs[holder][start : start + 16].astype(F32)
        ids = (code[0:1] * 256.0 + code[1:2]).astype(jnp.int32)
        pick = (names == ids).astype(BF16)
        out_ref[q * width : (q + 1) * width] = mm(rows, pick).T.astype(BF16)


def arranged(low, masks, first):
    device = lax.axis_index("gy")
    rows = low.shape[0]
    per_device = rows >> len(masks)
    half = rows // 2
    place = lax.broadcasted_iota(jnp.int32, (half, rows), 0) + first
    target = lax.broadcasted_iota(jnp.int32, (half, rows), 1)
    piece = place // per_device
    source = piece * 0 + device
    for bit, mask in enumerate(masks):
        source = source ^ (((piece >> bit) & 1) * mask)
    pick = (source * per_device + place % per_device == target).astype(BF16)
    return mm(pick, low).astype(BF16)


def coarse_kernel(rows, masks, near_ref, far_ref, keep_ref, halo_ref, *rest):
    got_refs, next_ref, send_ref = rest[:-2], rest[-2], rest[-1]
    total = keep_ref[...]
    for ref in got_refs:
        total = total + ref[:rows].astype(F32)
    low = total.astype(BF16)
    half = next_ref.shape[0]
    value = mm(near_ref[...], arranged(low, masks, 0))
    value = value + mm(far_ref[...], arranged(low, masks, rows // 2))
    next_ref[...] = value[:half]
    send_ref[:half] = value[half:].astype(BF16)
    send_ref[half:] = halo_ref[...]


def halve_halo_kernel(keep_ref, got_ref, halo_ref, next_ref, send_ref):
    rows = keep_ref.shape[0]
    half = rows // 2
    total = keep_ref[...] + got_ref[:rows].astype(F32)
    next_ref[...] = total[:half]
    send_ref[:half] = total[half:].astype(BF16)
    send_ref[half:] = halo_ref[...]


def spread_pick(rows, spill):
    spill = jnp.concatenate([spill[d : d + 1] for d in range(4)], axis=1)
    iota = lax.broadcasted_iota(jnp.int32, (rows, spill.shape[1]), 0)
    return (iota == spill).astype(BF16)


def received(subs, sub, width, groups, pair_x, other_x, pair_y, other_y, even_x, even_y):
    west = groups(sub - 1, 1) if sub > 0 else jnp.where(even_x, other_x, pair_x)
    east = groups(sub + 1, 0) if sub < subs - 1 else jnp.where(even_x, pair_x, other_x)
    rows = slice(sub * width, (sub + 1) * width)
    south = jnp.where(even_y, other_y[rows], pair_y[rows])
    north = jnp.where(even_y, pair_y[rows], other_y[rows])
    return jnp.concatenate([west, east, south, north], axis=0)


def other_neighbour(axis):
    device = lax.axis_index(axis)
    even = device % 2 == 0
    other = jnp.where(even, device - 1, device + 1)
    return device, even, other


def from_other(axis, refs, masks, distance):
    device, even, _ = other_neighbour(axis)
    source = jnp.where(even, device - distance, device + distance)
    size, refs = refs
    value = jnp.zeros((size, refs[0].shape[1]), BF16)
    for ref, mask in zip(refs, masks):
        value = jnp.where((device ^ mask) == source, ref[ref.shape[0] - size :], value)
    return even, value


def correction_kernel(
    count_x, width, own_ref, margin_ref, spill_ref, basis_ref, operator_ref, keep_ref, *rest
):
    x_refs, rest = rest[:count_x], rest[count_x:]
    y_refs, (out_ref, low_ref, image_ref, *sends) = rest[:-7], rest[-7:]
    subs, rows, columns = own_ref.shape
    functions = basis_ref.shape[2]
    picked = keep_ref[...] + x_refs[-1][: keep_ref.shape[0]].astype(F32)
    halo = subs * width
    x_masks = [mask_of(step) for step in range(2, len(x_refs) + 1)]
    y_masks = [mirror(bit) for bit in range(1, len(y_refs))]
    even_x, other_x = from_other("gx", (width, x_refs[1:]), x_masks, 1)
    even_y, other_y = from_other("gy", (halo, y_refs[1:]), y_masks, 2)
    pair_x = x_refs[0][x_refs[0].shape[0] - width :]
    first = y_refs[0].shape[0] - 2 * halo
    pair_y = y_refs[0][first : first + halo]

    def margins(sub, number):
        return margin_ref[sub, number * width : (number + 1) * width]

    for s in range(subs):
        values = received(
            subs, s, width, margins, pair_x, other_x, pair_y, other_y, even_x, even_y
        )
        part = picked[s * functions : (s + 1) * functions]
        high = part.astype(BF16)
        low = (part - high.astype(F32)).astype(BF16)
        basis = basis_ref[s, 0]
        coarse = lax.dot_general(
            jnp.concatenate([basis, basis], axis=0),
            jnp.concatenate([high, low], axis=0),
            CONTRACT_FIRST,
            preferred_element_type=F32,
        )
        value = own_ref[s] + mm(spread_pick(rows, spill_ref[s, 0]), values) + coarse
        out_ref[s] = value
        low = value.astype(BF16)
        low_ref[s] = low
        image_ref[s] = mm(operator_ref[s, 0, rows:], low).astype(BF16)

    def images(sub, number):
        return image_ref[sub, number * width : (number + 1) * width]

    outward(width, images, subs, *sends)


def image_kernel(operator_ref, low_ref, rhs_ref, correction_ref, part_ref, out_ref, sems):
    subs, rows, _ = low_ref.shape
    copies = copies_of([(correction_ref.at[s], out_ref.at[s, 0]) for s in range(subs)], sems)
    for s in range(subs):
        part_ref[s] = rhs_ref[s, 0] - mm(operator_ref[s, 0, :rows], low_ref[s])
    for copy in copies:
        copy.wait()


def residual_kernel(
    width, part_ref, image_ref, spill_ref, xp_ref, xo_ref, yp_ref, yo_ref, out_ref, value_ref, sems
):
    subs, rows, _ = part_ref.shape
    even_x = lax.axis_index("gx") % 2 == 0
    even_y = lax.axis_index("gy") % 2 == 0

    def margins(sub, number):
        return image_ref[sub, number * width : (number + 1) * width]

    device, count = lax.axis_index("gx"), lax.axis_size("gx")
    inner = jnp.logical_and(device != 0, device != count - 1)
    other_x = jnp.where(inner, xo_ref[...], jnp.zeros(xo_ref.shape, BF16))
    copies = []
    for s in range(subs):
        values = received(
            subs, s, width, margins, xp_ref[...], other_x, yp_ref[...], yo_ref[...],
            even_x, even_y,
        )
        value_ref[s] = part_ref[s] - mm(spread_pick(rows, spill_ref[s, 0]), values)
        copies.append(pltpu.make_async_copy(value_ref.at[s], out_ref.at[s, 0], sems.at[s]))
        copies[s].start()
    for copy in copies:
        copy.wait()


VMEM = pl.BlockSpec(memory_space=pltpu.VMEM)
HBM = pl.BlockSpec(memory_space=pltpu.HBM)
ANY = pl.BlockSpec(memory_space=pl.ANY)
MIB = 1024 * 1024


def call(kernel, outs, args, name, scratch=(), ins=None, out_specs=None, limit=4, cost=10**9):
    return pl.pallas_call(
        kernel,
        out_shape=[jax.ShapeDtypeStruct(shape, dtype) for shape, dtype in outs],
        in_specs=ins or [VMEM] * len(args),
        out_specs=out_specs or [VMEM] * len(outs),
        scratch_shapes=list(scratch),
        compiler_params=pltpu.CompilerParams(vmem_limit_bytes=limit * MIB),
        cost_estimate=pl.CostEstimate(flops=cost, bytes_accessed=MIB, transcendentals=0),
        name=name,
    )(*args)


def body(
    adjoint_rhs, local_inverse, local_operator, spill_rows, coarse_basis, coarse_ids, coarse_inverse
):
    subs, _, rows, width = adjoint_rhs.shape
    margin = spill_rows.shape[3]
    functions = coarse_ids.shape[2]
    order = coarse_inverse.shape[1]
    count_x, count_y = lax.axis_size("gx"), lax.axis_size("gy")
    steps_x, steps_y = bits_of(count_x), bits_of(count_y)
    listed = subs * functions
    halo = subs * margin
    dma = pltpu.SemaphoreType.DMA
    block = (subs, rows, width)
    messages = [((margin, width), BF16)] * 2 + [((halo, width), BF16)] * 2

    gather_masks = [1 << (steps_y - 1 - i) for i in range(steps_y)]
    near = coarse_inverse
    far = swap(near, "gy", gather_masks[0])

    size = order // 2
    keep, send, low = call(
        functools.partial(terms_kernel, steps_x),
        [((size, width), F32), ((size + 16, listed), BF16), (block, BF16)],
        [pltpu.with_memory_space_constraint(x, pltpu.HBM) for x in (adjoint_rhs, coarse_basis, coarse_ids)],
        "coarse_terms",
        ins=[HBM] * 3,
        scratch=[
            pltpu.VMEM(block, F32),
            pltpu.VMEM((subs, functions, rows), BF16),
            pltpu.VMEM(coarse_ids.shape, jnp.int32),
            dma((1 + 2 * subs,)),
        ],
        limit=12,
    )
    got = swap(send, "gx", mask_of(1))
    id_places = [(send, size, 0)]
    for step in range(2, steps_x + 1):
        half = size // 2
        known = 16 * len(id_places)
        id_places = id_places + [(got, size + 16 * i, 0) for i in range(len(id_places))]
        keep, send = call(
            functools.partial(halve_kernel, known),
            [((half, width), F32), ((half + 2 * known, listed), BF16)],
            [keep, got, send],
            "coarse_halve",
        )
        got = swap(send, "gx", mask_of(step))
        size = half
    id_places = id_places + [(got, size + 16 * i, 0) for i in range(len(id_places))]

    own, margins, halo_xp, halo_xo, halo_yp, halo_yo = call(
        functools.partial(solve_kernel, margin),
        [(block, F32), ((subs, 4 * margin, width), BF16)] + messages,
        [local_inverse, low, send],
        "local_solve",
        ins=[VMEM, VMEM, ANY],
        limit=12,
    )

    def join(near, far, token):
        shape = (2 * near.shape[0], near.shape[1])
        return call(
            join_kernel, [(shape, BF16)], [near, far, token], "inverse_join", ins=[VMEM, VMEM, ANY]
        )[0]

    near = join(near, far, own)
    far = swap(near, "gy", gather_masks[1])

    keep, send = call(
        sum_kernel,
        [((size, width), F32), ((size + 2 * halo, width), BF16)],
        [keep, got, halo_yp, halo_yo],
        "coarse_sum",
    )
    got = swap(send, "gy", mask_of(1))
    y_got = [got]
    for mask in gather_masks[2:]:
        near = join(near, far, got)
        far = swap(near, "gy", mask)
    pending = [got]
    bit = 1
    while bit < steps_y:
        for extra in pending[1:]:
            keep = keep + extra[:size].astype(F32)
        keep, send = call(
            forward_kernel,
            [((size, width), F32), ((size + halo, width), BF16)],
            [keep, pending[0]],
            "coarse_sum",
        )
        masks = [mirror(bit)] + [mirror(bit + 1)] * (bit + 1 < steps_y)
        pending = [swap(send, "gy", mask) for mask in masks]
        y_got += pending
        if len(masks) > 1:
            pending.append(swap(send[:size], "gy", masks[0] ^ masks[1]))
        bit += 2

    holders, places = [], []
    for q in range(count_x):
        p = sum(((q >> (steps_x - k)) & 1) << (k - 1) for k in range(1, steps_x + 1))
        array, start, _ = id_places[p]
        found = [i for i, holder in enumerate(holders) if holder is array]
        if not found:
            holders.append(array)
            found = [len(holders) - 1]
        places.append((found[0], start))
    def picked(value, token):
        return call(
            functools.partial(pick_kernel, places),
            [((count_x * listed, value.shape[0]), BF16)],
            [value, token, *holders],
            "inverse_pick",
            ins=[VMEM, ANY] + [VMEM] * len(holders),
            limit=8,
        )[0]

    near, far = picked(near, send), picked(far, send)

    half = count_x * listed // 2
    keep, send = call(
        functools.partial(coarse_kernel, size, gather_masks),
        [((half, width), F32), ((half + margin, width), BF16)],
        [near, far, keep, halo_xp, *pending],
        "coarse_solve",
    )
    x_got = [swap(send, "gx", mask_of(1))]
    for step in range(2, steps_x + 1):
        half = half // 2
        keep, send = call(
            halve_halo_kernel,
            [((half, width), F32), ((half + margin, width), BF16)],
            [keep, x_got[-1], halo_xo],
            "picked_halve",
        )
        x_got.append(swap(send, "gx", mask_of(step)))

    correction, low, image, *sends = call(
        functools.partial(correction_kernel, len(x_got), margin),
        [(block, F32), (block, BF16), ((subs, 4 * margin, width), BF16)] + messages,
        [own, margins, spill_rows, coarse_basis, local_operator, keep, *x_got, *y_got],
        "correction",
        limit=12,
    )

    got_yo = other(sends[3], "gy")
    got_xo = other(sends[1], "gx", closed=True)
    got_yp = swap(sends[2], "gy", 1)
    got_xp = swap(sends[0], "gx", 1)

    part, correction = call(
        image_kernel,
        [(block, F32), (adjoint_rhs.shape, F32)],
        [local_operator, low, adjoint_rhs, correction],
        "image_own",
        out_specs=[VMEM, HBM],
        scratch=[dma((subs,))],
        limit=12,
    )
    (residual,) = call(
        functools.partial(residual_kernel, margin),
        [(adjoint_rhs.shape, F32)],
        [part, image, spill_rows, got_xp, got_xo, got_yp, got_yo],
        "residual",
        out_specs=[HBM],
        scratch=[pltpu.VMEM(block, F32), dma((subs,))],
    )
    return correction, residual


def solution(mesh):
    in_specs = (
        P("gx", "gy", None, None),
        P("gx", "gy", None, None),
        P("gx", "gy", None, None),
        P("gx", "gy", None, None),
        P("gx", "gy", None, None),
        P("gx", "gy", None),
        P(("gx", "gy"), None),
    )
    out_specs = (P("gx", "gy", None, None), P("gx", "gy", None, None))
    return jax.shard_map(body, mesh=mesh, in_specs=in_specs, out_specs=out_specs, check_vma=False)
```

time: 227 us -> 44.2 us (0.19)
  the two profiles are of different devices: /device:TPU:6 before, /device:TPU:2 now
where the time goes in v2:
time: 44.2 us; the launch traced here: 44.1 us
  waiting for transfers between devices  17.9 us (40%)
  starting transfers between devices  17.5 us (40%)
  Pallas kernels  7.81 us (18%)
  between operations  0.82 us (2%)
    ppermute x13, waiting for transfers between devices, swap(): return lax.ppermute(value, axis, [(i, i ^ mask) for i in range(count)])  14.6 us
    ppermute x13, starting transfers between devices, swap(): return lax.ppermute(value, axis, [(i, i ^ mask) for i in range(count)])  13.6 us
    pallas_call x14, Pallas kernels, call(): pl.pallas_call(kernel, out_shape=[jax.ShapeDtypeStruct(shape, dtype) for...  7.81 us
    ppermute x2, starting transfers between devices, other(): return lax.ppermute(value, axis, pairs + [(j, i) for i, j in pairs])  3.86 us
    ppermute x2, waiting for transfers between devices, other(): return lax.ppermute(value, axis, pairs + [(j, i) for i, j in pairs])  3.36 us
  transfers between devices with their start and end apart: 15, of which 8 were waited for; matrix products, arithmetic and copies ran while one was open for 0% of the time, Pallas kernels for 7%

profile of v2, /device:TPU:2, one launch (start us, length us, event | category | flops | bytes accessed | tf_op | source)
XLA Modules:
  0.0 44.1 jit_solution(1737121840793419751)
XLA Ops:
  0.7 2.0 %coarse_terms.1 = (f32[512,128]{1,0:T(8,128)S(1)}, bf16[528,128]{1,0:T(8,128)(2,1)S(1)}, bf16[2,768,128]{2,1,0:T(8,128)(2,1)S(1)}) custom-call(f32[2,1,768,128]{3,2,1,0:T(8,128)} %rhs_ref.1, bf16[2,1,64,768]{3,2,1,0:T(8,128)(2,1)} %basis_ref.1, s32[2,1,64]{2,1,0:T(1,128)} %ids_hbm.1), custom_call_target="tpu_custom_call" | custom-call | flops 1000000000 | bytes 1048576 | tf_op jit(solution)/shard_map/coarse_terms/pallas_call | solution.py:339
  2.7 0.1 collective-permute-start
  2.8 2.7 %collective-permute-start.1 = (bf16[32,1024]{1,0:T(8,128)(2,1)S(1)}, bf16[32,1024]{1,0:T(8,128)(2,1)S(1)}, u32[]{:S(2)}, u32[]{:S(2)}) collective-permute-start(bf16[32,1024]{1,0:T(8,128)(2,1)S(1)} %copy-done.5), channel_id=1, source_target_pairs={{0,4},{1,5},{2,6},{3,7},{4,0},{5,1},{6,2},{7,3},{8,12},{9,13},{10,... | collective-permute-start | bytes 196616 | tf_op jit(solution)/shard_map/ppermute | solution.py:28
  5.4 1.4 %collective-permute-start.3 = (bf16[288,128]{1,0:T(8,128)(2,1)S(1)}, bf16[288,128]{1,0:T(8,128)(2,1)S(1)}, u32[]{:S(2)}, u32[]{:S(2)}) collective-permute-start(bf16[288,128]{1,0:T(8,128)(2,1)S(1)} %get-tuple-element.33.token_ref), channel_id=1, source_target_pairs={{0,24},{8,16},{16,8},{24,0},{1,25},{9,17},{17,9},{25,1},{2,26},{10... | collective-permute-start | bytes 221192 | tf_op jit(solution)/shard_map/ppermute | solution.py:28
  6.8 1.0 %local_solve.1 = (f32[2,768,128]{2,1,0:T(8,128)S(1)}, bf16[2,256,128]{2,1,0:T(8,128)(2,1)S(1)}, bf16[64,128]{1,0:T(8,128)(2,1)S(1)}, bf16[64,128]{1,0:T(8,128)(2...) custom-call(bf16[2,1,1024,768]{3,2,1,0:T(8,128)(2,1)S(1)} %copy-done.4, ...), custom_call_target="tpu_custom_call" | custom-call | flops 1000000000 | bytes 1048576 | tf_op jit(solution)/shard_map/local_solve/pallas_call | solution.py:339
  7.8 1.8 %collective-permute-done.1.far_ref = bf16[32,1024]{1,0:T(8,128)(2,1)S(1)} collective-permute-done((bf16[32,1024]{1,0:T(8,128)(2,1)S(1)}, bf16[32,1024]{1,0:T(8,128)(2,1)S(1)}, u32[]{:S(2)}, u32[]{:S(2)}) %collective-permute-start.1) | collective-permute-done | bytes 65568 | tf_op jit(solution)/shard_map/ppermute | solution.py:28
  9.6 0.8 %collective-permute-start.2 = (bf16[64,1024]{1,0:T(8,128)(2,1)S(1)}, bf16[64,1024]{1,0:T(8,128)(2,1)S(1)}, u32[]{:S(2)}, u32[]{:S(2)}) collective-permute-start(bf16[64,1024]{1,0:T(8,128)(2,1)S(1)} %inverse_join.2.near_ref), channel_id=1, source_target_pairs={{0,2},{1,3},{2,0},{3,1},{4,6},{5,7},{6,4},{7,5},{8,10},{9,11},{10,... | collective-permute-start | bytes 393224 | tf_op jit(solution)/shard_map/ppermute | solution.py:28
  10.4 0.6 %collective-permute-start.4 = (bf16[512,128]{1,0:T(8,128)(2,1)S(1)}, bf16[512,128]{1,0:T(8,128)(2,1)S(1)}, u32[]{:S(2)}, u32[]{:S(2)}) collective-permute-start(bf16[512,128]{1,0:T(8,128)(2,1)S(1)} %get-tuple-element.39), channel_id=1, source_target_pairs={{0,1},{1,0},{2,3},{3,2},{4,5},{5,4},{6,7},{7,6},{8,9},{9,8},{10,11... | collective-permute-start | bytes 393224 | tf_op jit(solution)/shard_map/ppermute | solution.py:28
  11.0 3.6 %collective-permute-done.2.far_ref = bf16[64,1024]{1,0:T(8,128)(2,1)S(1)} collective-permute-done((bf16[64,1024]{1,0:T(8,128)(2,1)S(1)}, bf16[64,1024]{1,0:T(8,128)(2,1)S(1)}, u32[]{:S(2)}, u32[]{:S(2)}) %collective-permute-start.2) | collective-permute-done | bytes 131104 | tf_op jit(solution)/shard_map/ppermute | solution.py:28
  14.6 1.0 %collective-permute-done.4.token_ref.got_ref.rest_2_ = bf16[512,128]{1,0:T(8,128)(2,1)S(1)} collective-permute-done((bf16[512,128]{1,0:T(8,128)(2,1)S(1)}, bf16[512,128]{1,0:T(8,128)(2,1)S(1)}, u32[]{:S(2)}, u32[]{:S(2)}) %collective-permute-start.4) | collective-permute-done | bytes 131104 | tf_op jit(solution)/shard_map/ppermute | solution.py:28
  15.6 0.6 %collective-permute-start.5 = (bf16[128,1024]{1,0:T(8,128)(2,1)S(1)}, bf16[128,1024]{1,0:T(8,128)(2,1)S(1)}, u32[]{:S(2)}, u32[]{:S(2)}) collective-permute-start(bf16[128,1024]{1,0:T(8,128)(2,1)S(1)} %inverse_join.3.rows_ref), channel_id=1, source_target_pairs={{0,1},{1,0},{2,3},{3,2},{4,5},{5,4},{6,7},{7,6},{8,9},{9,8},{10,11... | collective-permute-start | bytes 786440 | tf_op jit(solution)/shard_map/ppermute | solution.py:28
  16.3 3.2 %collective-permute-start.7 = (bf16[384,128]{1,0:T(8,128)(2,1)S(1)}, bf16[384,128]{1,0:T(8,128)(2,1)S(1)}, u32[]{:S(2)}, u32[]{:S(2)}) collective-permute-start(bf16[384,128]{1,0:T(8,128)(2,1)S(1)} %get-tuple-element.41.token_ref), channel_id=1, source_target_pairs={{0,6},{1,7},{2,4},{3,5},{4,2},{5,3},{6,0},{7,1},{8,14},{9,15},{10,... | collective-permute-start | bytes 294920 | tf_op jit(solution)/shard_map/ppermute | solution.py:28
  19.4 0.8 %collective-permute-start.6 = (bf16[384,128]{1,0:T(8,128)(2,1)S(1)}, bf16[384,128]{1,0:T(8,128)(2,1)S(1)}, u32[]{:S(2)}, u32[]{:S(2)}) collective-permute-start(bf16[384,128]{1,0:T(8,128)(2,1)S(1)} %get-tuple-element.41.token_ref), channel_id=1, source_target_pairs={{0,2},{1,3},{2,0},{3,1},{4,6},{5,7},{6,4},{7,5},{8,10},{9,11},{10,... | collective-permute-start | bytes 294920 | tf_op jit(solution)/shard_map/ppermute | solution.py:28
  20.3 0.4 %collective-permute-start.8 = (bf16[256,128]{1,0:T(8,128)(2,1)S(1)}, bf16[256,128]{1,0:T(8,128)(2,1)S(1)}, u32[]{:S(2)}, u32[]{:S(2)}) collective-permute-start(bf16[256,128]{1,0:T(8,128)(2,1)S(1)} %slice.3), channel_id=1, source_target_pairs={{0,4},{1,5},{2,6},{3,7},{4,0},{5,1},{6,2},{7,3},{8,12},{9,13},{10,... | collective-permute-start | bytes 196616 | tf_op jit(solution)/shard_map/ppermute | solution.py:28
  20.7 0.5 %inverse_pick.2.near_ref = bf16[512,128]{1,0:T(8,128)(2,1)S(1)} custom-call(bf16[128,1024]{1,0:T(8,128)(2,1)S(1)} %inverse_join.3.rows_ref, bf16[384,128]{1,0:T(8,128)(2,1)S(1)} %get-tuple-element.41.token_ref, bf16[528,128]{1,0:T(8,128)(2,1)S(1)} %get-tuple-element.32.sent_ref.rest_0_, bf16[288,128]{1,0:T(8,128)(2,1)S(1)} %collective-permute-done.3.got_ref.rest_1_, ...), custom_call_target="tpu_custom_call" | custom-call | flops 1000000000 | bytes 1048576 | tf_op jit(solution)/shard_map/inverse_pick/pallas_call | solution.py:339
  21.2 1.6 %collective-permute-done.5.rows_ref = bf16[128,1024]{1,0:T(8,128)(2,1)S(1)} collective-permute-done((bf16[128,1024]{1,0:T(8,128)(2,1)S(1)}, bf16[128,1024]{1,0:T(8,128)(2,1)S(1)}, u32[]{:S(2)}, u32[]{:S(2)}) %collective-permute-start.5) | collective-permute-done | bytes 262176 | tf_op jit(solution)/shard_map/ppermute | solution.py:28
  22.8 0.5 %inverse_pick.3.far_ref = bf16[512,128]{1,0:T(8,128)(2,1)S(1)} custom-call(bf16[128,1024]{1,0:T(8,128)(2,1)S(1)} %collective-permute-done.5.rows_ref, bf16[384,128]{1,0:T(8,128)(2,1)S(1)} %get-tuple-element.41.token_ref, bf16[528,128]{1,0:T(8,128)(2,1)S(1)} %get-tuple-element.32.sent_ref.rest_0_, ...), custom_call_target="tpu_custom_call" | custom-call | flops 1000000000 | bytes 1048576 | tf_op jit(solution)/shard_map/inverse_pick/pallas_call | solution.py:339
  23.3 2.9 %collective-permute-done.8.rest_2_ = bf16[256,128]{1,0:T(8,128)(2,1)S(1)} collective-permute-done((bf16[256,128]{1,0:T(8,128)(2,1)S(1)}, bf16[256,128]{1,0:T(8,128)(2,1)S(1)}, u32[]{:S(2)}, u32[]{:S(2)}) %collective-permute-start.8) | collective-permute-done | bytes 65568 | tf_op jit(solution)/shard_map/ppermute | solution.py:28
  26.2 0.0 copy-start.2
  26.2 0.4 coarse_solve.1
  26.7 0.1 collective-permute-start.9
  26.8 1.3 %collective-permute-done.9.got_ref.rest_0_ = bf16[320,128]{1,0:T(8,128)(2,1)S(1)} collective-permute-done((bf16[320,128]{1,0:T(8,128)(2,1)S(1)}, bf16[320,128]{1,0:T(8,128)(2,1)S(1)}, u32[]{:S(2)}, u32[]{:S(2)}) %collective-permute-start.9) | collective-permute-done | bytes 81952 | tf_op jit(solution)/shard_map/ppermute | solution.py:28
  28.1 1.3 %collective-permute-start.10 = (bf16[192,128]{1,0:T(8,128)(2,1)S(1)}, bf16[192,128]{1,0:T(8,128)(2,1)S(1)}, u32[]{:S(2)}, u32[]{:S(2)}) collective-permute-start(bf16[192,128]{1,0:T(8,128)(2,1)S(1)} %get-tuple-element.48), channel_id=1, source_target_pairs={{0,24},{8,16},{16,8},{24,0},{1,25},{9,17},{17,9},{25,1},{2,26},{10... | collective-permute-start | bytes 147464 | tf_op jit(solution)/shard_map/ppermute | solution.py:28
  29.4 2.4 %collective-permute-done.10.rest_1_ = bf16[192,128]{1,0:T(8,128)(2,1)S(1)} collective-permute-done((bf16[192,128]{1,0:T(8,128)(2,1)S(1)}, bf16[192,128]{1,0:T(8,128)(2,1)S(1)}, u32[]{:S(2)}, u32[]{:S(2)}) %collective-permute-start.10) | collective-permute-done | bytes 49184 | tf_op jit(solution)/shard_map/ppermute | solution.py:28
  31.8 1.0 %correction.1 = (f32[2,768,128]{2,1,0:T(8,128)S(1)}, bf16[2,768,128]{2,1,0:T(8,128)(2,1)S(1)}, bf16[2,256,128]{2,1,0:T(8,128)(2,1)S(1)}, bf16[64,128]{1,0:T(8,12...) custom-call(f32[2,768,128]{2,1,0:T(8,128)S(1)} %get-tuple-element.34.token_ref., ...), custom_call_target="tpu_custom_call" | custom-call | flops 1000000000 | bytes 1048576 | tf_op jit(solution)/shard_map/correction/pallas_call | solution.py:339
  32.9 0.2 collective-permute-start.11
  33.1 1.5 %collective-permute-start.12 = (bf16[64,128]{1,0:T(8,128)(2,1)S(1)}, bf16[64,128]{1,0:T(8,128)(2,1)S(1)}, u32[]{:S(2)}, u32[]{:S(2)}) collective-permute-start(bf16[64,128]{1,0:T(8,128)(2,1)S(1)} %get-tuple-element.55), channel_id=1, source_target_pairs={{8,16},{0,24},{16,8},{24,0},{9,17},{1,25},{17,9},{25,1},{10,18},{2... | collective-permute-start | bytes 49160 | tf_op jit(solution)/shard_map/ppermute | solution.py:34
  34.6 1.5 %collective-permute-start.13 = (bf16[128,128]{1,0:T(8,128)(2,1)S(1)}, bf16[128,128]{1,0:T(8,128)(2,1)S(1)}, u32[]{:S(2)}, u32[]{:S(2)}) collective-permute-start(bf16[128,128]{1,0:T(8,128)(2,1)S(1)} %get-tuple-element.56), channel_id=1, source_target_pairs={{0,1},{1,0},{2,3},{3,2},{4,5},{5,4},{6,7},{7,6},{8,9},{9,8},{10,11... | collective-permute-start | bytes 98312 | tf_op jit(solution)/shard_map/ppermute | solution.py:28
  36.1 2.4 %collective-permute-start.14 = (bf16[128,128]{1,0:T(8,128)(2,1)S(1)}, bf16[128,128]{1,0:T(8,128)(2,1)S(1)}, u32[]{:S(2)}, u32[]{:S(2)}) collective-permute-start(bf16[128,128]{1,0:T(8,128)(2,1)S(1)} %get-tuple-element.57), channel_id=1, source_target_pairs={{1,2},{3,4},{5,6},{2,1},{4,3},{6,5},{9,10},{11,12},{13,14},{10,9},... | collective-permute-start | bytes 98312 | tf_op jit(solution)/shard_map/ppermute | solution.py:34
  38.5 0.9 %image_own.1 = (f32[2,768,128]{2,1,0:T(8,128)S(1)}, f32[2,1,768,128]{3,2,1,0:T(8,128)}) custom-call(bf16[2,1,1024,768]{3,2,1,0:T(8,128)(2,1)S(1)} %copy-done, bf16[2,768,128]{2,1,0:T(8,128)(2,1)S(1)} %get-tuple-element.49.low_ref, f32[2,1,768,128]{3,2,1,0:T(8,128)S(1)} %copy-done.1, f32[2,768,128]{2,1,0:T(8,128)S(1)} %get-tuple-element.50.correction_ref), custom_call_target="tpu_custom_call" | custom-call | flops 1000000000 | bytes 1048576 | tf_op jit(solution)/shard_map/image_own/pallas_call | solution.py:339
  39.4 3.4 %collective-permute-done.14.yo_ref = bf16[128,128]{1,0:T(8,128)(2,1)S(1)} collective-permute-done((bf16[128,128]{1,0:T(8,128)(2,1)S(1)}, bf16[128,128]{1,0:T(8,128)(2,1)S(1)}, u32[]{:S(2)}, u32[]{:S(2)}) %collective-permute-start.14) | collective-permute-done | bytes 32800 | tf_op jit(solution)/shard_map/ppermute | solution.py:34
  42.8 1.3 %residual.1 = f32[2,1,768,128]{3,2,1,0:T(8,128)} custom-call(f32[2,768,128]{2,1,0:T(8,128)S(1)} %get-tuple-element.52.part_ref, bf16[2,256,128]{2,1,0:T(8,128)(2,1)S(1)} %get-tuple-element.53.image_ref, s32[2,1,4,64]{3,2,1,0:T(4,128)S(1)} %copy-done.3, bf16[64,128]{1,0:T(8,128)(2,1)S(1)} %collective-permute-done.11.xp_ref, ...), custom_call_target="tpu_custom_call" | custom-call | flops 1000000000 | bytes 1048576 | tf_op jit(solution)/shard_map/residual/pallas_call | solution.py:339
  (25 shorter events, 0.2 us)
Async XLA Ops:
  0.6 2.1 %copy-start.5 = (bf16[32,1024]{1,0:T(8,128)(2,1)S(1)}, bf16[32,1024]{1,0:T(8,128)(2,1)}, u32[]{:S(2)}) copy-start(bf16[32,1024]{1,0:T(8,128)(2,1)} %near_ref.1) | copy-start | bytes 196612
  0.6 6.2 %copy-start.4 = (bf16[2,1,1024,768]{3,2,1,0:T(8,128)(2,1)S(1)}, bf16[2,1,1024,768]{3,2,1,0:T(8,128)(2,1)}, u32[]{:S(2)}) copy-start(bf16[2,1,1024,768]{3,2,1,0:T(8,128)(2,1)} %inverse_ref.1) | copy-start | bytes 9437188
  2.7 2.7 %collective-permute-start = (bf16[528,128]{1,0:T(8,128)(2,1)S(1)}, bf16[528,128]{1,0:T(8,128)(2,1)S(1)}, u32[]{:S(2)}, u32[]{:S(2)}) collective-permute-start(bf16[528,128]{1,0:T(8,128)(2,1)S(1)} %get-tuple-element.32.sent_ref.rest_0_), channel_id=1, source_target_pairs={{0,8},{8,0},{16,24},{24,16},{1,9},{9,1},{17,25},{25,17},{2,10},{10... | collective-permute-start | bytes 405512 | tf_op jit(solution)/shard_map/ppermute | solution.py:28
  2.8 6.8 %collective-permute-start.1 = (bf16[32,1024]{1,0:T(8,128)(2,1)S(1)}, bf16[32,1024]{1,0:T(8,128)(2,1)S(1)}, u32[]{:S(2)}, u32[]{:S(2)}) collective-permute-start(bf16[32,1024]{1,0:T(8,128)(2,1)S(1)} %copy-done.5), channel_id=1, source_target_pairs={{0,4},{1,5},{2,6},{3,7},{4,0},{5,1},{6,2},{7,3},{8,12},{9,13},{10,... | collective-permute-start | bytes 196616 | tf_op jit(solution)/shard_map/ppermute | solution.py:28
  5.4 4.9 %collective-permute-start.3 = (bf16[288,128]{1,0:T(8,128)(2,1)S(1)}, bf16[288,128]{1,0:T(8,128)(2,1)S(1)}, u32[]{:S(2)}, u32[]{:S(2)}) collective-permute-start(bf16[288,128]{1,0:T(8,128)(2,1)S(1)} %get-tuple-element.33.token_ref), channel_id=1, source_target_pairs={{0,24},{8,16},{16,8},{24,0},{1,25},{9,17},{17,9},{25,1},{2,26},{10... | collective-permute-start | bytes 221192 | tf_op jit(solution)/shard_map/ppermute | solution.py:28
  9.6 5.0 %collective-permute-start.2 = (bf16[64,1024]{1,0:T(8,128)(2,1)S(1)}, bf16[64,1024]{1,0:T(8,128)(2,1)S(1)}, u32[]{:S(2)}, u32[]{:S(2)}) collective-permute-start(bf16[64,1024]{1,0:T(8,128)(2,1)S(1)} %inverse_join.2.near_ref), channel_id=1, source_target_pairs={{0,2},{1,3},{2,0},{3,1},{4,6},{5,7},{6,4},{7,5},{8,10},{9,11},{10,... | collective-permute-start | bytes 393224 | tf_op jit(solution)/shard_map/ppermute | solution.py:28
  10.4 5.2 %collective-permute-start.4 = (bf16[512,128]{1,0:T(8,128)(2,1)S(1)}, bf16[512,128]{1,0:T(8,128)(2,1)S(1)}, u32[]{:S(2)}, u32[]{:S(2)}) collective-permute-start(bf16[512,128]{1,0:T(8,128)(2,1)S(1)} %get-tuple-element.39), channel_id=1, source_target_pairs={{0,1},{1,0},{2,3},{3,2},{4,5},{5,4},{6,7},{7,6},{8,9},{9,8},{10,11... | collective-permute-start | bytes 393224 | tf_op jit(solution)/shard_map/ppermute | solution.py:28
  15.6 7.2 %collective-permute-start.5 = (bf16[128,1024]{1,0:T(8,128)(2,1)S(1)}, bf16[128,1024]{1,0:T(8,128)(2,1)S(1)}, u32[]{:S(2)}, u32[]{:S(2)}) collective-permute-start(bf16[128,1024]{1,0:T(8,128)(2,1)S(1)} %inverse_join.3.rows_ref), channel_id=1, source_target_pairs={{0,1},{1,0},{2,3},{3,2},{4,5},{5,4},{6,7},{7,6},{8,9},{9,8},{10,11... | collective-permute-start | bytes 786440 | tf_op jit(solution)/shard_map/ppermute | solution.py:28
  16.3 10.0 %collective-permute-start.7 = (bf16[384,128]{1,0:T(8,128)(2,1)S(1)}, bf16[384,128]{1,0:T(8,128)(2,1)S(1)}, u32[]{:S(2)}, u32[]{:S(2)}) collective-permute-start(bf16[384,128]{1,0:T(8,128)(2,1)S(1)} %get-tuple-element.41.token_ref), channel_id=1, source_target_pairs={{0,6},{1,7},{2,4},{3,5},{4,2},{5,3},{6,0},{7,1},{8,14},{9,15},{10,... | collective-permute-start | bytes 294920 | tf_op jit(solution)/shard_map/ppermute | solution.py:28
  19.4 6.8 %collective-permute-start.6 = (bf16[384,128]{1,0:T(8,128)(2,1)S(1)}, bf16[384,128]{1,0:T(8,128)(2,1)S(1)}, u32[]{:S(2)}, u32[]{:S(2)}) collective-permute-start(bf16[384,128]{1,0:T(8,128)(2,1)S(1)} %get-tuple-element.41.token_ref), channel_id=1, source_target_pairs={{0,2},{1,3},{2,0},{3,1},{4,6},{5,7},{6,4},{7,5},{8,10},{9,11},{10,... | collective-permute-start | bytes 294920 | tf_op jit(solution)/shard_map/ppermute | solution.py:28
  20.3 5.9 %collective-permute-start.8 = (bf16[256,128]{1,0:T(8,128)(2,1)S(1)}, bf16[256,128]{1,0:T(8,128)(2,1)S(1)}, u32[]{:S(2)}, u32[]{:S(2)}) collective-permute-start(bf16[256,128]{1,0:T(8,128)(2,1)S(1)} %slice.3), channel_id=1, source_target_pairs={{0,4},{1,5},{2,6},{3,7},{4,0},{5,1},{6,2},{7,3},{8,12},{9,13},{10,... | collective-permute-start | bytes 196616 | tf_op jit(solution)/shard_map/ppermute | solution.py:28
  26.2 5.6 %copy-start = (bf16[2,1,1024,768]{3,2,1,0:T(8,128)(2,1)S(1)}, bf16[2,1,1024,768]{3,2,1,0:T(8,128)(2,1)}, u32[]{:S(2)}) copy-start(bf16[2,1,1024,768]{3,2,1,0:T(8,128)(2,1)} %operator_ref.3) | copy-start | bytes 9437188
  26.2 5.6 %copy-start.2 = (bf16[2,1,64,768]{3,2,1,0:T(8,128)(2,1)S(1)}, bf16[2,1,64,768]{3,2,1,0:T(8,128)(2,1)}, u32[]{:S(2)}) copy-start(bf16[2,1,64,768]{3,2,1,0:T(8,128)(2,1)} %basis_ref.1) | copy-start | bytes 589828
  26.2 5.6 %copy-start.3 = (s32[2,1,4,64]{3,2,1,0:T(4,128)S(1)}, s32[2,1,4,64]{3,2,1,0:T(4,128)}, u32[]{:S(2)}) copy-start(s32[2,1,4,64]{3,2,1,0:T(4,128)} %spill_ref.3) | copy-start | bytes 6148
  26.7 1.3 %collective-permute-start.9 = (bf16[320,128]{1,0:T(8,128)(2,1)S(1)}, bf16[320,128]{1,0:T(8,128)(2,1)S(1)}, u32[]{:S(2)}, u32[]{:S(2)}) collective-permute-start(bf16[320,128]{1,0:T(8,128)(2,1)S(1)} %get-tuple-element.45), channel_id=1, source_target_pairs={{0,8},{8,0},{16,24},{24,16},{1,9},{9,1},{17,25},{25,17},{2,10},{10... | collective-permute-start | bytes 245768 | tf_op jit(solution)/shard_map/ppermute | solution.py:28
  28.0 10.4 %copy-start.1 = (f32[2,1,768,128]{3,2,1,0:T(8,128)S(1)}, f32[2,1,768,128]{3,2,1,0:T(8,128)}, u32[]{:S(2)}) copy-start(f32[2,1,768,128]{3,2,1,0:T(8,128)} %rhs_ref.1) | copy-start | bytes 2359300
  28.1 3.8 %collective-permute-start.10 = (bf16[192,128]{1,0:T(8,128)(2,1)S(1)}, bf16[192,128]{1,0:T(8,128)(2,1)S(1)}, u32[]{:S(2)}, u32[]{:S(2)}) collective-permute-start(bf16[192,128]{1,0:T(8,128)(2,1)S(1)} %get-tuple-element.48), channel_id=1, source_target_pairs={{0,24},{8,16},{16,8},{24,0},{1,25},{9,17},{17,9},{25,1},{2,26},{10... | collective-permute-start | bytes 147464 | tf_op jit(solution)/shard_map/ppermute | solution.py:28
  32.9 6.5 %collective-permute-start.11 = (bf16[64,128]{1,0:T(8,128)(2,1)S(1)}, bf16[64,128]{1,0:T(8,128)(2,1)S(1)}, u32[]{:S(2)}, u32[]{:S(2)}) collective-permute-start(bf16[64,128]{1,0:T(8,128)(2,1)S(1)} %get-tuple-element.54), channel_id=1, source_target_pairs={{0,8},{8,0},{16,24},{24,16},{1,9},{9,1},{17,25},{25,17},{2,10},{10... | collective-permute-start | bytes 49160 | tf_op jit(solution)/shard_map/ppermute | solution.py:28
  33.1 6.3 %collective-permute-start.12 = (bf16[64,128]{1,0:T(8,128)(2,1)S(1)}, bf16[64,128]{1,0:T(8,128)(2,1)S(1)}, u32[]{:S(2)}, u32[]{:S(2)}) collective-permute-start(bf16[64,128]{1,0:T(8,128)(2,1)S(1)} %get-tuple-element.55), channel_id=1, source_target_pairs={{8,16},{0,24},{16,8},{24,0},{9,17},{1,25},{17,9},{25,1},{10,18},{2... | collective-permute-start | bytes 49160 | tf_op jit(solution)/shard_map/ppermute | solution.py:34
  34.6 4.8 %collective-permute-start.13 = (bf16[128,128]{1,0:T(8,128)(2,1)S(1)}, bf16[128,128]{1,0:T(8,128)(2,1)S(1)}, u32[]{:S(2)}, u32[]{:S(2)}) collective-permute-start(bf16[128,128]{1,0:T(8,128)(2,1)S(1)} %get-tuple-element.56), channel_id=1, source_target_pairs={{0,1},{1,0},{2,3},{3,2},{4,5},{5,4},{6,7},{7,6},{8,9},{9,8},{10,11... | collective-permute-start | bytes 98312 | tf_op jit(solution)/shard_map/ppermute | solution.py:28
  36.1 6.7 %collective-permute-start.14 = (bf16[128,128]{1,0:T(8,128)(2,1)S(1)}, bf16[128,128]{1,0:T(8,128)(2,1)S(1)}, u32[]{:S(2)}, u32[]{:S(2)}) collective-permute-start(bf16[128,128]{1,0:T(8,128)(2,1)S(1)} %get-tuple-element.57), channel_id=1, source_target_pairs={{1,2},{3,4},{5,6},{2,1},{4,3},{6,5},{9,10},{11,12},{13,14},{10,9},... | collective-permute-start | bytes 98312 | tf_op jit(solution)/shard_map/ppermute | solution.py:34

commit v3 on v2

--- a/solution.py
+++ b/solution.py
@@ -8,6 +8,7 @@
 
 F32 = jnp.float32
 BF16 = jnp.bfloat16
+CHUNKS = 2
 CONTRACT_FIRST = (((0,), (0,)), ((), ()))
 
 
@@ -28,10 +29,20 @@
     return lax.ppermute(value, axis, [(i, i ^ mask) for i in range(count)])
 
 
-def other(value, axis, closed=False):
-    count = lax.axis_size(axis)
-    pairs = [(i, i + 1) for i in range(1, count - 1, 2)] + [(0, count - 1)] * closed
-    return lax.ppermute(value, axis, pairs + [(j, i) for i, j in pairs])
+def other(value, axis):
+    count = {name: lax.axis_size(name) for name in ("gx", "gy")}
+    pairs = []
+    for x in range(count["gx"]):
+        for y in range(count["gy"]):
+            i = x if axis == "gx" else y
+            last = count[axis] - 1
+            j = (i - 1 if i % 2 == 0 else i + 1) % count[axis]
+            if axis == "gx":
+                target = (j, y)
+            else:
+                target = (x ^ 1, y) if i in (0, last) else (x, j)
+            pairs.append((x * count["gy"] + y, target[0] * count["gy"] + target[1]))
+    return lax.ppermute(value, ("gx", "gy"), pairs)
 
 
 def relative_block(block, device, steps):
@@ -103,6 +114,23 @@
     send_ref[:half] = total[half:].astype(BF16)
 
 
+def exchange_kernel(places, keep_ref, got_ref, other_ref, *rest):
+    holders, (next_ref, send_ref) = (got_ref, *rest[:-2]), rest[-2:]
+    rows = keep_ref.shape[0]
+    total = keep_ref[...] + got_ref[:rows].astype(F32)
+    next_ref[...] = total
+    send_ref[:rows] = total.astype(BF16)
+    end = send_ref.shape[0] - other_ref.shape[0]
+    row = lax.broadcasted_iota(jnp.int32, (end - rows, keep_ref.shape[1]), 0)
+    packed = jnp.zeros(row.shape, F32)
+    for q, (holder, start, _) in enumerate(places):
+        code = holders[holder][start : start + 16].astype(F32)
+        packed = jnp.where(row == 2 * q, code[0:1], packed)
+        packed = jnp.where(row == 2 * q + 1, code[1:2], packed)
+    send_ref[rows:end] = packed.astype(BF16)
+    send_ref[end:] = other_ref[...]
+
+
 def halve_kernel(known, keep_ref, got_ref, sent_ref, next_ref, send_ref):
     rows = keep_ref.shape[0]
     half = rows // 2
@@ -131,13 +159,13 @@
         at += ref.shape[0]
 
 
-def forward_kernel(keep_ref, got_ref, next_ref, send_ref):
+def forward_kernel(keep_ref, got_ref, pair_ref, next_ref, send_ref):
     rows = keep_ref.shape[0]
     total = keep_ref[...] + got_ref[:rows].astype(F32)
     next_ref[...] = total
     send_ref[:rows] = total.astype(BF16)
-    start = got_ref.shape[0] - (send_ref.shape[0] - rows)
-    send_ref[rows:] = got_ref[start:]
+    start = pair_ref.shape[0] - (send_ref.shape[0] - rows)
+    send_ref[rows:] = pair_ref[start:]
 
 
 def outward(width, groups, subs, send_xp, send_xo, send_yp, send_yo):
@@ -167,15 +195,21 @@
 
 def pick_kernel(places, rows_ref, token_ref, *rest):
     id_refs, out_ref = rest[:-1], rest[-1]
-    order = rows_ref.shape[1]
+    half, order = rows_ref.shape
     width = id_refs[0].shape[1]
+    if out_ref.shape[1] > half:
+        out_ref[...] = jnp.zeros(out_ref.shape, BF16)
     names = lax.broadcasted_iota(jnp.int32, (order, width), 0)
     rows = rows_ref[...]
-    for q, (holder, start) in enumerate(places):
-        code = id_refs[holder][start : start + 16].astype(F32)
+    for q, (holder, start, row) in enumerate(places):
+        code = id_refs[holder][start : start + 16].astype(F32)[row : row + 2]
         ids = (code[0:1] * 256.0 + code[1:2]).astype(jnp.int32)
         pick = (names == ids).astype(BF16)
-        out_ref[q * width : (q + 1) * width] = mm(rows, pick).T.astype(BF16)
+        out_ref[q * width : (q + 1) * width, :half] = mm(rows, pick).T.astype(BF16)
+    end = len(places) * width
+    if out_ref.shape[0] > end:
+        carried_ref = id_refs[-1]
+        out_ref[end:, : carried_ref.shape[1]] = carried_ref[...]
 
 
 def arranged(low, masks, first):
@@ -200,8 +234,9 @@
         total = total + ref[:rows].astype(F32)
     low = total.astype(BF16)
     half = next_ref.shape[0]
+    count = near_ref.shape[0]
     value = mm(near_ref[...], arranged(low, masks, 0))
-    value = value + mm(far_ref[...], arranged(low, masks, rows // 2))
+    value = value + mm(far_ref[:count, : rows // 2], arranged(low, masks, rows // 2))
     next_ref[...] = value[:half]
     send_ref[:half] = value[half:].astype(BF16)
     send_ref[half:] = halo_ref[...]
@@ -216,19 +251,21 @@
     send_ref[half:] = halo_ref[...]
 
 
-def spread_pick(rows, spill):
-    spill = jnp.concatenate([spill[d : d + 1] for d in range(4)], axis=1)
+def spread_pick(rows, spill, sides):
+    spill = jnp.concatenate([spill[d : d + 1] for d in sides], axis=1)
     iota = lax.broadcasted_iota(jnp.int32, (rows, spill.shape[1]), 0)
     return (iota == spill).astype(BF16)
 
 
-def received(subs, sub, width, groups, pair_x, other_x, pair_y, other_y, even_x, even_y):
-    west = groups(sub - 1, 1) if sub > 0 else jnp.where(even_x, other_x, pair_x)
-    east = groups(sub + 1, 0) if sub < subs - 1 else jnp.where(even_x, pair_x, other_x)
+def west_east(subs, sub, groups, pair, other, even):
+    west = groups(sub - 1, 1) if sub > 0 else jnp.where(even, other, pair)
+    east = groups(sub + 1, 0) if sub < subs - 1 else jnp.where(even, pair, other)
+    return [west, east]
+
+
+def south_north(sub, width, pair, other, even):
     rows = slice(sub * width, (sub + 1) * width)
-    south = jnp.where(even_y, other_y[rows], pair_y[rows])
-    north = jnp.where(even_y, pair_y[rows], other_y[rows])
-    return jnp.concatenate([west, east, south, north], axis=0)
+    return [jnp.where(even, other[rows], pair[rows]), jnp.where(even, pair[rows], other[rows])]
 
 
 def other_neighbour(axis):
@@ -248,41 +285,40 @@
     return even, value
 
 
-def correction_kernel(
-    count_x, width, own_ref, margin_ref, spill_ref, basis_ref, operator_ref, keep_ref, *rest
-):
-    x_refs, rest = rest[:count_x], rest[count_x:]
-    y_refs, (out_ref, low_ref, image_ref, *sends) = rest[:-7], rest[-7:]
-    subs, rows, columns = own_ref.shape
-    functions = basis_ref.shape[2]
+def local_kernel(own_ref, spill_ref, basis_ref, token_ref, far_ref, *rest):
+    y_refs, (out_ref, left_ref) = rest[:-2], rest[-2:]
+    subs, rows, _ = own_ref.shape
+    width = spill_ref.shape[3]
+    halo = subs * width
+    masks = [mirror(bit) for bit in range(1, len(y_refs))]
+    even, other = from_other("gy", (halo, y_refs[1:]), masks, 2)
+    pair = far_ref[far_ref.shape[0] - halo :, : own_ref.shape[2]]
+    for s in range(subs):
+        values = jnp.concatenate(south_north(s, width, pair, other, even), axis=0)
+        out_ref[s] = own_ref[s] + mm(spread_pick(rows, spill_ref[s, 0], (2, 3)), values)
+        left_ref[s, :, : 2 * width] = spread_pick(rows, spill_ref[s, 0], (0, 1))
+        basis = basis_ref[s, 0].astype(F32)
+        left_ref[s, :, 2 * width :] = jnp.concatenate([basis, basis], axis=0).T.astype(BF16)
+
+
+def correction_kernel(width, local_ref, left_ref, margin_ref, operator_ref, keep_ref, *rest):
+    x_refs, (out_ref, low_ref, image_ref, *sends) = rest[:-7], rest[-7:]
+    subs, rows, columns = local_ref.shape
+    functions = keep_ref.shape[0] // subs
     picked = keep_ref[...] + x_refs[-1][: keep_ref.shape[0]].astype(F32)
-    halo = subs * width
-    x_masks = [mask_of(step) for step in range(2, len(x_refs) + 1)]
-    y_masks = [mirror(bit) for bit in range(1, len(y_refs))]
-    even_x, other_x = from_other("gx", (width, x_refs[1:]), x_masks, 1)
-    even_y, other_y = from_other("gy", (halo, y_refs[1:]), y_masks, 2)
-    pair_x = x_refs[0][x_refs[0].shape[0] - width :]
-    first = y_refs[0].shape[0] - 2 * halo
-    pair_y = y_refs[0][first : first + halo]
+    masks = [mask_of(step) for step in range(2, len(x_refs) + 1)]
+    even, other = from_other("gx", (width, x_refs[1:]), masks, 1)
+    pair = x_refs[0][x_refs[0].shape[0] - width :]
 
     def margins(sub, number):
         return margin_ref[sub, number * width : (number + 1) * width]
 
     for s in range(subs):
-        values = received(
-            subs, s, width, margins, pair_x, other_x, pair_y, other_y, even_x, even_y
-        )
         part = picked[s * functions : (s + 1) * functions]
         high = part.astype(BF16)
         low = (part - high.astype(F32)).astype(BF16)
-        basis = basis_ref[s, 0]
-        coarse = lax.dot_general(
-            jnp.concatenate([basis, basis], axis=0),
-            jnp.concatenate([high, low], axis=0),
-            CONTRACT_FIRST,
-            preferred_element_type=F32,
-        )
-        value = own_ref[s] + mm(spread_pick(rows, spill_ref[s, 0]), values) + coarse
+        values = west_east(subs, s, margins, pair, other, even) + [high, low]
+        value = local_ref[s] + mm(left_ref[s], jnp.concatenate(values, axis=0))
         out_ref[s] = value
         low = value.astype(BF16)
         low_ref[s] = low
@@ -294,17 +330,26 @@
     outward(width, images, subs, *sends)
 
 
-def image_kernel(operator_ref, low_ref, rhs_ref, correction_ref, part_ref, out_ref, sems):
+def image_kernel(
+    operator_ref, low_ref, rhs_ref, correction_ref, spill_ref, part_ref, pick_ref, out_ref, sems
+):
     subs, rows, _ = low_ref.shape
     copies = copies_of([(correction_ref.at[s], out_ref.at[s, 0]) for s in range(subs)], sems)
     for s in range(subs):
         part_ref[s] = rhs_ref[s, 0] - mm(operator_ref[s, 0, :rows], low_ref[s])
+        pick_ref[s] = spread_pick(rows, spill_ref[s, 0], range(4))
     for copy in copies:
         copy.wait()
 
 
+def inner(axis, value):
+    device, count = lax.axis_index(axis), lax.axis_size(axis)
+    has = jnp.logical_and(device != 0, device != count - 1)
+    return jnp.where(has, value, jnp.zeros(value.shape, value.dtype))
+
+
 def residual_kernel(
-    width, part_ref, image_ref, spill_ref, xp_ref, xo_ref, yp_ref, yo_ref, out_ref, value_ref, sems
+    width, part_ref, image_ref, pick_ref, xp_ref, xo_ref, yp_ref, yo_ref, out_ref, value_ref, sems
 ):
     subs, rows, _ = part_ref.shape
     even_x = lax.axis_index("gx") % 2 == 0
@@ -313,18 +358,19 @@
     def margins(sub, number):
         return image_ref[sub, number * width : (number + 1) * width]
 
-    device, count = lax.axis_index("gx"), lax.axis_size("gx")
-    inner = jnp.logical_and(device != 0, device != count - 1)
-    other_x = jnp.where(inner, xo_ref[...], jnp.zeros(xo_ref.shape, BF16))
+    other_x, other_y = inner("gx", xo_ref[...]), inner("gy", yo_ref[...])
     copies = []
-    for s in range(subs):
-        values = received(
-            subs, s, width, margins, xp_ref[...], other_x, yp_ref[...], yo_ref[...],
-            even_x, even_y,
-        )
-        value_ref[s] = part_ref[s] - mm(spread_pick(rows, spill_ref[s, 0]), values)
-        copies.append(pltpu.make_async_copy(value_ref.at[s], out_ref.at[s, 0], sems.at[s]))
-        copies[s].start()
+    tile = rows // CHUNKS
+    for s in range(subs):
+        values = west_east(subs, s, margins, xp_ref[...], other_x, even_x)
+        values += south_north(s, width, yp_ref[...], other_y, even_y)
+        values = jnp.concatenate(values, axis=0)
+        for at in range(0, rows, tile):
+            part = slice(at, at + tile)
+            value_ref[s, part] = part_ref[s, part] - mm(pick_ref[s, part], values)
+            source, target = value_ref.at[s, pl.ds(at, tile)], out_ref.at[s, 0, pl.ds(at, tile)]
+            copies.append(pltpu.make_async_copy(source, target, sems.at[len(copies)]))
+            copies[-1].start()
     for copy in copies:
         copy.wait()
 
@@ -398,6 +444,16 @@
         size = half
     id_places = id_places + [(got, size + 16 * i, 0) for i in range(len(id_places))]
 
+    holders, places = [got], []
+    for q in range(count_x):
+        p = sum(((q >> (steps_x - k)) & 1) << (k - 1) for k in range(1, steps_x + 1))
+        array, start, _ = id_places[p]
+        found = [i for i, holder in enumerate(holders) if holder is array]
+        if not found:
+            holders.append(array)
+            found = [len(holders) - 1]
+        places.append((found[0], start, 0))
+
     own, margins, halo_xp, halo_xo, halo_yp, halo_yo = call(
         functools.partial(solve_kernel, margin),
         [(block, F32), ((subs, 4 * margin, width), BF16)] + messages,
@@ -413,20 +469,36 @@
             join_kernel, [(shape, BF16)], [near, far, token], "inverse_join", ins=[VMEM, VMEM, ANY]
         )[0]
 
+    def picked(value, token, places, holders, *carried):
+        rows = count_x * listed
+        wide = rows + halo * len(carried)
+        return call(
+            functools.partial(pick_kernel, places),
+            [((wide, max(value.shape[0], width * len(carried))), BF16)],
+            [value, token, *holders, *carried],
+            "inverse_pick",
+            ins=[VMEM, ANY] + [VMEM] * (len(holders) + len(carried)),
+            limit=8,
+        )[0]
+
     near = join(near, far, own)
     far = swap(near, "gy", gather_masks[1])
 
+    packed = -(-2 * count_x // 16) * 16
     keep, send = call(
-        sum_kernel,
-        [((size, width), F32), ((size + 2 * halo, width), BF16)],
-        [keep, got, halo_yp, halo_yo],
+        functools.partial(exchange_kernel, places),
+        [((size, width), F32), ((size + packed + halo, width), BF16)],
+        [keep, got, halo_yo, *holders[1:]],
         "coarse_sum",
     )
     got = swap(send, "gy", mask_of(1))
     y_got = [got]
-    for mask in gather_masks[2:]:
+    for mask in gather_masks[2:-1]:
         near = join(near, far, got)
         far = swap(near, "gy", mask)
+    near = join(near, far, got)
+    partner = [(0, size + 2 * q // 16 * 16, 2 * q % 16) for q in range(count_x)]
+    far = swap(picked(near, got, partner, [got], halo_yp), "gy", gather_masks[-1])
     pending = [got]
     bit = 1
     while bit < steps_y:
@@ -435,36 +507,15 @@
         keep, send = call(
             forward_kernel,
             [((size, width), F32), ((size + halo, width), BF16)],
-            [keep, pending[0]],
+            [keep, pending[0], y_got[-1]],
             "coarse_sum",
         )
-        masks = [mirror(bit)] + [mirror(bit + 1)] * (bit + 1 < steps_y)
+        masks = [1 << bit]
         pending = [swap(send, "gy", mask) for mask in masks]
         y_got += pending
-        if len(masks) > 1:
-            pending.append(swap(send[:size], "gy", masks[0] ^ masks[1]))
-        bit += 2
-
-    holders, places = [], []
-    for q in range(count_x):
-        p = sum(((q >> (steps_x - k)) & 1) << (k - 1) for k in range(1, steps_x + 1))
-        array, start, _ = id_places[p]
-        found = [i for i, holder in enumerate(holders) if holder is array]
-        if not found:
-            holders.append(array)
-            found = [len(holders) - 1]
-        places.append((found[0], start))
-    def picked(value, token):
-        return call(
-            functools.partial(pick_kernel, places),
-            [((count_x * listed, value.shape[0]), BF16)],
-            [value, token, *holders],
-            "inverse_pick",
-            ins=[VMEM, ANY] + [VMEM] * len(holders),
-            limit=8,
-        )[0]
-
-    near, far = picked(near, send), picked(far, send)
+        bit += 1
+
+    near = picked(near, send, places, holders)
 
     half = count_x * listed // 2
     keep, send = call(
@@ -484,35 +535,42 @@
         )
         x_got.append(swap(send, "gx", mask_of(step)))
 
+    local, left = call(
+        local_kernel,
+        [(block, F32), ((subs, rows, 2 * margin + 2 * functions), BF16)],
+        [own, spill_rows, coarse_basis, send, far, *y_got],
+        "local_spread",
+        ins=[VMEM] * 3 + [ANY] + [VMEM] * (1 + len(y_got)),
+        limit=8,
+    )
     correction, low, image, *sends = call(
-        functools.partial(correction_kernel, len(x_got), margin),
+        functools.partial(correction_kernel, margin),
         [(block, F32), (block, BF16), ((subs, 4 * margin, width), BF16)] + messages,
-        [own, margins, spill_rows, coarse_basis, local_operator, keep, *x_got, *y_got],
+        [local, left, margins, local_operator, keep, *x_got],
         "correction",
         limit=12,
     )
-
     got_yo = other(sends[3], "gy")
-    got_xo = other(sends[1], "gx", closed=True)
+    got_xo = other(sends[1], "gx")
     got_yp = swap(sends[2], "gy", 1)
     got_xp = swap(sends[0], "gx", 1)
 
-    part, correction = call(
+    part, pick, correction = call(
         image_kernel,
-        [(block, F32), (adjoint_rhs.shape, F32)],
-        [local_operator, low, adjoint_rhs, correction],
+        [(block, F32), ((subs, rows, 4 * margin), BF16), (adjoint_rhs.shape, F32)],
+        [local_operator, low, adjoint_rhs, correction, spill_rows],
         "image_own",
-        out_specs=[VMEM, HBM],
+        out_specs=[VMEM, VMEM, HBM],
         scratch=[dma((subs,))],
         limit=12,
     )
     (residual,) = call(
         functools.partial(residual_kernel, margin),
         [(adjoint_rhs.shape, F32)],
-        [part, image, spill_rows, got_xp, got_xo, got_yp, got_yo],
+        [part, image, pick, got_xp, got_xo, got_yp, got_yo],
         "residual",
         out_specs=[HBM],
-        scratch=[pltpu.VMEM(block, F32), dma((subs,))],
+        scratch=[pltpu.VMEM(block, F32), dma((CHUNKS * subs,))],
     )
     return correction, residual
 

time: 44.2 us -> 41 us (0.928)
  the two profiles are of different devices: /device:TPU:2 before, /device:TPU:8 now
where the time goes in v3:
time: 41 us; the launch traced here: 40.9 us
  waiting for transfers between devices  17.9 us (44%)
  starting transfers between devices  13.9 us (34%)
  Pallas kernels  8.28 us (20%)
  between operations  0.78 us (2%)
    ppermute x12, waiting for transfers between devices, swap(): return lax.ppermute(value, axis, [(i, i ^ mask) for i in range(count)])  15.5 us
    ppermute x12, starting transfers between devices, swap(): return lax.ppermute(value, axis, [(i, i ^ mask) for i in range(count)])  12 us
    pallas_call x16, Pallas kernels, call(): pl.pallas_call(kernel, out_shape=[jax.ShapeDtypeStruct(shape, dtype) for...  8.28 us
    ppermute x2, waiting for transfers between devices, other(): return lax.ppermute(value, ('gx', 'gy'), pairs)  2.39 us
    ppermute x2, starting transfers between devices, other(): return lax.ppermute(value, ('gx', 'gy'), pairs)  1.86 us
  transfers between devices with their start and end apart: 14, of which 10 were waited for; matrix products, arithmetic and copies ran while one was open for 0% of the time, Pallas kernels for 9%

profile of v3, /device:TPU:8, one launch (start us, length us, event | category | flops | bytes accessed | tf_op | source)
XLA Modules:
  0.0 40.9 jit_solution(9067106778806050441)
XLA Ops:
  0.7 2.0 %coarse_terms.1 = (f32[512,128]{1,0:T(8,128)S(1)}, bf16[528,128]{1,0:T(8,128)(2,1)S(1)}, bf16[2,768,128]{2,1,0:T(8,128)(2,1)S(1)}) custom-call(f32[2,1,768,128]{3,2,1,0:T(8,128)} %rhs_ref.1, bf16[2,1,64,768]{3,2,1,0:T(8,128)(2,1)} %basis_ref.1, s32[2,1,64]{2,1,0:T(1,128)} %ids_hbm.1), custom_call_target="tpu_custom_call" | custom-call | flops 1000000000 | bytes 1048576 | tf_op jit(solution)/shard_map/coarse_terms/pallas_call | solution.py:385
  2.7 0.1 collective-permute-start
  2.8 2.7 %collective-permute-start.1 = (bf16[32,1024]{1,0:T(8,128)(2,1)S(1)}, bf16[32,1024]{1,0:T(8,128)(2,1)S(1)}, u32[]{:S(2)}, u32[]{:S(2)}) collective-permute-start(bf16[32,1024]{1,0:T(8,128)(2,1)S(1)} %copy-done.5), channel_id=1, source_target_pairs={{0,4},{1,5},{2,6},{3,7},{4,0},{5,1},{6,2},{7,3},{8,12},{9,13},{10,... | collective-permute-start | bytes 196616 | tf_op jit(solution)/shard_map/ppermute | solution.py:29
  5.5 1.3 %collective-permute-start.3 = (bf16[288,128]{1,0:T(8,128)(2,1)S(1)}, bf16[288,128]{1,0:T(8,128)(2,1)S(1)}, u32[]{:S(2)}, u32[]{:S(2)}) collective-permute-start(bf16[288,128]{1,0:T(8,128)(2,1)S(1)} %get-tuple-element.38.token_ref), channel_id=1, source_target_pairs={{0,24},{8,16},{16,8},{24,0},{1,25},{9,17},{17,9},{25,1},{2,26},{10... | collective-permute-start | bytes 221192 | tf_op jit(solution)/shard_map/ppermute | solution.py:29
  6.8 1.0 %local_solve.1 = (f32[2,768,128]{2,1,0:T(8,128)S(1)}, bf16[2,256,128]{2,1,0:T(8,128)(2,1)S(1)}, bf16[64,128]{1,0:T(8,128)(2,1)S(1)}, bf16[64,128]{1,0:T(8,128)(2...) custom-call(bf16[2,1,1024,768]{3,2,1,0:T(8,128)(2,1)S(1)} %copy-done.3, ...), custom_call_target="tpu_custom_call" | custom-call | flops 1000000000 | bytes 1048576 | tf_op jit(solution)/shard_map/local_solve/pallas_call | solution.py:385
  7.8 1.9 %collective-permute-done.3.got_ref.rest_0_ = bf16[288,128]{1,0:T(8,128)(2,1)S(1)} collective-permute-done((bf16[288,128]{1,0:T(8,128)(2,1)S(1)}, bf16[288,128]{1,0:T(8,128)(2,1)S(1)}, u32[]{:S(2)}, u32[]{:S(2)}) %collective-permute-start.3) | collective-permute-done | bytes 73760 | tf_op jit(solution)/shard_map/ppermute | solution.py:29
  9.8 1.5 %collective-permute-start.4 = (bf16[400,128]{1,0:T(8,128)(2,1)S(1)}, bf16[400,128]{1,0:T(8,128)(2,1)S(1)}, u32[]{:S(2)}, u32[]{:S(2)}) collective-permute-start(bf16[400,128]{1,0:T(8,128)(2,1)S(1)} %get-tuple-element.42), channel_id=1, source_target_pairs={{0,1},{1,0},{2,3},{3,2},{4,5},{5,4},{6,7},{7,6},{8,9},{9,8},{10,11... | collective-permute-start | bytes 307208 | tf_op jit(solution)/shard_map/ppermute | solution.py:29
  11.3 0.5 %collective-permute-start.2 = (bf16[64,1024]{1,0:T(8,128)(2,1)S(1)}, bf16[64,1024]{1,0:T(8,128)(2,1)S(1)}, u32[]{:S(2)}, u32[]{:S(2)}) collective-permute-start(bf16[64,1024]{1,0:T(8,128)(2,1)S(1)} %inverse_join.2.near_ref), channel_id=1, source_target_pairs={{0,2},{1,3},{2,0},{3,1},{4,6},{5,7},{6,4},{7,5},{8,10},{9,11},{10,... | collective-permute-start | bytes 393224 | tf_op jit(solution)/shard_map/ppermute | solution.py:29
  11.9 2.9 %collective-permute-done.4.token_ref.got_ref.pair_ref.rest_0_ = bf16[400,128]{1,0:T(8,128)(2,1)S(1)} collective-permute-done((bf16[400,128]{1,0:T(8,128)(2,1)S(1)}, bf16[400,128]{1,0:T(8,128)(2,1)S(1)}, u32[]{:S(2)}, u32[]{:S(2)}) %collective-permute-start.4) | collective-permute-done | bytes 102432 | tf_op jit(solution)/shard_map/ppermute | solution.py:29
  14.8 0.5 %collective-permute-start.5 = (bf16[384,128]{1,0:T(8,128)(2,1)S(1)}, bf16[384,128]{1,0:T(8,128)(2,1)S(1)}, u32[]{:S(2)}, u32[]{:S(2)}) collective-permute-start(bf16[384,128]{1,0:T(8,128)(2,1)S(1)} %get-tuple-element.45), channel_id=1, source_target_pairs={{0,2},{1,3},{2,0},{3,1},{4,6},{5,7},{6,4},{7,5},{8,10},{9,11},{10,... | collective-permute-start | bytes 294920 | tf_op jit(solution)/shard_map/ppermute | solution.py:29
  15.3 1.4 %collective-permute-done.2.far_ref = bf16[64,1024]{1,0:T(8,128)(2,1)S(1)} collective-permute-done((bf16[64,1024]{1,0:T(8,128)(2,1)S(1)}, bf16[64,1024]{1,0:T(8,128)(2,1)S(1)}, u32[]{:S(2)}, u32[]{:S(2)}) %collective-permute-start.2) | collective-permute-done | bytes 131104 | tf_op jit(solution)/shard_map/ppermute | solution.py:29
  16.7 0.5 %inverse_pick.3 = bf16[640,128]{1,0:T(8,128)(2,1)S(1)} custom-call(bf16[128,1024]{1,0:T(8,128)(2,1)S(1)} %inverse_join.3.rows_ref, bf16[400,128]{1,0:T(8,128)(2,1)S(1)} %collective-permute-done.4.token_ref.got_ref.pair_ref.rest_0_, bf16[400,128]{1,0:T(8,128)(2,1)S(1)} %collective-permute-done.4.token_ref.got_ref.pair_ref.rest_0_, ...), custom_call_target="tpu_custom_call" | custom-call | flops 1000000000 | bytes 1048576 | tf_op jit(solution)/shard_map/inverse_pick/pallas_call | solution.py:385
  17.2 0.6 %collective-permute-start.6 = (bf16[640,128]{1,0:T(8,128)(2,1)S(1)}, bf16[640,128]{1,0:T(8,128)(2,1)S(1)}, u32[]{:S(2)}, u32[]{:S(2)}) collective-permute-start(bf16[640,128]{1,0:T(8,128)(2,1)S(1)} %inverse_pick.3), channel_id=1, source_target_pairs={{0,1},{1,0},{2,3},{3,2},{4,5},{5,4},{6,7},{7,6},{8,9},{9,8},{10,11... | collective-permute-start | bytes 491528 | tf_op jit(solution)/shard_map/ppermute | solution.py:29
  17.8 1.7 %collective-permute-done.5.got_ref.pair_ref.rest_1_ = bf16[384,128]{1,0:T(8,128)(2,1)S(1)} collective-permute-done((bf16[384,128]{1,0:T(8,128)(2,1)S(1)}, bf16[384,128]{1,0:T(8,128)(2,1)S(1)}, u32[]{:S(2)}, u32[]{:S(2)}) %collective-permute-start.5) | collective-permute-done | bytes 98336 | tf_op jit(solution)/shard_map/ppermute | solution.py:29
  19.5 1.6 %collective-permute-start.7 = (bf16[384,128]{1,0:T(8,128)(2,1)S(1)}, bf16[384,128]{1,0:T(8,128)(2,1)S(1)}, u32[]{:S(2)}, u32[]{:S(2)}) collective-permute-start(bf16[384,128]{1,0:T(8,128)(2,1)S(1)} %get-tuple-element.46.token_ref), channel_id=1, source_target_pairs={{0,4},{1,5},{2,6},{3,7},{4,0},{5,1},{6,2},{7,3},{8,12},{9,13},{10,... | collective-permute-start | bytes 294920 | tf_op jit(solution)/shard_map/ppermute | solution.py:29
  21.1 0.5 %inverse_pick.2.near_ref = bf16[512,128]{1,0:T(8,128)(2,1)S(1)} custom-call(bf16[128,1024]{1,0:T(8,128)(2,1)S(1)} %inverse_join.3.rows_ref, bf16[384,128]{1,0:T(8,128)(2,1)S(1)} %get-tuple-element.46.token_ref, bf16[288,128]{1,0:T(8,128)(2,1)S(1)} %collective-permute-done.3.got_ref.rest_0_, bf16[528,128]{1,0:T(8,128)(2,1)S(1)} %get-tuple-element.37.sent_ref.rest_0_.rest_1_, ...), custom_call_target="tpu_custom_call" | custom-call | flops 1000000000 | bytes 1048576 | tf_op jit(solution)/shard_map/inverse_pick/pallas_call | solution.py:385
  21.7 0.9 %collective-permute-done.6.far_ref = bf16[640,128]{1,0:T(8,128)(2,1)S(1)} collective-permute-done((bf16[640,128]{1,0:T(8,128)(2,1)S(1)}, bf16[640,128]{1,0:T(8,128)(2,1)S(1)}, u32[]{:S(2)}, u32[]{:S(2)}) %collective-permute-start.6) | collective-permute-done | bytes 163872 | tf_op jit(solution)/shard_map/ppermute | solution.py:29
  22.6 2.5 %collective-permute-done.7.rest_0_.rest_2_ = bf16[384,128]{1,0:T(8,128)(2,1)S(1)} collective-permute-done((bf16[384,128]{1,0:T(8,128)(2,1)S(1)}, bf16[384,128]{1,0:T(8,128)(2,1)S(1)}, u32[]{:S(2)}, u32[]{:S(2)}) %collective-permute-start.7) | collective-permute-done | bytes 98336 | tf_op jit(solution)/shard_map/ppermute | solution.py:29
  25.1 0.4 %coarse_solve.1 = (f32[256,128]{1,0:T(8,128)S(1)}, bf16[320,128]{1,0:T(8,128)(2,1)S(1)}) custom-call(bf16[512,128]{1,0:T(8,128)(2,1)S(1)} %inverse_pick.2.near_ref, bf16[640,128]{1,0:T(8,128)(2,1)S(1)} %collective-permute-done.6.far_ref, f32[256,128]{1,0:T(8,128)S(1)} %get-tuple-element.48.keep_ref, bf16[64,128]{1,0:T(8,128)(2,1)S(1)} %get-tuple-element.49.halo_ref, ...), custom_call_target="tpu_custom_call" | custom-call | flops 1000000000 | bytes 1048576 | tf_op jit(solution)/shard_map/coarse_solve/pallas_call | solution.py:385
  25.6 1.3 %collective-permute-done.8.got_ref.rest_0_ = bf16[320,128]{1,0:T(8,128)(2,1)S(1)} collective-permute-done((bf16[320,128]{1,0:T(8,128)(2,1)S(1)}, bf16[320,128]{1,0:T(8,128)(2,1)S(1)}, u32[]{:S(2)}, u32[]{:S(2)}) %collective-permute-start.8) | collective-permute-done | bytes 81952 | tf_op jit(solution)/shard_map/ppermute | solution.py:29
  26.9 1.3 %collective-permute-start.9 = (bf16[192,128]{1,0:T(8,128)(2,1)S(1)}, bf16[192,128]{1,0:T(8,128)(2,1)S(1)}, u32[]{:S(2)}, u32[]{:S(2)}) collective-permute-start(bf16[192,128]{1,0:T(8,128)(2,1)S(1)} %get-tuple-element.53.token_ref), channel_id=1, source_target_pairs={{0,24},{8,16},{16,8},{24,0},{1,25},{9,17},{17,9},{25,1},{2,26},{10... | collective-permute-start | bytes 147464 | tf_op jit(solution)/shard_map/ppermute | solution.py:29
  28.3 0.4 %local_spread.1 = (f32[2,768,128]{2,1,0:T(8,128)S(1)}, bf16[2,768,256]{2,1,0:T(8,128)(2,1)S(1)}) custom-call(f32[2,768,128]{2,1,0:T(8,128)S(1)} %get-tuple-element.39.token_ref.own_ref, s32[2,1,4,64]{3,2,1,0:T(4,128)S(1)} %copy-done.2, bf16[2,1,64,768]{3,2,1,0:T(8,128)(2,1)S(1)} %copy-done.4, bf16[192,128]{1,0:T(8,128)(2,1)S(1)} %get-tuple-element.53.token_ref, ...), custom_call_target="tpu_custom_call" | custom-call | flops 1000000000 | bytes 1048576 | tf_op jit(solution)/shard_map/local_spread/pallas_call | solution.py:385
  28.8 1.9 %collective-permute-done.9.rest_1_ = bf16[192,128]{1,0:T(8,128)(2,1)S(1)} collective-permute-done((bf16[192,128]{1,0:T(8,128)(2,1)S(1)}, bf16[192,128]{1,0:T(8,128)(2,1)S(1)}, u32[]{:S(2)}, u32[]{:S(2)}) %collective-permute-start.9) | collective-permute-done | bytes 49184 | tf_op jit(solution)/shard_map/ppermute | solution.py:29
  30.7 1.0 %correction.1 = (f32[2,768,128]{2,1,0:T(8,128)S(1)}, bf16[2,768,128]{2,1,0:T(8,128)(2,1)S(1)}, bf16[2,256,128]{2,1,0:T(8,128)(2,1)S(1)}, bf16[64,128]{1,0:T(8,12...) custom-call(f32[2,768,128]{2,1,0:T(8,128)S(1)} %get-tuple-element.54.local_ref,, ...), custom_call_target="tpu_custom_call" | custom-call | flops 1000000000 | bytes 1048576 | tf_op jit(solution)/shard_map/correction/pallas_call | solution.py:385
  31.7 0.2 collective-permute-start.10
  31.9 1.5 %collective-permute-start.11 = (bf16[64,128]{1,0:T(8,128)(2,1)S(1)}, bf16[64,128]{1,0:T(8,128)(2,1)S(1)}, u32[]{:S(2)}, u32[]{:S(2)}) collective-permute-start(bf16[64,128]{1,0:T(8,128)(2,1)S(1)} %get-tuple-element.65), channel_id=1, source_target_pairs={{0,24},{1,25},{2,26},{3,27},{4,28},{5,29},{6,30},{7,31},{8,16},{9,... | collective-permute-start | bytes 49160 | tf_op jit(solution)/shard_map/ppermute | solution.py:45
  33.4 1.5 %collective-permute-start.12 = (bf16[128,128]{1,0:T(8,128)(2,1)S(1)}, bf16[128,128]{1,0:T(8,128)(2,1)S(1)}, u32[]{:S(2)}, u32[]{:S(2)}) collective-permute-start(bf16[128,128]{1,0:T(8,128)(2,1)S(1)} %get-tuple-element.66), channel_id=1, source_target_pairs={{0,1},{1,0},{2,3},{3,2},{4,5},{5,4},{6,7},{7,6},{8,9},{9,8},{10,11... | collective-permute-start | bytes 98312 | tf_op jit(solution)/shard_map/ppermute | solution.py:29
  34.9 0.4 collective-permute-start.13
  35.3 1.1 %image_own.1 = (f32[2,768,128]{2,1,0:T(8,128)S(1)}, bf16[2,768,256]{2,1,0:T(8,128)(2,1)S(1)}, f32[2,1,768,128]{3,2,1,0:T(8,128)}) custom-call(bf16[2,1,1024,768]{3,2,1,0:T(8,128)(2,1)S(1)} %copy-done, bf16[2,768,128]{2,1,0:T(8,128)(2,1)S(1)} %get-tuple-element.58.low_ref, f32[2,1,768,128]{3,2,1,0:T(8,128)S(1)} %copy-done.1, ...), custom_call_target="tpu_custom_call" | custom-call | flops 1000000000 | bytes 1048576 | tf_op jit(solution)/shard_map/image_own/pallas_call | solution.py:385
  36.4 0.9 %collective-permute-done.12.yp_ref = bf16[128,128]{1,0:T(8,128)(2,1)S(1)} collective-permute-done((bf16[128,128]{1,0:T(8,128)(2,1)S(1)}, bf16[128,128]{1,0:T(8,128)(2,1)S(1)}, u32[]{:S(2)}, u32[]{:S(2)}) %collective-permute-start.12) | collective-permute-done | bytes 32800 | tf_op jit(solution)/shard_map/ppermute | solution.py:29
  37.3 2.4 %collective-permute-done.13.yo_ref = bf16[128,128]{1,0:T(8,128)(2,1)S(1)} collective-permute-done((bf16[128,128]{1,0:T(8,128)(2,1)S(1)}, bf16[128,128]{1,0:T(8,128)(2,1)S(1)}, u32[]{:S(2)}, u32[]{:S(2)}) %collective-permute-start.13) | collective-permute-done | bytes 32800 | tf_op jit(solution)/shard_map/ppermute | solution.py:45
  39.7 1.2 %residual.1 = f32[2,1,768,128]{3,2,1,0:T(8,128)} custom-call(f32[2,768,128]{2,1,0:T(8,128)S(1)} %get-tuple-element.61.part_ref, bf16[2,256,128]{2,1,0:T(8,128)(2,1)S(1)} %get-tuple-element.62.image_ref, bf16[2,768,256]{2,1,0:T(8,128)(2,1)S(1)} %get-tuple-element.63.pick_ref, bf16[64,128]{1,0:T(8,128)(2,1)S(1)} %collective-permute-done.10.xp_ref, ...), custom_call_target="tpu_custom_call" | custom-call | flops 1000000000 | bytes 1048576 | tf_op jit(solution)/shard_map/residual/pallas_call | solution.py:385
  (24 shorter events, 0.3 us)
Async XLA Ops:
  0.6 2.1 %copy-start.5 = (bf16[32,1024]{1,0:T(8,128)(2,1)S(1)}, bf16[32,1024]{1,0:T(8,128)(2,1)}, u32[]{:S(2)}) copy-start(bf16[32,1024]{1,0:T(8,128)(2,1)} %near_ref.1) | copy-start | bytes 196612
  0.6 6.2 %copy-start.3 = (bf16[2,1,1024,768]{3,2,1,0:T(8,128)(2,1)S(1)}, bf16[2,1,1024,768]{3,2,1,0:T(8,128)(2,1)}, u32[]{:S(2)}) copy-start(bf16[2,1,1024,768]{3,2,1,0:T(8,128)(2,1)} %inverse_ref.1) | copy-start | bytes 9437188
  2.7 2.8 %collective-permute-start = (bf16[528,128]{1,0:T(8,128)(2,1)S(1)}, bf16[528,128]{1,0:T(8,128)(2,1)S(1)}, u32[]{:S(2)}, u32[]{:S(2)}) collective-permute-start(bf16[528,128]{1,0:T(8,128)(2,1)S(1)} %get-tuple-element.37.sent_ref.rest_0_.rest_1_), channel_id=1, source_target_pairs={{0,8},{8,0},{16,24},{24,16},{1,9},{9,1},{17,25},{25,17},{2,10},{10... | collective-permute-start | bytes 405512 | tf_op jit(solution)/shard_map/ppermute | solution.py:29
  2.8 8.6 %collective-permute-start.1 = (bf16[32,1024]{1,0:T(8,128)(2,1)S(1)}, bf16[32,1024]{1,0:T(8,128)(2,1)S(1)}, u32[]{:S(2)}, u32[]{:S(2)}) collective-permute-start(bf16[32,1024]{1,0:T(8,128)(2,1)S(1)} %copy-done.5), channel_id=1, source_target_pairs={{0,4},{1,5},{2,6},{3,7},{4,0},{5,1},{6,2},{7,3},{8,12},{9,13},{10,... | collective-permute-start | bytes 196616 | tf_op jit(solution)/shard_map/ppermute | solution.py:29
  5.5 4.3 %collective-permute-start.3 = (bf16[288,128]{1,0:T(8,128)(2,1)S(1)}, bf16[288,128]{1,0:T(8,128)(2,1)S(1)}, u32[]{:S(2)}, u32[]{:S(2)}) collective-permute-start(bf16[288,128]{1,0:T(8,128)(2,1)S(1)} %get-tuple-element.38.token_ref), channel_id=1, source_target_pairs={{0,24},{8,16},{16,8},{24,0},{1,25},{9,17},{17,9},{25,1},{2,26},{10... | collective-permute-start | bytes 221192 | tf_op jit(solution)/shard_map/ppermute | solution.py:29
  9.8 5.0 %collective-permute-start.4 = (bf16[400,128]{1,0:T(8,128)(2,1)S(1)}, bf16[400,128]{1,0:T(8,128)(2,1)S(1)}, u32[]{:S(2)}, u32[]{:S(2)}) collective-permute-start(bf16[400,128]{1,0:T(8,128)(2,1)S(1)} %get-tuple-element.42), channel_id=1, source_target_pairs={{0,1},{1,0},{2,3},{3,2},{4,5},{5,4},{6,7},{7,6},{8,9},{9,8},{10,11... | collective-permute-start | bytes 307208 | tf_op jit(solution)/shard_map/ppermute | solution.py:29
  11.3 5.3 %collective-permute-start.2 = (bf16[64,1024]{1,0:T(8,128)(2,1)S(1)}, bf16[64,1024]{1,0:T(8,128)(2,1)S(1)}, u32[]{:S(2)}, u32[]{:S(2)}) collective-permute-start(bf16[64,1024]{1,0:T(8,128)(2,1)S(1)} %inverse_join.2.near_ref), channel_id=1, source_target_pairs={{0,2},{1,3},{2,0},{3,1},{4,6},{5,7},{6,4},{7,5},{8,10},{9,11},{10,... | collective-permute-start | bytes 393224 | tf_op jit(solution)/shard_map/ppermute | solution.py:29
  14.8 4.7 %collective-permute-start.5 = (bf16[384,128]{1,0:T(8,128)(2,1)S(1)}, bf16[384,128]{1,0:T(8,128)(2,1)S(1)}, u32[]{:S(2)}, u32[]{:S(2)}) collective-permute-start(bf16[384,128]{1,0:T(8,128)(2,1)S(1)} %get-tuple-element.45), channel_id=1, source_target_pairs={{0,2},{1,3},{2,0},{3,1},{4,6},{5,7},{6,4},{7,5},{8,10},{9,11},{10,... | collective-permute-start | bytes 294920 | tf_op jit(solution)/shard_map/ppermute | solution.py:29
  17.2 5.4 %collective-permute-start.6 = (bf16[640,128]{1,0:T(8,128)(2,1)S(1)}, bf16[640,128]{1,0:T(8,128)(2,1)S(1)}, u32[]{:S(2)}, u32[]{:S(2)}) collective-permute-start(bf16[640,128]{1,0:T(8,128)(2,1)S(1)} %inverse_pick.3), channel_id=1, source_target_pairs={{0,1},{1,0},{2,3},{3,2},{4,5},{5,4},{6,7},{7,6},{8,9},{9,8},{10,11... | collective-permute-start | bytes 491528 | tf_op jit(solution)/shard_map/ppermute | solution.py:29
  19.5 5.6 %collective-permute-start.7 = (bf16[384,128]{1,0:T(8,128)(2,1)S(1)}, bf16[384,128]{1,0:T(8,128)(2,1)S(1)}, u32[]{:S(2)}, u32[]{:S(2)}) collective-permute-start(bf16[384,128]{1,0:T(8,128)(2,1)S(1)} %get-tuple-element.46.token_ref), channel_id=1, source_target_pairs={{0,4},{1,5},{2,6},{3,7},{4,0},{5,1},{6,2},{7,3},{8,12},{9,13},{10,... | collective-permute-start | bytes 294920 | tf_op jit(solution)/shard_map/ppermute | solution.py:29
  25.1 3.1 %copy-start.2 = (s32[2,1,4,64]{3,2,1,0:T(4,128)S(1)}, s32[2,1,4,64]{3,2,1,0:T(4,128)}, u32[]{:S(2)}) copy-start(s32[2,1,4,64]{3,2,1,0:T(4,128)} %spill_ref.3) | copy-start | bytes 6148
  25.1 3.1 %copy-start.4 = (bf16[2,1,64,768]{3,2,1,0:T(8,128)(2,1)S(1)}, bf16[2,1,64,768]{3,2,1,0:T(8,128)(2,1)}, u32[]{:S(2)}) copy-start(bf16[2,1,64,768]{3,2,1,0:T(8,128)(2,1)} %basis_ref.1) | copy-start | bytes 589828
  25.6 1.3 %collective-permute-start.8 = (bf16[320,128]{1,0:T(8,128)(2,1)S(1)}, bf16[320,128]{1,0:T(8,128)(2,1)S(1)}, u32[]{:S(2)}, u32[]{:S(2)}) collective-permute-start(bf16[320,128]{1,0:T(8,128)(2,1)S(1)} %get-tuple-element.51), channel_id=1, source_target_pairs={{0,8},{8,0},{16,24},{24,16},{1,9},{9,1},{17,25},{25,17},{2,10},{10... | collective-permute-start | bytes 245768 | tf_op jit(solution)/shard_map/ppermute | solution.py:29
  26.9 3.8 %copy-start = (bf16[2,1,1024,768]{3,2,1,0:T(8,128)(2,1)S(1)}, bf16[2,1,1024,768]{3,2,1,0:T(8,128)(2,1)}, u32[]{:S(2)}) copy-start(bf16[2,1,1024,768]{3,2,1,0:T(8,128)(2,1)} %operator_ref.3) | copy-start | bytes 9437188
  26.9 3.8 %collective-permute-start.9 = (bf16[192,128]{1,0:T(8,128)(2,1)S(1)}, bf16[192,128]{1,0:T(8,128)(2,1)S(1)}, u32[]{:S(2)}, u32[]{:S(2)}) collective-permute-start(bf16[192,128]{1,0:T(8,128)(2,1)S(1)} %get-tuple-element.53.token_ref), channel_id=1, source_target_pairs={{0,24},{8,16},{16,8},{24,0},{1,25},{9,17},{17,9},{25,1},{2,26},{10... | collective-permute-start | bytes 147464 | tf_op jit(solution)/shard_map/ppermute | solution.py:29
  28.7 6.5 %copy-start.1 = (f32[2,1,768,128]{3,2,1,0:T(8,128)S(1)}, f32[2,1,768,128]{3,2,1,0:T(8,128)}, u32[]{:S(2)}) copy-start(f32[2,1,768,128]{3,2,1,0:T(8,128)} %rhs_ref.1) | copy-start | bytes 2359300
  31.7 4.7 %collective-permute-start.10 = (bf16[64,128]{1,0:T(8,128)(2,1)S(1)}, bf16[64,128]{1,0:T(8,128)(2,1)S(1)}, u32[]{:S(2)}, u32[]{:S(2)}) collective-permute-start(bf16[64,128]{1,0:T(8,128)(2,1)S(1)} %get-tuple-element.64), channel_id=1, source_target_pairs={{0,8},{8,0},{16,24},{24,16},{1,9},{9,1},{17,25},{25,17},{2,10},{10... | collective-permute-start | bytes 49160 | tf_op jit(solution)/shard_map/ppermute | solution.py:29
  31.9 4.5 %collective-permute-start.11 = (bf16[64,128]{1,0:T(8,128)(2,1)S(1)}, bf16[64,128]{1,0:T(8,128)(2,1)S(1)}, u32[]{:S(2)}, u32[]{:S(2)}) collective-permute-start(bf16[64,128]{1,0:T(8,128)(2,1)S(1)} %get-tuple-element.65), channel_id=1, source_target_pairs={{0,24},{1,25},{2,26},{3,27},{4,28},{5,29},{6,30},{7,31},{8,16},{9,... | collective-permute-start | bytes 49160 | tf_op jit(solution)/shard_map/ppermute | solution.py:45
  33.4 3.9 %collective-permute-start.12 = (bf16[128,128]{1,0:T(8,128)(2,1)S(1)}, bf16[128,128]{1,0:T(8,128)(2,1)S(1)}, u32[]{:S(2)}, u32[]{:S(2)}) collective-permute-start(bf16[128,128]{1,0:T(8,128)(2,1)S(1)} %get-tuple-element.66), channel_id=1, source_target_pairs={{0,1},{1,0},{2,3},{3,2},{4,5},{5,4},{6,7},{7,6},{8,9},{9,8},{10,11... | collective-permute-start | bytes 98312 | tf_op jit(solution)/shard_map/ppermute | solution.py:29
  34.9 4.8 %collective-permute-start.13 = (bf16[128,128]{1,0:T(8,128)(2,1)S(1)}, bf16[128,128]{1,0:T(8,128)(2,1)S(1)}, u32[]{:S(2)}, u32[]{:S(2)}) collective-permute-start(bf16[128,128]{1,0:T(8,128)(2,1)S(1)} %get-tuple-element.67), channel_id=1, source_target_pairs={{0,8},{1,2},{2,1},{3,4},{4,3},{5,6},{6,5},{7,15},{8,0},{9,10},{10,... | collective-permute-start | bytes 98312 | tf_op jit(solution)/shard_map/ppermute | solution.py:45

commit v4 on v3

--- a/solution.py
+++ b/solution.py
@@ -114,21 +114,19 @@
     send_ref[:half] = total[half:].astype(BF16)
 
 
-def exchange_kernel(places, keep_ref, got_ref, other_ref, *rest):
+def exchange_kernel(places, keep_ref, got_ref, *rest):
     holders, (next_ref, send_ref) = (got_ref, *rest[:-2]), rest[-2:]
     rows = keep_ref.shape[0]
     total = keep_ref[...] + got_ref[:rows].astype(F32)
     next_ref[...] = total
     send_ref[:rows] = total.astype(BF16)
-    end = send_ref.shape[0] - other_ref.shape[0]
-    row = lax.broadcasted_iota(jnp.int32, (end - rows, keep_ref.shape[1]), 0)
+    row = lax.broadcasted_iota(jnp.int32, (send_ref.shape[0] - rows, keep_ref.shape[1]), 0)
     packed = jnp.zeros(row.shape, F32)
     for q, (holder, start, _) in enumerate(places):
         code = holders[holder][start : start + 16].astype(F32)
         packed = jnp.where(row == 2 * q, code[0:1], packed)
         packed = jnp.where(row == 2 * q + 1, code[1:2], packed)
-    send_ref[rows:end] = packed.astype(BF16)
-    send_ref[end:] = other_ref[...]
+    send_ref[rows:] = packed.astype(BF16)
 
 
 def halve_kernel(known, keep_ref, got_ref, sent_ref, next_ref, send_ref):
@@ -159,13 +157,12 @@
         at += ref.shape[0]
 
 
-def forward_kernel(keep_ref, got_ref, pair_ref, next_ref, send_ref):
+def sum_kernel(keep_ref, got_ref, other_ref, next_ref, send_ref, copy_ref):
     rows = keep_ref.shape[0]
     total = keep_ref[...] + got_ref[:rows].astype(F32)
     next_ref[...] = total
-    send_ref[:rows] = total.astype(BF16)
-    start = pair_ref.shape[0] - (send_ref.shape[0] - rows)
-    send_ref[rows:] = pair_ref[start:]
+    send_ref[...] = total.astype(BF16)
+    copy_ref[...] = other_ref[...]
 
 
 def outward(width, groups, subs, send_xp, send_xo, send_yp, send_yo):
@@ -285,13 +282,17 @@
     return even, value
 
 
-def local_kernel(own_ref, spill_ref, basis_ref, token_ref, far_ref, *rest):
-    y_refs, (out_ref, left_ref) = rest[:-2], rest[-2:]
+def inner(axis, value):
+    device, count = lax.axis_index(axis), lax.axis_size(axis)
+    has = jnp.logical_and(device != 0, device != count - 1)
+    return jnp.where(has, value, jnp.zeros(value.shape, value.dtype))
+
+
+def local_kernel(own_ref, spill_ref, basis_ref, token_ref, far_ref, other_ref, out_ref, left_ref):
     subs, rows, _ = own_ref.shape
     width = spill_ref.shape[3]
     halo = subs * width
-    masks = [mirror(bit) for bit in range(1, len(y_refs))]
-    even, other = from_other("gy", (halo, y_refs[1:]), masks, 2)
+    even, other = lax.axis_index("gy") % 2 == 0, inner("gy", other_ref[...])
     pair = far_ref[far_ref.shape[0] - halo :, : own_ref.shape[2]]
     for s in range(subs):
         values = jnp.concatenate(south_north(s, width, pair, other, even), axis=0)
@@ -340,12 +341,6 @@
         pick_ref[s] = spread_pick(rows, spill_ref[s, 0], range(4))
     for copy in copies:
         copy.wait()
-
-
-def inner(axis, value):
-    device, count = lax.axis_index(axis), lax.axis_size(axis)
-    has = jnp.logical_and(device != 0, device != count - 1)
-    return jnp.where(has, value, jnp.zeros(value.shape, value.dtype))
 
 
 def residual_kernel(
@@ -487,33 +482,26 @@
     packed = -(-2 * count_x // 16) * 16
     keep, send = call(
         functools.partial(exchange_kernel, places),
-        [((size, width), F32), ((size + packed + halo, width), BF16)],
-        [keep, got, halo_yo, *holders[1:]],
+        [((size, width), F32), ((size + packed, width), BF16)],
+        [keep, got, *holders[1:]],
         "coarse_sum",
     )
     got = swap(send, "gy", mask_of(1))
-    y_got = [got]
     for mask in gather_masks[2:-1]:
         near = join(near, far, got)
         far = swap(near, "gy", mask)
     near = join(near, far, got)
     partner = [(0, size + 2 * q // 16 * 16, 2 * q % 16) for q in range(count_x)]
     far = swap(picked(near, got, partner, [got], halo_yp), "gy", gather_masks[-1])
-    pending = [got]
-    bit = 1
-    while bit < steps_y:
-        for extra in pending[1:]:
-            keep = keep + extra[:size].astype(F32)
-        keep, send = call(
-            forward_kernel,
-            [((size, width), F32), ((size + halo, width), BF16)],
-            [keep, pending[0], y_got[-1]],
+    for bit in range(1, steps_y):
+        keep, send, halo_yo = call(
+            sum_kernel,
+            [((size, width), F32), ((size, width), BF16), ((halo, width), BF16)],
+            [keep, got, halo_yo],
             "coarse_sum",
         )
-        masks = [1 << bit]
-        pending = [swap(send, "gy", mask) for mask in masks]
-        y_got += pending
-        bit += 1
+        got = swap(send, "gy", 1 << bit)
+    far_halo = other(halo_yo, "gy")
 
     near = picked(near, send, places, holders)
 
@@ -521,7 +509,7 @@
     keep, send = call(
         functools.partial(coarse_kernel, size, gather_masks),
         [((half, width), F32), ((half + margin, width), BF16)],
-        [near, far, keep, halo_xp, *pending],
+        [near, far, keep, halo_xp, got],
         "coarse_solve",
     )
     x_got = [swap(send, "gx", mask_of(1))]
@@ -538,9 +526,9 @@
     local, left = call(
         local_kernel,
         [(block, F32), ((subs, rows, 2 * margin + 2 * functions), BF16)],
-        [own, spill_rows, coarse_basis, send, far, *y_got],
+        [own, spill_rows, coarse_basis, send, far, far_halo],
         "local_spread",
-        ins=[VMEM] * 3 + [ANY] + [VMEM] * (1 + len(y_got)),
+        ins=[VMEM] * 3 + [ANY] + [VMEM] * 2,
         limit=8,
     )
     correction, low, image, *sends = call(

time: 41 us -> 40 us (0.976)
  waiting for transfers between devices: 17.9 us -> 16.3 us
  starting transfers between devices: 13.9 us -> 14.5 us
    ppermute x12, waiting for transfers between devices: 15.5 us -> 11.8 us  [swap(): return lax.ppermute(value, axis, [(i, i ^ mask) for i in range(count)])]
    ppermute x2 -> x3, waiting for transfers between devices: 2.39 us -> 4.45 us  [other(): return lax.ppermute(value, ('gx', 'gy'), pairs)]
    ppermute x2 -> x3, starting transfers between devices: 1.86 us -> 3.12 us  [other(): return lax.ppermute(value, ('gx', 'gy'), pairs)]
    ppermute x12, starting transfers between devices: 12 us -> 11.3 us  [swap(): return lax.ppermute(value, axis, [(i, i ^ mask) for i in range(count)])]
  transfers between devices with their start and end apart: 14 -> 15, of which waited for: 10 -> 8; matrix products, arithmetic and copies ran while one was open for 0% -> 0% of each run, Pallas kernels for 9% -> 9%
where the time goes in v4:
time: 40 us; the launch traced here: 39.9 us
  waiting for transfers between devices  16.3 us (41%)
  starting transfers between devices  14.5 us (36%)
  Pallas kernels  8.29 us (21%)
  between operations  0.8 us (2%)
    ppermute x12, waiting for transfers between devices, swap(): return lax.ppermute(value, axis, [(i, i ^ mask) for i in range(count)])  11.8 us
    ppermute x12, starting transfers between devices, swap(): return lax.ppermute(value, axis, [(i, i ^ mask) for i in range(count)])  11.3 us
    pallas_call x16, Pallas kernels, call(): pl.pallas_call(kernel, out_shape=[jax.ShapeDtypeStruct(shape, dtype) for...  8.29 us
    ppermute x3, waiting for transfers between devices, other(): return lax.ppermute(value, ('gx', 'gy'), pairs)  4.45 us
    ppermute x3, starting transfers between devices, other(): return lax.ppermute(value, ('gx', 'gy'), pairs)  3.12 us
  transfers between devices with their start and end apart: 15, of which 8 were waited for; matrix products, arithmetic and copies ran while one was open for 0% of the time, Pallas kernels for 9%

profile of v4, /device:TPU:8, one launch (start us, length us, event | category | flops | bytes accessed | tf_op | source)
XLA Modules:
  0.0 39.9 jit_solution(8674205264265853226)
XLA Ops:
  0.7 2.0 %coarse_terms.1 = (f32[512,128]{1,0:T(8,128)S(1)}, bf16[528,128]{1,0:T(8,128)(2,1)S(1)}, bf16[2,768,128]{2,1,0:T(8,128)(2,1)S(1)}) custom-call(f32[2,1,768,128]{3,2,1,0:T(8,128)} %rhs_ref.1, bf16[2,1,64,768]{3,2,1,0:T(8,128)(2,1)} %basis_ref.1, s32[2,1,64]{2,1,0:T(1,128)} %ids_hbm.1), custom_call_target="tpu_custom_call" | custom-call | flops 1000000000 | bytes 1048576 | tf_op jit(solution)/shard_map/coarse_terms/pallas_call | solution.py:380
  2.7 0.1 collective-permute-start
  2.8 2.7 %collective-permute-start.1 = (bf16[32,1024]{1,0:T(8,128)(2,1)S(1)}, bf16[32,1024]{1,0:T(8,128)(2,1)S(1)}, u32[]{:S(2)}, u32[]{:S(2)}) collective-permute-start(bf16[32,1024]{1,0:T(8,128)(2,1)S(1)} %copy-done.5), channel_id=1, source_target_pairs={{0,4},{1,5},{2,6},{3,7},{4,0},{5,1},{6,2},{7,3},{8,12},{9,13},{10,... | collective-permute-start | bytes 196616 | tf_op jit(solution)/shard_map/ppermute | solution.py:29
  5.5 1.3 %collective-permute-start.3 = (bf16[288,128]{1,0:T(8,128)(2,1)S(1)}, bf16[288,128]{1,0:T(8,128)(2,1)S(1)}, u32[]{:S(2)}, u32[]{:S(2)}) collective-permute-start(bf16[288,128]{1,0:T(8,128)(2,1)S(1)} %get-tuple-element.40.token_ref), channel_id=1, source_target_pairs={{0,24},{8,16},{16,8},{24,0},{1,25},{9,17},{17,9},{25,1},{2,26},{10... | collective-permute-start | bytes 221192 | tf_op jit(solution)/shard_map/ppermute | solution.py:29
  6.8 1.0 %local_solve.1 = (f32[2,768,128]{2,1,0:T(8,128)S(1)}, bf16[2,256,128]{2,1,0:T(8,128)(2,1)S(1)}, bf16[64,128]{1,0:T(8,128)(2,1)S(1)}, bf16[64,128]{1,0:T(8,128)(2...) custom-call(bf16[2,1,1024,768]{3,2,1,0:T(8,128)(2,1)S(1)} %copy-done.3, ...), custom_call_target="tpu_custom_call" | custom-call | flops 1000000000 | bytes 1048576 | tf_op jit(solution)/shard_map/local_solve/pallas_call | solution.py:380
  7.8 1.9 %collective-permute-done.3.got_ref.rest_0_ = bf16[288,128]{1,0:T(8,128)(2,1)S(1)} collective-permute-done((bf16[288,128]{1,0:T(8,128)(2,1)S(1)}, bf16[288,128]{1,0:T(8,128)(2,1)S(1)}, u32[]{:S(2)}, u32[]{:S(2)}) %collective-permute-start.3) | collective-permute-done | bytes 73760 | tf_op jit(solution)/shard_map/ppermute | solution.py:29
  9.8 1.5 %collective-permute-start.4 = (bf16[272,128]{1,0:T(8,128)(2,1)S(1)}, bf16[272,128]{1,0:T(8,128)(2,1)S(1)}, u32[]{:S(2)}, u32[]{:S(2)}) collective-permute-start(bf16[272,128]{1,0:T(8,128)(2,1)S(1)} %get-tuple-element.43), channel_id=1, source_target_pairs={{0,1},{1,0},{2,3},{3,2},{4,5},{5,4},{6,7},{7,6},{8,9},{9,8},{10,11... | collective-permute-start | bytes 208904 | tf_op jit(solution)/shard_map/ppermute | solution.py:29
  11.3 0.5 %collective-permute-start.2 = (bf16[64,1024]{1,0:T(8,128)(2,1)S(1)}, bf16[64,1024]{1,0:T(8,128)(2,1)S(1)}, u32[]{:S(2)}, u32[]{:S(2)}) collective-permute-start(bf16[64,1024]{1,0:T(8,128)(2,1)S(1)} %inverse_join.2.near_ref), channel_id=1, source_target_pairs={{0,2},{1,3},{2,0},{3,1},{4,6},{5,7},{6,4},{7,5},{8,10},{9,11},{10,... | collective-permute-start | bytes 393224 | tf_op jit(solution)/shard_map/ppermute | solution.py:29
  11.9 2.3 %collective-permute-done.4.token_ref.got_ref.rest_0_ = bf16[272,128]{1,0:T(8,128)(2,1)S(1)} collective-permute-done((bf16[272,128]{1,0:T(8,128)(2,1)S(1)}, bf16[272,128]{1,0:T(8,128)(2,1)S(1)}, u32[]{:S(2)}, u32[]{:S(2)}) %collective-permute-start.4) | collective-permute-done | bytes 69664 | tf_op jit(solution)/shard_map/ppermute | solution.py:29
  14.2 0.5 %collective-permute-start.5 = (bf16[256,128]{1,0:T(8,128)(2,1)S(1)}, bf16[256,128]{1,0:T(8,128)(2,1)S(1)}, u32[]{:S(2)}, u32[]{:S(2)}) collective-permute-start(bf16[256,128]{1,0:T(8,128)(2,1)S(1)} %get-tuple-element.47), channel_id=1, source_target_pairs={{0,2},{1,3},{2,0},{3,1},{4,6},{5,7},{6,4},{7,5},{8,10},{9,11},{10,... | collective-permute-start | bytes 196616 | tf_op jit(solution)/shard_map/ppermute | solution.py:29
  14.7 2.7 %collective-permute-done.2.far_ref = bf16[64,1024]{1,0:T(8,128)(2,1)S(1)} collective-permute-done((bf16[64,1024]{1,0:T(8,128)(2,1)S(1)}, bf16[64,1024]{1,0:T(8,128)(2,1)S(1)}, u32[]{:S(2)}, u32[]{:S(2)}) %collective-permute-start.2) | collective-permute-done | bytes 131104 | tf_op jit(solution)/shard_map/ppermute | solution.py:29
  17.4 0.5 %inverse_pick.3 = bf16[640,128]{1,0:T(8,128)(2,1)S(1)} custom-call(bf16[128,1024]{1,0:T(8,128)(2,1)S(1)} %inverse_join.3.rows_ref, bf16[272,128]{1,0:T(8,128)(2,1)S(1)} %collective-permute-done.4.token_ref.got_ref.rest_0_, bf16[272,128]{1,0:T(8,128)(2,1)S(1)} %collective-permute-done.4.token_ref.got_ref.rest_0_, bf16[128,128]{1,0:T(8,128)(2,1)S(1)} %get-tuple-element.50.rest_1_), custom_call_target="tpu_custom_call" | custom-call | flops 1000000000 | bytes 1048576 | tf_op jit(solution)/shard_map/inverse_pick/pallas_call | solution.py:380
  17.9 0.1 collective-permute-start.6
  18.0 0.5 %collective-permute-done.5.got_ref = bf16[256,128]{1,0:T(8,128)(2,1)S(1)} collective-permute-done((bf16[256,128]{1,0:T(8,128)(2,1)S(1)}, bf16[256,128]{1,0:T(8,128)(2,1)S(1)}, u32[]{:S(2)}, u32[]{:S(2)}) %collective-permute-start.5) | collective-permute-done | bytes 65568 | tf_op jit(solution)/shard_map/ppermute | solution.py:29
  18.5 1.6 %collective-permute-start.7 = (bf16[256,128]{1,0:T(8,128)(2,1)S(1)}, bf16[256,128]{1,0:T(8,128)(2,1)S(1)}, u32[]{:S(2)}, u32[]{:S(2)}) collective-permute-start(bf16[256,128]{1,0:T(8,128)(2,1)S(1)} %get-tuple-element.49.token_ref), channel_id=1, source_target_pairs={{0,4},{1,5},{2,6},{3,7},{4,0},{5,1},{6,2},{7,3},{8,12},{9,13},{10,... | collective-permute-start | bytes 196616 | tf_op jit(solution)/shard_map/ppermute | solution.py:29
  20.1 0.5 %inverse_pick.2.near_ref = bf16[512,128]{1,0:T(8,128)(2,1)S(1)} custom-call(bf16[128,1024]{1,0:T(8,128)(2,1)S(1)} %inverse_join.3.rows_ref, bf16[256,128]{1,0:T(8,128)(2,1)S(1)} %get-tuple-element.49.token_ref, bf16[288,128]{1,0:T(8,128)(2,1)S(1)} %collective-permute-done.3.got_ref.rest_0_, bf16[528,128]{1,0:T(8,128)(2,1)S(1)} %get-tuple-element.39.sent_ref.rest_0_.rest_1_, ...), custom_call_target="tpu_custom_call" | custom-call | flops 1000000000 | bytes 1048576 | tf_op jit(solution)/shard_map/inverse_pick/pallas_call | solution.py:380
  20.6 3.2 %collective-permute-done.7.rest_0_ = bf16[256,128]{1,0:T(8,128)(2,1)S(1)} collective-permute-done((bf16[256,128]{1,0:T(8,128)(2,1)S(1)}, bf16[256,128]{1,0:T(8,128)(2,1)S(1)}, u32[]{:S(2)}, u32[]{:S(2)}) %collective-permute-start.7) | collective-permute-done | bytes 65568 | tf_op jit(solution)/shard_map/ppermute | solution.py:29
  23.8 0.4 %coarse_solve.1 = (f32[256,128]{1,0:T(8,128)S(1)}, bf16[320,128]{1,0:T(8,128)(2,1)S(1)}) custom-call(bf16[512,128]{1,0:T(8,128)(2,1)S(1)} %inverse_pick.2.near_ref, bf16[640,128]{1,0:T(8,128)(2,1)S(1)} %collective-permute-done.6.far_ref, f32[256,128]{1,0:T(8,128)S(1)} %get-tuple-element.51.keep_ref, bf16[64,128]{1,0:T(8,128)(2,1)S(1)} %get-tuple-element.52.halo_ref, ...), custom_call_target="tpu_custom_call" | custom-call | flops 1000000000 | bytes 1048576 | tf_op jit(solution)/shard_map/coarse_solve/pallas_call | solution.py:380
  24.2 0.1 collective-permute-start.8
  24.3 1.5 %collective-permute-start.9 = (bf16[128,128]{1,0:T(8,128)(2,1)S(1)}, bf16[128,128]{1,0:T(8,128)(2,1)S(1)}, u32[]{:S(2)}, u32[]{:S(2)}) collective-permute-start(bf16[128,128]{1,0:T(8,128)(2,1)S(1)} %get-tuple-element.57), channel_id=1, source_target_pairs={{0,8},{1,2},{2,1},{3,4},{4,3},{5,6},{6,5},{7,15},{8,0},{9,10},{10,... | collective-permute-start | bytes 98312 | tf_op jit(solution)/shard_map/ppermute | solution.py:45
  25.8 1.4 %collective-permute-start.10 = (bf16[192,128]{1,0:T(8,128)(2,1)S(1)}, bf16[192,128]{1,0:T(8,128)(2,1)S(1)}, u32[]{:S(2)}, u32[]{:S(2)}) collective-permute-start(bf16[192,128]{1,0:T(8,128)(2,1)S(1)} %get-tuple-element.56.token_ref), channel_id=1, source_target_pairs={{0,24},{8,16},{16,8},{24,0},{1,25},{9,17},{17,9},{25,1},{2,26},{10... | collective-permute-start | bytes 147464 | tf_op jit(solution)/shard_map/ppermute | solution.py:29
  27.1 2.0 %collective-permute-done.9.other_ref = bf16[128,128]{1,0:T(8,128)(2,1)S(1)} collective-permute-done((bf16[128,128]{1,0:T(8,128)(2,1)S(1)}, bf16[128,128]{1,0:T(8,128)(2,1)S(1)}, u32[]{:S(2)}, u32[]{:S(2)}) %collective-permute-start.9) | collective-permute-done | bytes 32800 | tf_op jit(solution)/shard_map/ppermute | solution.py:45
  29.2 0.4 %local_spread.1 = (f32[2,768,128]{2,1,0:T(8,128)S(1)}, bf16[2,768,256]{2,1,0:T(8,128)(2,1)S(1)}) custom-call(f32[2,768,128]{2,1,0:T(8,128)S(1)} %get-tuple-element.41.token_ref.own_ref, s32[2,1,4,64]{3,2,1,0:T(4,128)S(1)} %copy-done.2, bf16[2,1,64,768]{3,2,1,0:T(8,128)(2,1)S(1)} %copy-done.4, bf16[192,128]{1,0:T(8,128)(2,1)S(1)} %get-tuple-element.56.token_ref, ...), custom_call_target="tpu_custom_call" | custom-call | flops 1000000000 | bytes 1048576 | tf_op jit(solution)/shard_map/local_spread/pallas_call | solution.py:380
  29.6 1.0 %correction.1 = (f32[2,768,128]{2,1,0:T(8,128)S(1)}, bf16[2,768,128]{2,1,0:T(8,128)(2,1)S(1)}, bf16[2,256,128]{2,1,0:T(8,128)(2,1)S(1)}, bf16[64,128]{1,0:T(8,12...) custom-call(f32[2,768,128]{2,1,0:T(8,128)S(1)} %get-tuple-element.58.local_ref,, ...), custom_call_target="tpu_custom_call" | custom-call | flops 1000000000 | bytes 1048576 | tf_op jit(solution)/shard_map/correction/pallas_call | solution.py:380
  30.6 0.1 collective-permute-start.11
  30.7 1.6 %collective-permute-start.12 = (bf16[64,128]{1,0:T(8,128)(2,1)S(1)}, bf16[64,128]{1,0:T(8,128)(2,1)S(1)}, u32[]{:S(2)}, u32[]{:S(2)}) collective-permute-start(bf16[64,128]{1,0:T(8,128)(2,1)S(1)} %get-tuple-element.69), channel_id=1, source_target_pairs={{0,24},{1,25},{2,26},{3,27},{4,28},{5,29},{6,30},{7,31},{8,16},{9,... | collective-permute-start | bytes 49160 | tf_op jit(solution)/shard_map/ppermute | solution.py:45
  32.3 1.5 %collective-permute-start.13 = (bf16[128,128]{1,0:T(8,128)(2,1)S(1)}, bf16[128,128]{1,0:T(8,128)(2,1)S(1)}, u32[]{:S(2)}, u32[]{:S(2)}) collective-permute-start(bf16[128,128]{1,0:T(8,128)(2,1)S(1)} %get-tuple-element.70), channel_id=1, source_target_pairs={{0,1},{1,0},{2,3},{3,2},{4,5},{5,4},{6,7},{7,6},{8,9},{9,8},{10,11... | collective-permute-start | bytes 98312 | tf_op jit(solution)/shard_map/ppermute | solution.py:29
  33.9 0.1 collective-permute-start.14
  33.9 1.1 %image_own.1 = (f32[2,768,128]{2,1,0:T(8,128)S(1)}, bf16[2,768,256]{2,1,0:T(8,128)(2,1)S(1)}, f32[2,1,768,128]{3,2,1,0:T(8,128)}) custom-call(bf16[2,1,1024,768]{3,2,1,0:T(8,128)(2,1)S(1)} %copy-done, bf16[2,768,128]{2,1,0:T(8,128)(2,1)S(1)} %get-tuple-element.62.low_ref, f32[2,1,768,128]{3,2,1,0:T(8,128)S(1)} %copy-done.1, ...), custom_call_target="tpu_custom_call" | custom-call | flops 1000000000 | bytes 1048576 | tf_op jit(solution)/shard_map/image_own/pallas_call | solution.py:380
  35.0 1.2 %collective-permute-done.13.yp_ref = bf16[128,128]{1,0:T(8,128)(2,1)S(1)} collective-permute-done((bf16[128,128]{1,0:T(8,128)(2,1)S(1)}, bf16[128,128]{1,0:T(8,128)(2,1)S(1)}, u32[]{:S(2)}, u32[]{:S(2)}) %collective-permute-start.13) | collective-permute-done | bytes 32800 | tf_op jit(solution)/shard_map/ppermute | solution.py:29
  36.3 2.4 %collective-permute-done.14.yo_ref = bf16[128,128]{1,0:T(8,128)(2,1)S(1)} collective-permute-done((bf16[128,128]{1,0:T(8,128)(2,1)S(1)}, bf16[128,128]{1,0:T(8,128)(2,1)S(1)}, u32[]{:S(2)}, u32[]{:S(2)}) %collective-permute-start.14) | collective-permute-done | bytes 32800 | tf_op jit(solution)/shard_map/ppermute | solution.py:45
  38.7 1.2 %residual.1 = f32[2,1,768,128]{3,2,1,0:T(8,128)} custom-call(f32[2,768,128]{2,1,0:T(8,128)S(1)} %get-tuple-element.65.part_ref, bf16[2,256,128]{2,1,0:T(8,128)(2,1)S(1)} %get-tuple-element.66.image_ref, bf16[2,768,256]{2,1,0:T(8,128)(2,1)S(1)} %get-tuple-element.67.pick_ref, bf16[64,128]{1,0:T(8,128)(2,1)S(1)} %collective-permute-done.11.xp_ref, ...), custom_call_target="tpu_custom_call" | custom-call | flops 1000000000 | bytes 1048576 | tf_op jit(solution)/shard_map/residual/pallas_call | solution.py:380
  (26 shorter events, 0.2 us)
Async XLA Ops:
  0.6 2.1 %copy-start.5 = (bf16[32,1024]{1,0:T(8,128)(2,1)S(1)}, bf16[32,1024]{1,0:T(8,128)(2,1)}, u32[]{:S(2)}) copy-start(bf16[32,1024]{1,0:T(8,128)(2,1)} %near_ref.1) | copy-start | bytes 196612
  0.6 6.2 %copy-start.3 = (bf16[2,1,1024,768]{3,2,1,0:T(8,128)(2,1)S(1)}, bf16[2,1,1024,768]{3,2,1,0:T(8,128)(2,1)}, u32[]{:S(2)}) copy-start(bf16[2,1,1024,768]{3,2,1,0:T(8,128)(2,1)} %inverse_ref.1) | copy-start | bytes 9437188
  2.7 2.8 %collective-permute-start = (bf16[528,128]{1,0:T(8,128)(2,1)S(1)}, bf16[528,128]{1,0:T(8,128)(2,1)S(1)}, u32[]{:S(2)}, u32[]{:S(2)}) collective-permute-start(bf16[528,128]{1,0:T(8,128)(2,1)S(1)} %get-tuple-element.39.sent_ref.rest_0_.rest_1_), channel_id=1, source_target_pairs={{0,8},{8,0},{16,24},{24,16},{1,9},{9,1},{17,25},{25,17},{2,10},{10... | collective-permute-start | bytes 405512 | tf_op jit(solution)/shard_map/ppermute | solution.py:29
  2.8 8.6 %collective-permute-start.1 = (bf16[32,1024]{1,0:T(8,128)(2,1)S(1)}, bf16[32,1024]{1,0:T(8,128)(2,1)S(1)}, u32[]{:S(2)}, u32[]{:S(2)}) collective-permute-start(bf16[32,1024]{1,0:T(8,128)(2,1)S(1)} %copy-done.5), channel_id=1, source_target_pairs={{0,4},{1,5},{2,6},{3,7},{4,0},{5,1},{6,2},{7,3},{8,12},{9,13},{10,... | collective-permute-start | bytes 196616 | tf_op jit(solution)/shard_map/ppermute | solution.py:29
  5.5 4.3 %collective-permute-start.3 = (bf16[288,128]{1,0:T(8,128)(2,1)S(1)}, bf16[288,128]{1,0:T(8,128)(2,1)S(1)}, u32[]{:S(2)}, u32[]{:S(2)}) collective-permute-start(bf16[288,128]{1,0:T(8,128)(2,1)S(1)} %get-tuple-element.40.token_ref), channel_id=1, source_target_pairs={{0,24},{8,16},{16,8},{24,0},{1,25},{9,17},{17,9},{25,1},{2,26},{10... | collective-permute-start | bytes 221192 | tf_op jit(solution)/shard_map/ppermute | solution.py:29
  9.8 4.4 %collective-permute-start.4 = (bf16[272,128]{1,0:T(8,128)(2,1)S(1)}, bf16[272,128]{1,0:T(8,128)(2,1)S(1)}, u32[]{:S(2)}, u32[]{:S(2)}) collective-permute-start(bf16[272,128]{1,0:T(8,128)(2,1)S(1)} %get-tuple-element.43), channel_id=1, source_target_pairs={{0,1},{1,0},{2,3},{3,2},{4,5},{5,4},{6,7},{7,6},{8,9},{9,8},{10,11... | collective-permute-start | bytes 208904 | tf_op jit(solution)/shard_map/ppermute | solution.py:29
  11.3 6.1 %collective-permute-start.2 = (bf16[64,1024]{1,0:T(8,128)(2,1)S(1)}, bf16[64,1024]{1,0:T(8,128)(2,1)S(1)}, u32[]{:S(2)}, u32[]{:S(2)}) collective-permute-start(bf16[64,1024]{1,0:T(8,128)(2,1)S(1)} %inverse_join.2.near_ref), channel_id=1, source_target_pairs={{0,2},{1,3},{2,0},{3,1},{4,6},{5,7},{6,4},{7,5},{8,10},{9,11},{10,... | collective-permute-start | bytes 393224 | tf_op jit(solution)/shard_map/ppermute | solution.py:29
  14.2 4.3 %collective-permute-start.5 = (bf16[256,128]{1,0:T(8,128)(2,1)S(1)}, bf16[256,128]{1,0:T(8,128)(2,1)S(1)}, u32[]{:S(2)}, u32[]{:S(2)}) collective-permute-start(bf16[256,128]{1,0:T(8,128)(2,1)S(1)} %get-tuple-element.47), channel_id=1, source_target_pairs={{0,2},{1,3},{2,0},{3,1},{4,6},{5,7},{6,4},{7,5},{8,10},{9,11},{10,... | collective-permute-start | bytes 196616 | tf_op jit(solution)/shard_map/ppermute | solution.py:29
  17.9 5.8 %collective-permute-start.6 = (bf16[640,128]{1,0:T(8,128)(2,1)S(1)}, bf16[640,128]{1,0:T(8,128)(2,1)S(1)}, u32[]{:S(2)}, u32[]{:S(2)}) collective-permute-start(bf16[640,128]{1,0:T(8,128)(2,1)S(1)} %inverse_pick.3), channel_id=1, source_target_pairs={{0,1},{1,0},{2,3},{3,2},{4,5},{5,4},{6,7},{7,6},{8,9},{9,8},{10,11... | collective-permute-start | bytes 491528 | tf_op jit(solution)/shard_map/ppermute | solution.py:29
  18.5 5.2 %collective-permute-start.7 = (bf16[256,128]{1,0:T(8,128)(2,1)S(1)}, bf16[256,128]{1,0:T(8,128)(2,1)S(1)}, u32[]{:S(2)}, u32[]{:S(2)}) collective-permute-start(bf16[256,128]{1,0:T(8,128)(2,1)S(1)} %get-tuple-element.49.token_ref), channel_id=1, source_target_pairs={{0,4},{1,5},{2,6},{3,7},{4,0},{5,1},{6,2},{7,3},{8,12},{9,13},{10,... | collective-permute-start | bytes 196616 | tf_op jit(solution)/shard_map/ppermute | solution.py:29
  23.8 5.4 %copy-start.2 = (s32[2,1,4,64]{3,2,1,0:T(4,128)S(1)}, s32[2,1,4,64]{3,2,1,0:T(4,128)}, u32[]{:S(2)}) copy-start(s32[2,1,4,64]{3,2,1,0:T(4,128)} %spill_ref.3) | copy-start | bytes 6148
  23.8 5.4 %copy-start.4 = (bf16[2,1,64,768]{3,2,1,0:T(8,128)(2,1)S(1)}, bf16[2,1,64,768]{3,2,1,0:T(8,128)(2,1)}, u32[]{:S(2)}) copy-start(bf16[2,1,64,768]{3,2,1,0:T(8,128)(2,1)} %basis_ref.1) | copy-start | bytes 589828
  24.2 1.6 %collective-permute-start.8 = (bf16[320,128]{1,0:T(8,128)(2,1)S(1)}, bf16[320,128]{1,0:T(8,128)(2,1)S(1)}, u32[]{:S(2)}, u32[]{:S(2)}) collective-permute-start(bf16[320,128]{1,0:T(8,128)(2,1)S(1)} %get-tuple-element.54), channel_id=1, source_target_pairs={{0,8},{8,0},{16,24},{24,16},{1,9},{9,1},{17,25},{25,17},{2,10},{10... | collective-permute-start | bytes 245768 | tf_op jit(solution)/shard_map/ppermute | solution.py:29
  24.3 4.9 %collective-permute-start.9 = (bf16[128,128]{1,0:T(8,128)(2,1)S(1)}, bf16[128,128]{1,0:T(8,128)(2,1)S(1)}, u32[]{:S(2)}, u32[]{:S(2)}) collective-permute-start(bf16[128,128]{1,0:T(8,128)(2,1)S(1)} %get-tuple-element.57), channel_id=1, source_target_pairs={{0,8},{1,2},{2,1},{3,4},{4,3},{5,6},{6,5},{7,15},{8,0},{9,10},{10,... | collective-permute-start | bytes 98312 | tf_op jit(solution)/shard_map/ppermute | solution.py:45
  25.7 3.9 %copy-start = (bf16[2,1,1024,768]{3,2,1,0:T(8,128)(2,1)S(1)}, bf16[2,1,1024,768]{3,2,1,0:T(8,128)(2,1)}, u32[]{:S(2)}) copy-start(bf16[2,1,1024,768]{3,2,1,0:T(8,128)(2,1)} %operator_ref.3) | copy-start | bytes 9437188
  25.8 3.9 %collective-permute-start.10 = (bf16[192,128]{1,0:T(8,128)(2,1)S(1)}, bf16[192,128]{1,0:T(8,128)(2,1)S(1)}, u32[]{:S(2)}, u32[]{:S(2)}) collective-permute-start(bf16[192,128]{1,0:T(8,128)(2,1)S(1)} %get-tuple-element.56.token_ref), channel_id=1, source_target_pairs={{0,24},{8,16},{16,8},{24,0},{1,25},{9,17},{17,9},{25,1},{2,26},{10... | collective-permute-start | bytes 147464 | tf_op jit(solution)/shard_map/ppermute | solution.py:29
  29.6 4.3 %copy-start.1 = (f32[2,1,768,128]{3,2,1,0:T(8,128)S(1)}, f32[2,1,768,128]{3,2,1,0:T(8,128)}, u32[]{:S(2)}) copy-start(f32[2,1,768,128]{3,2,1,0:T(8,128)} %rhs_ref.1) | copy-start | bytes 2359300
  30.6 4.4 %collective-permute-start.11 = (bf16[64,128]{1,0:T(8,128)(2,1)S(1)}, bf16[64,128]{1,0:T(8,128)(2,1)S(1)}, u32[]{:S(2)}, u32[]{:S(2)}) collective-permute-start(bf16[64,128]{1,0:T(8,128)(2,1)S(1)} %get-tuple-element.68), channel_id=1, source_target_pairs={{0,8},{8,0},{16,24},{24,16},{1,9},{9,1},{17,25},{25,17},{2,10},{10... | collective-permute-start | bytes 49160 | tf_op jit(solution)/shard_map/ppermute | solution.py:29
  30.7 4.3 %collective-permute-start.12 = (bf16[64,128]{1,0:T(8,128)(2,1)S(1)}, bf16[64,128]{1,0:T(8,128)(2,1)S(1)}, u32[]{:S(2)}, u32[]{:S(2)}) collective-permute-start(bf16[64,128]{1,0:T(8,128)(2,1)S(1)} %get-tuple-element.69), channel_id=1, source_target_pairs={{0,24},{1,25},{2,26},{3,27},{4,28},{5,29},{6,30},{7,31},{8,16},{9,... | collective-permute-start | bytes 49160 | tf_op jit(solution)/shard_map/ppermute | solution.py:45
  32.3 3.9 %collective-permute-start.13 = (bf16[128,128]{1,0:T(8,128)(2,1)S(1)}, bf16[128,128]{1,0:T(8,128)(2,1)S(1)}, u32[]{:S(2)}, u32[]{:S(2)}) collective-permute-start(bf16[128,128]{1,0:T(8,128)(2,1)S(1)} %get-tuple-element.70), channel_id=1, source_target_pairs={{0,1},{1,0},{2,3},{3,2},{4,5},{5,4},{6,7},{7,6},{8,9},{9,8},{10,11... | collective-permute-start | bytes 98312 | tf_op jit(solution)/shard_map/ppermute | solution.py:29
  33.9 4.8 %collective-permute-start.14 = (bf16[128,128]{1,0:T(8,128)(2,1)S(1)}, bf16[128,128]{1,0:T(8,128)(2,1)S(1)}, u32[]{:S(2)}, u32[]{:S(2)}) collective-permute-start(bf16[128,128]{1,0:T(8,128)(2,1)S(1)} %get-tuple-element.71), channel_id=1, source_target_pairs={{0,8},{1,2},{2,1},{3,4},{4,3},{5,6},{6,5},{7,15},{8,0},{9,10},{10,... | collective-permute-start | bytes 98312 | tf_op jit(solution)/shard_map/ppermute | solution.py:45

commit v5 on v4

--- a/solution.py
+++ b/solution.py
@@ -55,6 +55,21 @@
     return place
 
 
+def gathered_place(row, rows, steps):
+    per_device = rows >> steps
+    left = (row // per_device) ^ lax.axis_index("gy")
+    place = row % per_device
+    for bit in range(steps):
+        place = place + ((left >> bit) & 1) * (rows >> (bit + 1))
+    return place
+
+
+def regathered(value, bit):
+    part = value.shape[0] >> (bit + 1)
+    pieces = [value[i * part : (i + 1) * part] for i in range(2 << bit)]
+    return jnp.concatenate([pieces[i ^ 1] for i in range(2 << bit)], axis=0)
+
+
 def halves(value):
     high = value.astype(BF16)
     low = (value - high.astype(F32)).astype(BF16)
@@ -81,7 +96,7 @@
 
 
 def terms_kernel(
-    steps, rhs_hbm, basis_hbm, ids_hbm, keep_ref, send_ref, low_ref, rhs_ref, basis_ref, ids_ref, sems
+    steps, steps_y, rhs_hbm, basis_hbm, ids_hbm, keep_ref, send_ref, low_ref, rhs_ref, basis_ref, ids_ref, sems
 ):
     device = lax.axis_index("gx")
     subs, functions, _ = basis_ref.shape
@@ -97,7 +112,8 @@
     row = lax.broadcasted_iota(jnp.int32, (16, ids.shape[1]), 0)
     coded = jnp.where(row == 0, ids // 256, jnp.where(row == 1, ids % 256, 0))
     send_ref[half:] = coded.astype(F32).astype(BF16)
-    place = relative_block(ids // block, device, steps) * block + ids % block
+    place = relative_block(ids // block, device, steps) * block
+    place = place + gathered_place(ids % block, block, steps_y)
     rows = lax.broadcasted_iota(jnp.int32, (order, ids.shape[1]), 0)
     pick = (rows == place).astype(BF16)
     terms = []
@@ -109,7 +125,10 @@
         low = (value - high.astype(F32)).astype(BF16)
         low_ref[s] = high
         terms.append(joined(mm(basis_ref[s], jnp.concatenate([high, low], axis=1))))
-    total = joined(mm(pick, halves(jnp.concatenate(terms, axis=0))))
+    terms = jnp.concatenate(terms, axis=0)
+    high = terms.astype(BF16)
+    low = (terms - high.astype(F32)).astype(BF16)
+    total = mm(jnp.concatenate([pick, pick], axis=1), jnp.concatenate([high, low], axis=0))
     keep_ref[...] = total[:half]
     send_ref[:half] = total[half:].astype(BF16)
 
@@ -157,9 +176,9 @@
         at += ref.shape[0]
 
 
-def sum_kernel(keep_ref, got_ref, other_ref, next_ref, send_ref, copy_ref):
+def sum_kernel(bit, keep_ref, got_ref, other_ref, next_ref, send_ref, copy_ref):
     rows = keep_ref.shape[0]
-    total = keep_ref[...] + got_ref[:rows].astype(F32)
+    total = keep_ref[...] + regathered(got_ref[:rows].astype(F32), bit)
     next_ref[...] = total
     send_ref[...] = total.astype(BF16)
     copy_ref[...] = other_ref[...]
@@ -209,31 +228,14 @@
         out_ref[end:, : carried_ref.shape[1]] = carried_ref[...]
 
 
-def arranged(low, masks, first):
-    device = lax.axis_index("gy")
-    rows = low.shape[0]
-    per_device = rows >> len(masks)
-    half = rows // 2
-    place = lax.broadcasted_iota(jnp.int32, (half, rows), 0) + first
-    target = lax.broadcasted_iota(jnp.int32, (half, rows), 1)
-    piece = place // per_device
-    source = piece * 0 + device
-    for bit, mask in enumerate(masks):
-        source = source ^ (((piece >> bit) & 1) * mask)
-    pick = (source * per_device + place % per_device == target).astype(BF16)
-    return mm(pick, low).astype(BF16)
-
-
-def coarse_kernel(rows, masks, near_ref, far_ref, keep_ref, halo_ref, *rest):
-    got_refs, next_ref, send_ref = rest[:-2], rest[-2], rest[-1]
-    total = keep_ref[...]
-    for ref in got_refs:
-        total = total + ref[:rows].astype(F32)
+def coarse_kernel(bit, near_ref, far_ref, keep_ref, halo_ref, got_ref, next_ref, send_ref):
+    rows = keep_ref.shape[0]
+    total = keep_ref[...] + regathered(got_ref[...].astype(F32), bit)
     low = total.astype(BF16)
     half = next_ref.shape[0]
     count = near_ref.shape[0]
-    value = mm(near_ref[...], arranged(low, masks, 0))
-    value = value + mm(far_ref[:count, : rows // 2], arranged(low, masks, rows // 2))
+    left = jnp.concatenate([near_ref[...], far_ref[:count, : rows // 2]], axis=1)
+    value = mm(left, low)
     next_ref[...] = value[:half]
     send_ref[:half] = value[half:].astype(BF16)
     send_ref[half:] = halo_ref[...]
@@ -288,21 +290,25 @@
     return jnp.where(has, value, jnp.zeros(value.shape, value.dtype))
 
 
-def local_kernel(own_ref, spill_ref, basis_ref, token_ref, far_ref, other_ref, out_ref, left_ref):
+def local_kernel(own_ref, spill_ref, basis_ref, token_ref, far_ref, out_ref, left_ref):
     subs, rows, _ = own_ref.shape
     width = spill_ref.shape[3]
     halo = subs * width
-    even, other = lax.axis_index("gy") % 2 == 0, inner("gy", other_ref[...])
+    even = lax.axis_index("gy") % 2 == 0
     pair = far_ref[far_ref.shape[0] - halo :, : own_ref.shape[2]]
     for s in range(subs):
-        values = jnp.concatenate(south_north(s, width, pair, other, even), axis=0)
-        out_ref[s] = own_ref[s] + mm(spread_pick(rows, spill_ref[s, 0], (2, 3)), values)
-        left_ref[s, :, : 2 * width] = spread_pick(rows, spill_ref[s, 0], (0, 1))
+        spill = spill_ref[s, 0]
+        near = jnp.where(even, spill[3:4], spill[2:3])
+        value = pair[s * width : (s + 1) * width]
+        out_ref[s] = own_ref[s] + mm(spread_pick(rows, near, (0,)), value)
+        left_ref[s, :, : 2 * width] = spread_pick(rows, spill, (0, 1))
+        far = jnp.where(even, spill[2:3], spill[3:4])
         basis = basis_ref[s, 0].astype(F32)
-        left_ref[s, :, 2 * width :] = jnp.concatenate([basis, basis], axis=0).T.astype(BF16)
-
-
-def correction_kernel(width, local_ref, left_ref, margin_ref, operator_ref, keep_ref, *rest):
+        basis = jnp.concatenate([basis, basis], axis=0).T.astype(BF16)
+        left_ref[s, :, 2 * width :] = jnp.concatenate([spread_pick(rows, far, (0,)), basis], axis=1)
+
+
+def correction_kernel(width, local_ref, left_ref, margin_ref, operator_ref, far_ref, keep_ref, *rest):
     x_refs, (out_ref, low_ref, image_ref, *sends) = rest[:-7], rest[-7:]
     subs, rows, columns = local_ref.shape
     functions = keep_ref.shape[0] // subs
@@ -310,6 +316,7 @@
     masks = [mask_of(step) for step in range(2, len(x_refs) + 1)]
     even, other = from_other("gx", (width, x_refs[1:]), masks, 1)
     pair = x_refs[0][x_refs[0].shape[0] - width :]
+    far = inner("gy", far_ref[...])
 
     def margins(sub, number):
         return margin_ref[sub, number * width : (number + 1) * width]
@@ -318,7 +325,8 @@
         part = picked[s * functions : (s + 1) * functions]
         high = part.astype(BF16)
         low = (part - high.astype(F32)).astype(BF16)
-        values = west_east(subs, s, margins, pair, other, even) + [high, low]
+        values = west_east(subs, s, margins, pair, other, even)
+        values += [far[s * width : (s + 1) * width], high, low]
         value = local_ref[s] + mm(left_ref[s], jnp.concatenate(values, axis=0))
         out_ref[s] = value
         low = value.astype(BF16)
@@ -410,7 +418,7 @@
 
     size = order // 2
     keep, send, low = call(
-        functools.partial(terms_kernel, steps_x),
+        functools.partial(terms_kernel, steps_x, steps_y),
         [((size, width), F32), ((size + 16, listed), BF16), (block, BF16)],
         [pltpu.with_memory_space_constraint(x, pltpu.HBM) for x in (adjoint_rhs, coarse_basis, coarse_ids)],
         "coarse_terms",
@@ -495,7 +503,7 @@
     far = swap(picked(near, got, partner, [got], halo_yp), "gy", gather_masks[-1])
     for bit in range(1, steps_y):
         keep, send, halo_yo = call(
-            sum_kernel,
+            functools.partial(sum_kernel, bit - 1),
             [((size, width), F32), ((size, width), BF16), ((halo, width), BF16)],
             [keep, got, halo_yo],
             "coarse_sum",
@@ -507,7 +515,7 @@
 
     half = count_x * listed // 2
     keep, send = call(
-        functools.partial(coarse_kernel, size, gather_masks),
+        functools.partial(coarse_kernel, steps_y - 1),
         [((half, width), F32), ((half + margin, width), BF16)],
         [near, far, keep, halo_xp, got],
         "coarse_solve",
@@ -525,16 +533,16 @@
 
     local, left = call(
         local_kernel,
-        [(block, F32), ((subs, rows, 2 * margin + 2 * functions), BF16)],
-        [own, spill_rows, coarse_basis, send, far, far_halo],
+        [(block, F32), ((subs, rows, 3 * margin + 2 * functions), BF16)],
+        [own, spill_rows, coarse_basis, send, far],
         "local_spread",
-        ins=[VMEM] * 3 + [ANY] + [VMEM] * 2,
+        ins=[VMEM] * 3 + [ANY, VMEM],
         limit=8,
     )
     correction, low, image, *sends = call(
         functools.partial(correction_kernel, margin),
         [(block, F32), (block, BF16), ((subs, 4 * margin, width), BF16)] + messages,
-        [local, left, margins, local_operator, keep, *x_got],
+        [local, left, margins, local_operator, far_halo, keep, *x_got],
         "correction",
         limit=12,
     )

time: 40 us -> 39.5 us (0.988)
  waiting for transfers between devices: 16.3 us -> 15.8 us
    ppermute x3, waiting for transfers between devices: 4.45 us -> 3.7 us  [other(): return lax.ppermute(value, ('gx', 'gy'), pairs)]
  transfers between devices with their start and end apart: 15 -> 15, of which waited for: 8 -> 9; matrix products, arithmetic and copies ran while one was open for 0% -> 0% of each run, Pallas kernels for 9% -> 10%
where the time goes in v5:
time: 39.5 us; the launch traced here: 39.3 us
  waiting for transfers between devices  15.8 us (40%)
  starting transfers between devices  14.6 us (37%)
  Pallas kernels  8.15 us (21%)
  between operations  0.78 us (2%)
    ppermute x12, waiting for transfers between devices, swap(): return lax.ppermute(value, axis, [(i, i ^ mask) for i in range(count)])  12.1 us
    ppermute x12, starting transfers between devices, swap(): return lax.ppermute(value, axis, [(i, i ^ mask) for i in range(count)])  11.3 us
    pallas_call x16, Pallas kernels, call(): pl.pallas_call(kernel, out_shape=[jax.ShapeDtypeStruct(shape, dtype) for...  8.15 us
    ppermute x3, waiting for transfers between devices, other(): return lax.ppermute(value, ('gx', 'gy'), pairs)  3.7 us
    ppermute x3, starting transfers between devices, other(): return lax.ppermute(value, ('gx', 'gy'), pairs)  3.3 us
  transfers between devices with their start and end apart: 15, of which 9 were waited for; matrix products, arithmetic and copies ran while one was open for 0% of the time, Pallas kernels for 10%

profile of v5, /device:TPU:8, one launch (start us, length us, event | category | flops | bytes accessed | tf_op | source)
XLA Modules:
  0.0 39.3 jit_solution(9935008902510517131)
XLA Ops:
  0.7 2.0 %coarse_terms.1 = (f32[512,128]{1,0:T(8,128)S(1)}, bf16[528,128]{1,0:T(8,128)(2,1)S(1)}, bf16[2,768,128]{2,1,0:T(8,128)(2,1)S(1)}) custom-call(f32[2,1,768,128]{3,2,1,0:T(8,128)} %rhs_ref.1, bf16[2,1,64,768]{3,2,1,0:T(8,128)(2,1)} %basis_ref.1, s32[2,1,64]{2,1,0:T(1,128)} %ids_hbm.1), custom_call_target="tpu_custom_call" | custom-call | flops 1000000000 | bytes 1048576 | tf_op jit(solution)/shard_map/coarse_terms/pallas_call | solution.py:388
  2.7 0.1 collective-permute-start
  2.8 2.7 %collective-permute-start.1 = (bf16[32,1024]{1,0:T(8,128)(2,1)S(1)}, bf16[32,1024]{1,0:T(8,128)(2,1)S(1)}, u32[]{:S(2)}, u32[]{:S(2)}) collective-permute-start(bf16[32,1024]{1,0:T(8,128)(2,1)S(1)} %copy-done.5), channel_id=1, source_target_pairs={{0,4},{1,5},{2,6},{3,7},{4,0},{5,1},{6,2},{7,3},{8,12},{9,13},{10,... | collective-permute-start | bytes 196616 | tf_op jit(solution)/shard_map/ppermute | solution.py:29
  5.5 1.3 %collective-permute-start.3 = (bf16[288,128]{1,0:T(8,128)(2,1)S(1)}, bf16[288,128]{1,0:T(8,128)(2,1)S(1)}, u32[]{:S(2)}, u32[]{:S(2)}) collective-permute-start(bf16[288,128]{1,0:T(8,128)(2,1)S(1)} %get-tuple-element.40.token_ref), channel_id=1, source_target_pairs={{0,24},{8,16},{16,8},{24,0},{1,25},{9,17},{17,9},{25,1},{2,26},{10... | collective-permute-start | bytes 221192 | tf_op jit(solution)/shard_map/ppermute | solution.py:29
  6.8 1.0 %local_solve.1 = (f32[2,768,128]{2,1,0:T(8,128)S(1)}, bf16[2,256,128]{2,1,0:T(8,128)(2,1)S(1)}, bf16[64,128]{1,0:T(8,128)(2,1)S(1)}, bf16[64,128]{1,0:T(8,128)(2...) custom-call(bf16[2,1,1024,768]{3,2,1,0:T(8,128)(2,1)S(1)} %copy-done.3, ...), custom_call_target="tpu_custom_call" | custom-call | flops 1000000000 | bytes 1048576 | tf_op jit(solution)/shard_map/local_solve/pallas_call | solution.py:388
  7.8 1.9 %collective-permute-done.3.got_ref.rest_0_ = bf16[288,128]{1,0:T(8,128)(2,1)S(1)} collective-permute-done((bf16[288,128]{1,0:T(8,128)(2,1)S(1)}, bf16[288,128]{1,0:T(8,128)(2,1)S(1)}, u32[]{:S(2)}, u32[]{:S(2)}) %collective-permute-start.3) | collective-permute-done | bytes 73760 | tf_op jit(solution)/shard_map/ppermute | solution.py:29
  9.8 1.6 %collective-permute-start.4 = (bf16[272,128]{1,0:T(8,128)(2,1)S(1)}, bf16[272,128]{1,0:T(8,128)(2,1)S(1)}, u32[]{:S(2)}, u32[]{:S(2)}) collective-permute-start(bf16[272,128]{1,0:T(8,128)(2,1)S(1)} %get-tuple-element.43), channel_id=1, source_target_pairs={{0,1},{1,0},{2,3},{3,2},{4,5},{5,4},{6,7},{7,6},{8,9},{9,8},{10,11... | collective-permute-start | bytes 208904 | tf_op jit(solution)/shard_map/ppermute | solution.py:29
  11.4 0.5 %collective-permute-start.2 = (bf16[64,1024]{1,0:T(8,128)(2,1)S(1)}, bf16[64,1024]{1,0:T(8,128)(2,1)S(1)}, u32[]{:S(2)}, u32[]{:S(2)}) collective-permute-start(bf16[64,1024]{1,0:T(8,128)(2,1)S(1)} %inverse_join.2.near_ref), channel_id=1, source_target_pairs={{0,2},{1,3},{2,0},{3,1},{4,6},{5,7},{6,4},{7,5},{8,10},{9,11},{10,... | collective-permute-start | bytes 393224 | tf_op jit(solution)/shard_map/ppermute | solution.py:29
  11.9 2.3 %collective-permute-done.4.token_ref.got_ref.rest_0_ = bf16[272,128]{1,0:T(8,128)(2,1)S(1)} collective-permute-done((bf16[272,128]{1,0:T(8,128)(2,1)S(1)}, bf16[272,128]{1,0:T(8,128)(2,1)S(1)}, u32[]{:S(2)}, u32[]{:S(2)}) %collective-permute-start.4) | collective-permute-done | bytes 69664 | tf_op jit(solution)/shard_map/ppermute | solution.py:29
  14.2 0.5 %collective-permute-start.5 = (bf16[256,128]{1,0:T(8,128)(2,1)S(1)}, bf16[256,128]{1,0:T(8,128)(2,1)S(1)}, u32[]{:S(2)}, u32[]{:S(2)}) collective-permute-start(bf16[256,128]{1,0:T(8,128)(2,1)S(1)} %get-tuple-element.47), channel_id=1, source_target_pairs={{0,2},{1,3},{2,0},{3,1},{4,6},{5,7},{6,4},{7,5},{8,10},{9,11},{10,... | collective-permute-start | bytes 196616 | tf_op jit(solution)/shard_map/ppermute | solution.py:29
  14.7 2.7 %collective-permute-done.2.far_ref = bf16[64,1024]{1,0:T(8,128)(2,1)S(1)} collective-permute-done((bf16[64,1024]{1,0:T(8,128)(2,1)S(1)}, bf16[64,1024]{1,0:T(8,128)(2,1)S(1)}, u32[]{:S(2)}, u32[]{:S(2)}) %collective-permute-start.2) | collective-permute-done | bytes 131104 | tf_op jit(solution)/shard_map/ppermute | solution.py:29
  17.4 0.5 %inverse_pick.3 = bf16[640,128]{1,0:T(8,128)(2,1)S(1)} custom-call(bf16[128,1024]{1,0:T(8,128)(2,1)S(1)} %inverse_join.3.rows_ref, bf16[272,128]{1,0:T(8,128)(2,1)S(1)} %collective-permute-done.4.token_ref.got_ref.rest_0_, bf16[272,128]{1,0:T(8,128)(2,1)S(1)} %collective-permute-done.4.token_ref.got_ref.rest_0_, bf16[128,128]{1,0:T(8,128)(2,1)S(1)} %get-tuple-element.50.rest_1_), custom_call_target="tpu_custom_call" | custom-call | flops 1000000000 | bytes 1048576 | tf_op jit(solution)/shard_map/inverse_pick/pallas_call | solution.py:388
  18.0 0.1 collective-permute-start.6
  18.0 0.5 %collective-permute-done.5.got_ref = bf16[256,128]{1,0:T(8,128)(2,1)S(1)} collective-permute-done((bf16[256,128]{1,0:T(8,128)(2,1)S(1)}, bf16[256,128]{1,0:T(8,128)(2,1)S(1)}, u32[]{:S(2)}, u32[]{:S(2)}) %collective-permute-start.5) | collective-permute-done | bytes 65568 | tf_op jit(solution)/shard_map/ppermute | solution.py:29
  18.5 1.6 %collective-permute-start.7 = (bf16[256,128]{1,0:T(8,128)(2,1)S(1)}, bf16[256,128]{1,0:T(8,128)(2,1)S(1)}, u32[]{:S(2)}, u32[]{:S(2)}) collective-permute-start(bf16[256,128]{1,0:T(8,128)(2,1)S(1)} %get-tuple-element.49.token_ref), channel_id=1, source_target_pairs={{0,4},{1,5},{2,6},{3,7},{4,0},{5,1},{6,2},{7,3},{8,12},{9,13},{10,... | collective-permute-start | bytes 196616 | tf_op jit(solution)/shard_map/ppermute | solution.py:29
  20.1 0.5 %inverse_pick.2.near_ref = bf16[512,128]{1,0:T(8,128)(2,1)S(1)} custom-call(bf16[128,1024]{1,0:T(8,128)(2,1)S(1)} %inverse_join.3.rows_ref, bf16[256,128]{1,0:T(8,128)(2,1)S(1)} %get-tuple-element.49.token_ref, bf16[288,128]{1,0:T(8,128)(2,1)S(1)} %collective-permute-done.3.got_ref.rest_0_, bf16[528,128]{1,0:T(8,128)(2,1)S(1)} %get-tuple-element.39.sent_ref.rest_0_.rest_1_, ...), custom_call_target="tpu_custom_call" | custom-call | flops 1000000000 | bytes 1048576 | tf_op jit(solution)/shard_map/inverse_pick/pallas_call | solution.py:388
  20.6 3.2 %collective-permute-done.7.got_ref = bf16[256,128]{1,0:T(8,128)(2,1)S(1)} collective-permute-done((bf16[256,128]{1,0:T(8,128)(2,1)S(1)}, bf16[256,128]{1,0:T(8,128)(2,1)S(1)}, u32[]{:S(2)}, u32[]{:S(2)}) %collective-permute-start.7) | collective-permute-done | bytes 65568 | tf_op jit(solution)/shard_map/ppermute | solution.py:29
  23.8 0.2 coarse_solve.1
  24.1 1.5 %collective-permute-start.9 = (bf16[128,128]{1,0:T(8,128)(2,1)S(1)}, bf16[128,128]{1,0:T(8,128)(2,1)S(1)}, u32[]{:S(2)}, u32[]{:S(2)}) collective-permute-start(bf16[128,128]{1,0:T(8,128)(2,1)S(1)} %get-tuple-element.60), channel_id=1, source_target_pairs={{0,8},{1,2},{2,1},{3,4},{4,3},{5,6},{6,5},{7,15},{8,0},{9,10},{10,... | collective-permute-start | bytes 98312 | tf_op jit(solution)/shard_map/ppermute | solution.py:45
  25.6 1.3 %collective-permute-start.10 = (bf16[192,128]{1,0:T(8,128)(2,1)S(1)}, bf16[192,128]{1,0:T(8,128)(2,1)S(1)}, u32[]{:S(2)}, u32[]{:S(2)}) collective-permute-start(bf16[192,128]{1,0:T(8,128)(2,1)S(1)} %get-tuple-element.56.token_ref), channel_id=1, source_target_pairs={{0,24},{8,16},{16,8},{24,0},{1,25},{9,17},{17,9},{25,1},{2,26},{10... | collective-permute-start | bytes 147464 | tf_op jit(solution)/shard_map/ppermute | solution.py:29
  26.9 0.6 %local_spread.1 = (f32[2,768,128]{2,1,0:T(8,128)S(1)}, bf16[2,768,320]{2,1,0:T(8,128)(2,1)S(1)}) custom-call(f32[2,768,128]{2,1,0:T(8,128)S(1)} %get-tuple-element.41.token_ref.own_ref, s32[2,1,4,64]{3,2,1,0:T(4,128)S(1)} %copy-done.2, bf16[2,1,64,768]{3,2,1,0:T(8,128)(2,1)S(1)} %copy-done.4, bf16[192,128]{1,0:T(8,128)(2,1)S(1)} %get-tuple-element.56.token_ref, ...), custom_call_target="tpu_custom_call" | custom-call | flops 1000000000 | bytes 1048576 | tf_op jit(solution)/shard_map/local_spread/pallas_call | solution.py:388
  27.5 1.5 %collective-permute-done.9.far_ref = bf16[128,128]{1,0:T(8,128)(2,1)S(1)} collective-permute-done((bf16[128,128]{1,0:T(8,128)(2,1)S(1)}, bf16[128,128]{1,0:T(8,128)(2,1)S(1)}, u32[]{:S(2)}, u32[]{:S(2)}) %collective-permute-start.9) | collective-permute-done | bytes 32800 | tf_op jit(solution)/shard_map/ppermute | solution.py:45
  29.0 0.4 collective-permute-done.10.rest_1_
  29.4 0.9 %correction.1 = (f32[2,768,128]{2,1,0:T(8,128)S(1)}, bf16[2,768,128]{2,1,0:T(8,128)(2,1)S(1)}, bf16[2,256,128]{2,1,0:T(8,128)(2,1)S(1)}, bf16[64,128]{1,0:T(8,12...) custom-call(f32[2,768,128]{2,1,0:T(8,128)S(1)} %get-tuple-element.57.local_ref,, ...), custom_call_target="tpu_custom_call" | custom-call | flops 1000000000 | bytes 1048576 | tf_op jit(solution)/shard_map/correction/pallas_call | solution.py:388
  30.3 0.2 collective-permute-start.11
  30.5 1.5 %collective-permute-start.12 = (bf16[64,128]{1,0:T(8,128)(2,1)S(1)}, bf16[64,128]{1,0:T(8,128)(2,1)S(1)}, u32[]{:S(2)}, u32[]{:S(2)}) collective-permute-start(bf16[64,128]{1,0:T(8,128)(2,1)S(1)} %get-tuple-element.69), channel_id=1, source_target_pairs={{0,24},{1,25},{2,26},{3,27},{4,28},{5,29},{6,30},{7,31},{8,16},{9,... | collective-permute-start | bytes 49160 | tf_op jit(solution)/shard_map/ppermute | solution.py:45
  32.0 1.3 %collective-permute-start.13 = (bf16[128,128]{1,0:T(8,128)(2,1)S(1)}, bf16[128,128]{1,0:T(8,128)(2,1)S(1)}, u32[]{:S(2)}, u32[]{:S(2)}) collective-permute-start(bf16[128,128]{1,0:T(8,128)(2,1)S(1)} %get-tuple-element.70), channel_id=1, source_target_pairs={{0,1},{1,0},{2,3},{3,2},{4,5},{5,4},{6,7},{7,6},{8,9},{9,8},{10,11... | collective-permute-start | bytes 98312 | tf_op jit(solution)/shard_map/ppermute | solution.py:29
  33.3 0.4 collective-permute-start.14
  33.7 1.1 %image_own.1 = (f32[2,768,128]{2,1,0:T(8,128)S(1)}, bf16[2,768,256]{2,1,0:T(8,128)(2,1)S(1)}, f32[2,1,768,128]{3,2,1,0:T(8,128)}) custom-call(bf16[2,1,1024,768]{3,2,1,0:T(8,128)(2,1)S(1)} %copy-done, bf16[2,768,128]{2,1,0:T(8,128)(2,1)S(1)} %get-tuple-element.62.low_ref, f32[2,1,768,128]{3,2,1,0:T(8,128)S(1)} %copy-done.1, ...), custom_call_target="tpu_custom_call" | custom-call | flops 1000000000 | bytes 1048576 | tf_op jit(solution)/shard_map/image_own/pallas_call | solution.py:388
  34.8 1.1 %collective-permute-done.13.yp_ref = bf16[128,128]{1,0:T(8,128)(2,1)S(1)} collective-permute-done((bf16[128,128]{1,0:T(8,128)(2,1)S(1)}, bf16[128,128]{1,0:T(8,128)(2,1)S(1)}, u32[]{:S(2)}, u32[]{:S(2)}) %collective-permute-start.13) | collective-permute-done | bytes 32800 | tf_op jit(solution)/shard_map/ppermute | solution.py:29
  35.9 2.2 %collective-permute-done.14.yo_ref = bf16[128,128]{1,0:T(8,128)(2,1)S(1)} collective-permute-done((bf16[128,128]{1,0:T(8,128)(2,1)S(1)}, bf16[128,128]{1,0:T(8,128)(2,1)S(1)}, u32[]{:S(2)}, u32[]{:S(2)}) %collective-permute-start.14) | collective-permute-done | bytes 32800 | tf_op jit(solution)/shard_map/ppermute | solution.py:45
  38.1 1.2 %residual.1 = f32[2,1,768,128]{3,2,1,0:T(8,128)} custom-call(f32[2,768,128]{2,1,0:T(8,128)S(1)} %get-tuple-element.65.part_ref, bf16[2,256,128]{2,1,0:T(8,128)(2,1)S(1)} %get-tuple-element.66.image_ref, bf16[2,768,256]{2,1,0:T(8,128)(2,1)S(1)} %get-tuple-element.67.pick_ref, bf16[64,128]{1,0:T(8,128)(2,1)S(1)} %collective-permute-done.11.xp_ref, ...), custom_call_target="tpu_custom_call" | custom-call | flops 1000000000 | bytes 1048576 | tf_op jit(solution)/shard_map/residual/pallas_call | solution.py:388
  (26 shorter events, 0.3 us)
Async XLA Ops:
  0.6 2.1 %copy-start.5 = (bf16[32,1024]{1,0:T(8,128)(2,1)S(1)}, bf16[32,1024]{1,0:T(8,128)(2,1)}, u32[]{:S(2)}) copy-start(bf16[32,1024]{1,0:T(8,128)(2,1)} %near_ref.1) | copy-start | bytes 196612
  0.6 6.2 %copy-start.3 = (bf16[2,1,1024,768]{3,2,1,0:T(8,128)(2,1)S(1)}, bf16[2,1,1024,768]{3,2,1,0:T(8,128)(2,1)}, u32[]{:S(2)}) copy-start(bf16[2,1,1024,768]{3,2,1,0:T(8,128)(2,1)} %inverse_ref.1) | copy-start | bytes 9437188
  2.7 2.7 %collective-permute-start = (bf16[528,128]{1,0:T(8,128)(2,1)S(1)}, bf16[528,128]{1,0:T(8,128)(2,1)S(1)}, u32[]{:S(2)}, u32[]{:S(2)}) collective-permute-start(bf16[528,128]{1,0:T(8,128)(2,1)S(1)} %get-tuple-element.39.sent_ref.rest_0_.rest_1_), channel_id=1, source_target_pairs={{0,8},{8,0},{16,24},{24,16},{1,9},{9,1},{17,25},{25,17},{2,10},{10... | collective-permute-start | bytes 405512 | tf_op jit(solution)/shard_map/ppermute | solution.py:29
  2.8 8.6 %collective-permute-start.1 = (bf16[32,1024]{1,0:T(8,128)(2,1)S(1)}, bf16[32,1024]{1,0:T(8,128)(2,1)S(1)}, u32[]{:S(2)}, u32[]{:S(2)}) collective-permute-start(bf16[32,1024]{1,0:T(8,128)(2,1)S(1)} %copy-done.5), channel_id=1, source_target_pairs={{0,4},{1,5},{2,6},{3,7},{4,0},{5,1},{6,2},{7,3},{8,12},{9,13},{10,... | collective-permute-start | bytes 196616 | tf_op jit(solution)/shard_map/ppermute | solution.py:29
  5.5 4.3 %collective-permute-start.3 = (bf16[288,128]{1,0:T(8,128)(2,1)S(1)}, bf16[288,128]{1,0:T(8,128)(2,1)S(1)}, u32[]{:S(2)}, u32[]{:S(2)}) collective-permute-start(bf16[288,128]{1,0:T(8,128)(2,1)S(1)} %get-tuple-element.40.token_ref), channel_id=1, source_target_pairs={{0,24},{8,16},{16,8},{24,0},{1,25},{9,17},{17,9},{25,1},{2,26},{10... | collective-permute-start | bytes 221192 | tf_op jit(solution)/shard_map/ppermute | solution.py:29
  9.8 4.4 %collective-permute-start.4 = (bf16[272,128]{1,0:T(8,128)(2,1)S(1)}, bf16[272,128]{1,0:T(8,128)(2,1)S(1)}, u32[]{:S(2)}, u32[]{:S(2)}) collective-permute-start(bf16[272,128]{1,0:T(8,128)(2,1)S(1)} %get-tuple-element.43), channel_id=1, source_target_pairs={{0,1},{1,0},{2,3},{3,2},{4,5},{5,4},{6,7},{7,6},{8,9},{9,8},{10,11... | collective-permute-start | bytes 208904 | tf_op jit(solution)/shard_map/ppermute | solution.py:29
  11.4 6.1 %collective-permute-start.2 = (bf16[64,1024]{1,0:T(8,128)(2,1)S(1)}, bf16[64,1024]{1,0:T(8,128)(2,1)S(1)}, u32[]{:S(2)}, u32[]{:S(2)}) collective-permute-start(bf16[64,1024]{1,0:T(8,128)(2,1)S(1)} %inverse_join.2.near_ref), channel_id=1, source_target_pairs={{0,2},{1,3},{2,0},{3,1},{4,6},{5,7},{6,4},{7,5},{8,10},{9,11},{10,... | collective-permute-start | bytes 393224 | tf_op jit(solution)/shard_map/ppermute | solution.py:29
  14.2 4.3 %collective-permute-start.5 = (bf16[256,128]{1,0:T(8,128)(2,1)S(1)}, bf16[256,128]{1,0:T(8,128)(2,1)S(1)}, u32[]{:S(2)}, u32[]{:S(2)}) collective-permute-start(bf16[256,128]{1,0:T(8,128)(2,1)S(1)} %get-tuple-element.47), channel_id=1, source_target_pairs={{0,2},{1,3},{2,0},{3,1},{4,6},{5,7},{6,4},{7,5},{8,10},{9,11},{10,... | collective-permute-start | bytes 196616 | tf_op jit(solution)/shard_map/ppermute | solution.py:29
  18.0 5.8 %collective-permute-start.6 = (bf16[640,128]{1,0:T(8,128)(2,1)S(1)}, bf16[640,128]{1,0:T(8,128)(2,1)S(1)}, u32[]{:S(2)}, u32[]{:S(2)}) collective-permute-start(bf16[640,128]{1,0:T(8,128)(2,1)S(1)} %inverse_pick.3), channel_id=1, source_target_pairs={{0,1},{1,0},{2,3},{3,2},{4,5},{5,4},{6,7},{7,6},{8,9},{9,8},{10,11... | collective-permute-start | bytes 491528 | tf_op jit(solution)/shard_map/ppermute | solution.py:29
  18.5 5.2 %collective-permute-start.7 = (bf16[256,128]{1,0:T(8,128)(2,1)S(1)}, bf16[256,128]{1,0:T(8,128)(2,1)S(1)}, u32[]{:S(2)}, u32[]{:S(2)}) collective-permute-start(bf16[256,128]{1,0:T(8,128)(2,1)S(1)} %get-tuple-element.49.token_ref), channel_id=1, source_target_pairs={{0,4},{1,5},{2,6},{3,7},{4,0},{5,1},{6,2},{7,3},{8,12},{9,13},{10,... | collective-permute-start | bytes 196616 | tf_op jit(solution)/shard_map/ppermute | solution.py:29
  23.8 3.2 %copy-start.2 = (s32[2,1,4,64]{3,2,1,0:T(4,128)S(1)}, s32[2,1,4,64]{3,2,1,0:T(4,128)}, u32[]{:S(2)}) copy-start(s32[2,1,4,64]{3,2,1,0:T(4,128)} %spill_ref.3) | copy-start | bytes 6148
  23.8 3.2 %copy-start.4 = (bf16[2,1,64,768]{3,2,1,0:T(8,128)(2,1)S(1)}, bf16[2,1,64,768]{3,2,1,0:T(8,128)(2,1)}, u32[]{:S(2)}) copy-start(bf16[2,1,64,768]{3,2,1,0:T(8,128)(2,1)} %basis_ref.1) | copy-start | bytes 589828
  24.0 1.6 %collective-permute-start.8 = (bf16[320,128]{1,0:T(8,128)(2,1)S(1)}, bf16[320,128]{1,0:T(8,128)(2,1)S(1)}, u32[]{:S(2)}, u32[]{:S(2)}) collective-permute-start(bf16[320,128]{1,0:T(8,128)(2,1)S(1)} %get-tuple-element.54), channel_id=1, source_target_pairs={{0,8},{8,0},{16,24},{24,16},{1,9},{9,1},{17,25},{25,17},{2,10},{10... | collective-permute-start | bytes 245768 | tf_op jit(solution)/shard_map/ppermute | solution.py:29
  24.1 4.9 %collective-permute-start.9 = (bf16[128,128]{1,0:T(8,128)(2,1)S(1)}, bf16[128,128]{1,0:T(8,128)(2,1)S(1)}, u32[]{:S(2)}, u32[]{:S(2)}) collective-permute-start(bf16[128,128]{1,0:T(8,128)(2,1)S(1)} %get-tuple-element.60), channel_id=1, source_target_pairs={{0,8},{1,2},{2,1},{3,4},{4,3},{5,6},{6,5},{7,15},{8,0},{9,10},{10,... | collective-permute-start | bytes 98312 | tf_op jit(solution)/shard_map/ppermute | solution.py:45
  25.6 3.8 %copy-start = (bf16[2,1,1024,768]{3,2,1,0:T(8,128)(2,1)S(1)}, bf16[2,1,1024,768]{3,2,1,0:T(8,128)(2,1)}, u32[]{:S(2)}) copy-start(bf16[2,1,1024,768]{3,2,1,0:T(8,128)(2,1)} %operator_ref.3) | copy-start | bytes 9437188
  25.6 3.8 %collective-permute-start.10 = (bf16[192,128]{1,0:T(8,128)(2,1)S(1)}, bf16[192,128]{1,0:T(8,128)(2,1)S(1)}, u32[]{:S(2)}, u32[]{:S(2)}) collective-permute-start(bf16[192,128]{1,0:T(8,128)(2,1)S(1)} %get-tuple-element.56.token_ref), channel_id=1, source_target_pairs={{0,24},{8,16},{16,8},{24,0},{1,25},{9,17},{17,9},{25,1},{2,26},{10... | collective-permute-start | bytes 147464 | tf_op jit(solution)/shard_map/ppermute | solution.py:29
  27.5 6.2 %copy-start.1 = (f32[2,1,768,128]{3,2,1,0:T(8,128)S(1)}, f32[2,1,768,128]{3,2,1,0:T(8,128)}, u32[]{:S(2)}) copy-start(f32[2,1,768,128]{3,2,1,0:T(8,128)} %rhs_ref.1) | copy-start | bytes 2359300
  30.3 4.5 %collective-permute-start.11 = (bf16[64,128]{1,0:T(8,128)(2,1)S(1)}, bf16[64,128]{1,0:T(8,128)(2,1)S(1)}, u32[]{:S(2)}, u32[]{:S(2)}) collective-permute-start(bf16[64,128]{1,0:T(8,128)(2,1)S(1)} %get-tuple-element.68), channel_id=1, source_target_pairs={{0,8},{8,0},{16,24},{24,16},{1,9},{9,1},{17,25},{25,17},{2,10},{10... | collective-permute-start | bytes 49160 | tf_op jit(solution)/shard_map/ppermute | solution.py:29
  30.5 4.3 %collective-permute-start.12 = (bf16[64,128]{1,0:T(8,128)(2,1)S(1)}, bf16[64,128]{1,0:T(8,128)(2,1)S(1)}, u32[]{:S(2)}, u32[]{:S(2)}) collective-permute-start(bf16[64,128]{1,0:T(8,128)(2,1)S(1)} %get-tuple-element.69), channel_id=1, source_target_pairs={{0,24},{1,25},{2,26},{3,27},{4,28},{5,29},{6,30},{7,31},{8,16},{9,... | collective-permute-start | bytes 49160 | tf_op jit(solution)/shard_map/ppermute | solution.py:45
  32.0 3.9 %collective-permute-start.13 = (bf16[128,128]{1,0:T(8,128)(2,1)S(1)}, bf16[128,128]{1,0:T(8,128)(2,1)S(1)}, u32[]{:S(2)}, u32[]{:S(2)}) collective-permute-start(bf16[128,128]{1,0:T(8,128)(2,1)S(1)} %get-tuple-element.70), channel_id=1, source_target_pairs={{0,1},{1,0},{2,3},{3,2},{4,5},{5,4},{6,7},{7,6},{8,9},{9,8},{10,11... | collective-permute-start | bytes 98312 | tf_op jit(solution)/shard_map/ppermute | solution.py:29
  33.3 4.8 %collective-permute-start.14 = (bf16[128,128]{1,0:T(8,128)(2,1)S(1)}, bf16[128,128]{1,0:T(8,128)(2,1)S(1)}, u32[]{:S(2)}, u32[]{:S(2)}) collective-permute-start(bf16[128,128]{1,0:T(8,128)(2,1)S(1)} %get-tuple-element.71), channel_id=1, source_target_pairs={{0,8},{1,2},{2,1},{3,4},{4,3},{5,6},{6,5},{7,15},{8,0},{9,10},{10,... | collective-permute-start | bytes 98312 | tf_op jit(solution)/shard_map/ppermute | solution.py:45

commit v6 on v5

--- a/solution.py
+++ b/solution.py
@@ -48,10 +48,8 @@
 def relative_block(block, device, steps):
     left = block ^ device
     place = left * 0
-    for step in range(steps, 0, -1):
-        bit = (left >> (step - 1)) & 1
-        place = place | (bit << (steps - step))
-        left = left ^ (bit * mask_of(step))
+    for step in range(steps):
+        place = place | (((left >> step) & 1) << (steps - 1 - step))
     return place
 
 
@@ -443,13 +441,15 @@
             [keep, got, send],
             "coarse_halve",
         )
-        got = swap(send, "gx", mask_of(step))
+        got = swap(send, "gx", 1 << (step - 1))
         size = half
     id_places = id_places + [(got, size + 16 * i, 0) for i in range(len(id_places))]
 
     holders, places = [got], []
     for q in range(count_x):
-        p = sum(((q >> (steps_x - k)) & 1) << (k - 1) for k in range(1, steps_x + 1))
+        p = 0
+        for k in range(1, steps_x + 1):
+            p ^= ((q >> (steps_x - k)) & 1) * mask_of(k)
         array, start, _ = id_places[p]
         found = [i for i, holder in enumerate(holders) if holder is array]
         if not found:
@@ -556,6 +556,7 @@
         [(block, F32), ((subs, rows, 4 * margin), BF16), (adjoint_rhs.shape, F32)],
         [local_operator, low, adjoint_rhs, correction, spill_rows],
         "image_own",
+        cost=1,
         out_specs=[VMEM, VMEM, HBM],
         scratch=[dma((subs,))],
         limit=12,

time: 39.5 us -> 38.6 us (0.977)
  the two profiles are of different devices: /device:TPU:8 before, /device:TPU:0 now
where the time goes in v6:
time: 38.6 us; the launch traced here: 38.4 us
  starting transfers between devices  18.1 us (47%)
  waiting for transfers between devices  11.4 us (30%)
  Pallas kernels  8.13 us (21%)
  between operations  0.76 us (2%)
    ppermute x12, starting transfers between devices, swap(): return lax.ppermute(value, axis, [(i, i ^ mask) for i in range(count)])  16.4 us
    ppermute x12, waiting for transfers between devices, swap(): return lax.ppermute(value, axis, [(i, i ^ mask) for i in range(count)])  10.5 us
    pallas_call x16, Pallas kernels, call(): pl.pallas_call(kernel, out_shape=[jax.ShapeDtypeStruct(shape, dtype) for...  8.13 us
    ppermute x3, starting transfers between devices, other(): return lax.ppermute(value, ('gx', 'gy'), pairs)  1.63 us
    ppermute x3, waiting for transfers between devices, other(): return lax.ppermute(value, ('gx', 'gy'), pairs)  0.95 us
  transfers between devices with their start and end apart: 15, of which 8 were waited for; matrix products, arithmetic and copies ran while one was open for 0% of the time, Pallas kernels for 10%

profile of v6, /device:TPU:0, one launch (start us, length us, event | category | flops | bytes accessed | tf_op | source)
XLA Modules:
  0.0 38.4 jit_solution(7044039362593135182)
XLA Ops:
  0.7 2.0 %coarse_terms.1 = (f32[512,128]{1,0:T(8,128)S(1)}, bf16[528,128]{1,0:T(8,128)(2,1)S(1)}, bf16[2,768,128]{2,1,0:T(8,128)(2,1)S(1)}) custom-call(f32[2,1,768,128]{3,2,1,0:T(8,128)} %rhs_ref.1, bf16[2,1,64,768]{3,2,1,0:T(8,128)(2,1)} %basis_ref.1, s32[2,1,64]{2,1,0:T(1,128)} %ids_hbm.1), custom_call_target="tpu_custom_call" | custom-call | flops 1000000000 | bytes 1048576 | tf_op jit(solution)/shard_map/coarse_terms/pallas_call | solution.py:386
  2.7 0.5 %collective-permute-start = (bf16[528,128]{1,0:T(8,128)(2,1)S(1)}, bf16[528,128]{1,0:T(8,128)(2,1)S(1)}, u32[]{:S(2)}, u32[]{:S(2)}) collective-permute-start(bf16[528,128]{1,0:T(8,128)(2,1)S(1)} %get-tuple-element.39.sent_ref.rest_0_.rest_1_), channel_id=1, source_target_pairs={{0,8},{8,0},{16,24},{24,16},{1,9},{9,1},{17,25},{25,17},{2,10},{10... | collective-permute-start | bytes 405512 | tf_op jit(solution)/shard_map/ppermute | solution.py:29
  3.2 3.7 %collective-permute-start.1 = (bf16[32,1024]{1,0:T(8,128)(2,1)S(1)}, bf16[32,1024]{1,0:T(8,128)(2,1)S(1)}, u32[]{:S(2)}, u32[]{:S(2)}) collective-permute-start(bf16[32,1024]{1,0:T(8,128)(2,1)S(1)} %copy-done.5), channel_id=1, source_target_pairs={{0,4},{1,5},{2,6},{3,7},{4,0},{5,1},{6,2},{7,3},{8,12},{9,13},{10,... | collective-permute-start | bytes 196616 | tf_op jit(solution)/shard_map/ppermute | solution.py:29
  6.9 1.6 %collective-permute-start.3 = (bf16[288,128]{1,0:T(8,128)(2,1)S(1)}, bf16[288,128]{1,0:T(8,128)(2,1)S(1)}, u32[]{:S(2)}, u32[]{:S(2)}) collective-permute-start(bf16[288,128]{1,0:T(8,128)(2,1)S(1)} %get-tuple-element.40.token_ref), channel_id=1, source_target_pairs={{0,16},{8,24},{16,0},{24,8},{1,17},{9,25},{17,1},{25,9},{2,18},{10... | collective-permute-start | bytes 221192 | tf_op jit(solution)/shard_map/ppermute | solution.py:29
  8.5 1.0 %local_solve.1 = (f32[2,768,128]{2,1,0:T(8,128)S(1)}, bf16[2,256,128]{2,1,0:T(8,128)(2,1)S(1)}, bf16[64,128]{1,0:T(8,128)(2,1)S(1)}, bf16[64,128]{1,0:T(8,128)(2...) custom-call(bf16[2,1,1024,768]{3,2,1,0:T(8,128)(2,1)S(1)} %copy-done.3, ...), custom_call_target="tpu_custom_call" | custom-call | flops 1000000000 | bytes 1048576 | tf_op jit(solution)/shard_map/local_solve/pallas_call | solution.py:386
  9.5 1.8 %collective-permute-done.3.got_ref.rest_0_ = bf16[288,128]{1,0:T(8,128)(2,1)S(1)} collective-permute-done((bf16[288,128]{1,0:T(8,128)(2,1)S(1)}, bf16[288,128]{1,0:T(8,128)(2,1)S(1)}, u32[]{:S(2)}, u32[]{:S(2)}) %collective-permute-start.3) | collective-permute-done | bytes 73760 | tf_op jit(solution)/shard_map/ppermute | solution.py:29
  11.4 1.6 %collective-permute-start.4 = (bf16[272,128]{1,0:T(8,128)(2,1)S(1)}, bf16[272,128]{1,0:T(8,128)(2,1)S(1)}, u32[]{:S(2)}, u32[]{:S(2)}) collective-permute-start(bf16[272,128]{1,0:T(8,128)(2,1)S(1)} %get-tuple-element.43), channel_id=1, source_target_pairs={{0,1},{1,0},{2,3},{3,2},{4,5},{5,4},{6,7},{7,6},{8,9},{9,8},{10,11... | collective-permute-start | bytes 208904 | tf_op jit(solution)/shard_map/ppermute | solution.py:29
  12.9 1.6 %collective-permute-start.2 = (bf16[64,1024]{1,0:T(8,128)(2,1)S(1)}, bf16[64,1024]{1,0:T(8,128)(2,1)S(1)}, u32[]{:S(2)}, u32[]{:S(2)}) collective-permute-start(bf16[64,1024]{1,0:T(8,128)(2,1)S(1)} %inverse_join.2.near_ref), channel_id=1, source_target_pairs={{0,2},{1,3},{2,0},{3,1},{4,6},{5,7},{6,4},{7,5},{8,10},{9,11},{10,... | collective-permute-start | bytes 393224 | tf_op jit(solution)/shard_map/ppermute | solution.py:29
  14.6 1.2 %collective-permute-done.4.token_ref.got_ref.rest_0_ = bf16[272,128]{1,0:T(8,128)(2,1)S(1)} collective-permute-done((bf16[272,128]{1,0:T(8,128)(2,1)S(1)}, bf16[272,128]{1,0:T(8,128)(2,1)S(1)}, u32[]{:S(2)}, u32[]{:S(2)}) %collective-permute-start.4) | collective-permute-done | bytes 69664 | tf_op jit(solution)/shard_map/ppermute | solution.py:29
  15.8 1.6 %collective-permute-start.5 = (bf16[256,128]{1,0:T(8,128)(2,1)S(1)}, bf16[256,128]{1,0:T(8,128)(2,1)S(1)}, u32[]{:S(2)}, u32[]{:S(2)}) collective-permute-start(bf16[256,128]{1,0:T(8,128)(2,1)S(1)} %get-tuple-element.47), channel_id=1, source_target_pairs={{0,2},{1,3},{2,0},{3,1},{4,6},{5,7},{6,4},{7,5},{8,10},{9,11},{10,... | collective-permute-start | bytes 196616 | tf_op jit(solution)/shard_map/ppermute | solution.py:29
  17.4 1.3 %collective-permute-done.2.far_ref = bf16[64,1024]{1,0:T(8,128)(2,1)S(1)} collective-permute-done((bf16[64,1024]{1,0:T(8,128)(2,1)S(1)}, bf16[64,1024]{1,0:T(8,128)(2,1)S(1)}, u32[]{:S(2)}, u32[]{:S(2)}) %collective-permute-start.2) | collective-permute-done | bytes 131104 | tf_op jit(solution)/shard_map/ppermute | solution.py:29
  18.7 0.5 %inverse_pick.3 = bf16[640,128]{1,0:T(8,128)(2,1)S(1)} custom-call(bf16[128,1024]{1,0:T(8,128)(2,1)S(1)} %inverse_join.3.rows_ref, bf16[272,128]{1,0:T(8,128)(2,1)S(1)} %collective-permute-done.4.token_ref.got_ref.rest_0_, bf16[272,128]{1,0:T(8,128)(2,1)S(1)} %collective-permute-done.4.token_ref.got_ref.rest_0_, bf16[128,128]{1,0:T(8,128)(2,1)S(1)} %get-tuple-element.50.rest_1_), custom_call_target="tpu_custom_call" | custom-call | flops 1000000000 | bytes 1048576 | tf_op jit(solution)/shard_map/inverse_pick/pallas_call | solution.py:386
  19.2 0.3 collective-permute-start.6
  19.6 0.5 %collective-permute-done.5.got_ref = bf16[256,128]{1,0:T(8,128)(2,1)S(1)} collective-permute-done((bf16[256,128]{1,0:T(8,128)(2,1)S(1)}, bf16[256,128]{1,0:T(8,128)(2,1)S(1)}, u32[]{:S(2)}, u32[]{:S(2)}) %collective-permute-start.5) | collective-permute-done | bytes 65568 | tf_op jit(solution)/shard_map/ppermute | solution.py:29
  20.1 1.6 %collective-permute-start.7 = (bf16[256,128]{1,0:T(8,128)(2,1)S(1)}, bf16[256,128]{1,0:T(8,128)(2,1)S(1)}, u32[]{:S(2)}, u32[]{:S(2)}) collective-permute-start(bf16[256,128]{1,0:T(8,128)(2,1)S(1)} %get-tuple-element.49.token_ref), channel_id=1, source_target_pairs={{0,4},{1,5},{2,6},{3,7},{4,0},{5,1},{6,2},{7,3},{8,12},{9,13},{10,... | collective-permute-start | bytes 196616 | tf_op jit(solution)/shard_map/ppermute | solution.py:29
  21.8 0.5 %inverse_pick.2.near_ref = bf16[512,128]{1,0:T(8,128)(2,1)S(1)} custom-call(bf16[128,1024]{1,0:T(8,128)(2,1)S(1)} %inverse_join.3.rows_ref, bf16[256,128]{1,0:T(8,128)(2,1)S(1)} %get-tuple-element.49.token_ref, bf16[288,128]{1,0:T(8,128)(2,1)S(1)} %collective-permute-done.3.got_ref.rest_0_, bf16[528,128]{1,0:T(8,128)(2,1)S(1)} %get-tuple-element.39.sent_ref.rest_0_.rest_1_, ...), custom_call_target="tpu_custom_call" | custom-call | flops 1000000000 | bytes 1048576 | tf_op jit(solution)/shard_map/inverse_pick/pallas_call | solution.py:386
  22.3 3.1 %collective-permute-done.7.got_ref = bf16[256,128]{1,0:T(8,128)(2,1)S(1)} collective-permute-done((bf16[256,128]{1,0:T(8,128)(2,1)S(1)}, bf16[256,128]{1,0:T(8,128)(2,1)S(1)}, u32[]{:S(2)}, u32[]{:S(2)}) %collective-permute-start.7) | collective-permute-done | bytes 65568 | tf_op jit(solution)/shard_map/ppermute | solution.py:29
  25.4 0.2 coarse_solve.1
  25.6 0.1 collective-permute-start.8
  25.7 0.5 %collective-permute-start.9 = (bf16[128,128]{1,0:T(8,128)(2,1)S(1)}, bf16[128,128]{1,0:T(8,128)(2,1)S(1)}, u32[]{:S(2)}, u32[]{:S(2)}) collective-permute-start(bf16[128,128]{1,0:T(8,128)(2,1)S(1)} %get-tuple-element.60), channel_id=1, source_target_pairs={{0,8},{1,2},{2,1},{3,4},{4,3},{5,6},{6,5},{7,15},{8,0},{9,10},{10,... | collective-permute-start | bytes 98312 | tf_op jit(solution)/shard_map/ppermute | solution.py:45
  26.2 0.8 %collective-permute-done.8.got_ref.rest_0_ = bf16[320,128]{1,0:T(8,128)(2,1)S(1)} collective-permute-done((bf16[320,128]{1,0:T(8,128)(2,1)S(1)}, bf16[320,128]{1,0:T(8,128)(2,1)S(1)}, u32[]{:S(2)}, u32[]{:S(2)}) %collective-permute-start.8) | collective-permute-done | bytes 81952 | tf_op jit(solution)/shard_map/ppermute | solution.py:29
  27.0 1.3 %collective-permute-start.10 = (bf16[192,128]{1,0:T(8,128)(2,1)S(1)}, bf16[192,128]{1,0:T(8,128)(2,1)S(1)}, u32[]{:S(2)}, u32[]{:S(2)}) collective-permute-start(bf16[192,128]{1,0:T(8,128)(2,1)S(1)} %get-tuple-element.56.token_ref), channel_id=1, source_target_pairs={{0,24},{8,16},{16,8},{24,0},{1,25},{9,17},{17,9},{25,1},{2,26},{10... | collective-permute-start | bytes 147464 | tf_op jit(solution)/shard_map/ppermute | solution.py:29
  28.3 0.5 %local_spread.1 = (f32[2,768,128]{2,1,0:T(8,128)S(1)}, bf16[2,768,320]{2,1,0:T(8,128)(2,1)S(1)}) custom-call(f32[2,768,128]{2,1,0:T(8,128)S(1)} %get-tuple-element.41.token_ref.own_ref, s32[2,1,4,64]{3,2,1,0:T(4,128)S(1)} %copy-done.2, bf16[2,1,64,768]{3,2,1,0:T(8,128)(2,1)S(1)} %copy-done.4, bf16[192,128]{1,0:T(8,128)(2,1)S(1)} %get-tuple-element.56.token_ref, ...), custom_call_target="tpu_custom_call" | custom-call | flops 1000000000 | bytes 1048576 | tf_op jit(solution)/shard_map/local_spread/pallas_call | solution.py:386
  28.9 0.0 copy-start.1
  28.9 1.8 %collective-permute-done.10.rest_1_ = bf16[192,128]{1,0:T(8,128)(2,1)S(1)} collective-permute-done((bf16[192,128]{1,0:T(8,128)(2,1)S(1)}, bf16[192,128]{1,0:T(8,128)(2,1)S(1)}, u32[]{:S(2)}, u32[]{:S(2)}) %collective-permute-start.10) | collective-permute-done | bytes 49184 | tf_op jit(solution)/shard_map/ppermute | solution.py:29
  30.7 0.9 %correction.1 = (f32[2,768,128]{2,1,0:T(8,128)S(1)}, bf16[2,768,128]{2,1,0:T(8,128)(2,1)S(1)}, bf16[2,256,128]{2,1,0:T(8,128)(2,1)S(1)}, bf16[64,128]{1,0:T(8,12...) custom-call(f32[2,768,128]{2,1,0:T(8,128)S(1)} %get-tuple-element.57.local_ref,, ...), custom_call_target="tpu_custom_call" | custom-call | flops 1000000000 | bytes 1048576 | tf_op jit(solution)/shard_map/correction/pallas_call | solution.py:386
  31.6 1.9 %collective-permute-start.13 = (bf16[128,128]{1,0:T(8,128)(2,1)S(1)}, bf16[128,128]{1,0:T(8,128)(2,1)S(1)}, u32[]{:S(2)}, u32[]{:S(2)}) collective-permute-start(bf16[128,128]{1,0:T(8,128)(2,1)S(1)} %get-tuple-element.70), channel_id=1, source_target_pairs={{0,1},{1,0},{2,3},{3,2},{4,5},{5,4},{6,7},{7,6},{8,9},{9,8},{10,11... | collective-permute-start | bytes 98312 | tf_op jit(solution)/shard_map/ppermute | solution.py:29
  33.5 0.5 %collective-permute-start.11 = (bf16[64,128]{1,0:T(8,128)(2,1)S(1)}, bf16[64,128]{1,0:T(8,128)(2,1)S(1)}, u32[]{:S(2)}, u32[]{:S(2)}) collective-permute-start(bf16[64,128]{1,0:T(8,128)(2,1)S(1)} %get-tuple-element.68), channel_id=1, source_target_pairs={{0,8},{8,0},{16,24},{24,16},{1,9},{9,1},{17,25},{25,17},{2,10},{10... | collective-permute-start | bytes 49160 | tf_op jit(solution)/shard_map/ppermute | solution.py:29
  34.1 1.1 %collective-permute-start.12 = (bf16[64,128]{1,0:T(8,128)(2,1)S(1)}, bf16[64,128]{1,0:T(8,128)(2,1)S(1)}, u32[]{:S(2)}, u32[]{:S(2)}) collective-permute-start(bf16[64,128]{1,0:T(8,128)(2,1)S(1)} %get-tuple-element.69), channel_id=1, source_target_pairs={{0,24},{1,25},{2,26},{3,27},{4,28},{5,29},{6,30},{7,31},{8,16},{9,... | collective-permute-start | bytes 49160 | tf_op jit(solution)/shard_map/ppermute | solution.py:45
  35.2 1.1 %image_own.1 = (f32[2,768,128]{2,1,0:T(8,128)S(1)}, bf16[2,768,256]{2,1,0:T(8,128)(2,1)S(1)}, f32[2,1,768,128]{3,2,1,0:T(8,128)}) custom-call(bf16[2,1,1024,768]{3,2,1,0:T(8,128)(2,1)S(1)} %copy-done, bf16[2,768,128]{2,1,0:T(8,128)(2,1)S(1)} %get-tuple-element.62.low_ref, f32[2,1,768,128]{3,2,1,0:T(8,128)S(1)} %copy-done.1, ...), custom_call_target="tpu_custom_call" | custom-call | flops 1 | bytes 1048576 | tf_op jit(solution)/shard_map/image_own/pallas_call | solution.py:386
  36.3 0.9 %collective-permute-done.12.xo_ref = bf16[64,128]{1,0:T(8,128)(2,1)S(1)} collective-permute-done((bf16[64,128]{1,0:T(8,128)(2,1)S(1)}, bf16[64,128]{1,0:T(8,128)(2,1)S(1)}, u32[]{:S(2)}, u32[]{:S(2)}) %collective-permute-start.12) | collective-permute-done | bytes 16416 | tf_op jit(solution)/shard_map/ppermute | solution.py:45
  37.2 1.2 %residual.1 = f32[2,1,768,128]{3,2,1,0:T(8,128)} custom-call(f32[2,768,128]{2,1,0:T(8,128)S(1)} %get-tuple-element.65.part_ref, bf16[2,256,128]{2,1,0:T(8,128)(2,1)S(1)} %get-tuple-element.66.image_ref, bf16[2,768,256]{2,1,0:T(8,128)(2,1)S(1)} %get-tuple-element.67.pick_ref, bf16[64,128]{1,0:T(8,128)(2,1)S(1)} %collective-permute-done.11.xp_ref, ...), custom_call_target="tpu_custom_call" | custom-call | flops 1000000000 | bytes 1048576 | tf_op jit(solution)/shard_map/residual/pallas_call | solution.py:386
  (26 shorter events, 0.2 us)
Async XLA Ops:
  0.6 2.6 %copy-start.5 = (bf16[32,1024]{1,0:T(8,128)(2,1)S(1)}, bf16[32,1024]{1,0:T(8,128)(2,1)}, u32[]{:S(2)}) copy-start(bf16[32,1024]{1,0:T(8,128)(2,1)} %near_ref.1) | copy-start | bytes 196612
  0.6 7.9 %copy-start.3 = (bf16[2,1,1024,768]{3,2,1,0:T(8,128)(2,1)S(1)}, bf16[2,1,1024,768]{3,2,1,0:T(8,128)(2,1)}, u32[]{:S(2)}) copy-start(bf16[2,1,1024,768]{3,2,1,0:T(8,128)(2,1)} %inverse_ref.1) | copy-start | bytes 9437188
  2.7 4.2 %collective-permute-start = (bf16[528,128]{1,0:T(8,128)(2,1)S(1)}, bf16[528,128]{1,0:T(8,128)(2,1)S(1)}, u32[]{:S(2)}, u32[]{:S(2)}) collective-permute-start(bf16[528,128]{1,0:T(8,128)(2,1)S(1)} %get-tuple-element.39.sent_ref.rest_0_.rest_1_), channel_id=1, source_target_pairs={{0,8},{8,0},{16,24},{24,16},{1,9},{9,1},{17,25},{25,17},{2,10},{10... | collective-permute-start | bytes 405512 | tf_op jit(solution)/shard_map/ppermute | solution.py:29
  3.2 9.7 %collective-permute-start.1 = (bf16[32,1024]{1,0:T(8,128)(2,1)S(1)}, bf16[32,1024]{1,0:T(8,128)(2,1)S(1)}, u32[]{:S(2)}, u32[]{:S(2)}) collective-permute-start(bf16[32,1024]{1,0:T(8,128)(2,1)S(1)} %copy-done.5), channel_id=1, source_target_pairs={{0,4},{1,5},{2,6},{3,7},{4,0},{5,1},{6,2},{7,3},{8,12},{9,13},{10,... | collective-permute-start | bytes 196616 | tf_op jit(solution)/shard_map/ppermute | solution.py:29
  6.9 4.4 %collective-permute-start.3 = (bf16[288,128]{1,0:T(8,128)(2,1)S(1)}, bf16[288,128]{1,0:T(8,128)(2,1)S(1)}, u32[]{:S(2)}, u32[]{:S(2)}) collective-permute-start(bf16[288,128]{1,0:T(8,128)(2,1)S(1)} %get-tuple-element.40.token_ref), channel_id=1, source_target_pairs={{0,16},{8,24},{16,0},{24,8},{1,17},{9,25},{17,1},{25,9},{2,18},{10... | collective-permute-start | bytes 221192 | tf_op jit(solution)/shard_map/ppermute | solution.py:29
  11.4 4.4 %collective-permute-start.4 = (bf16[272,128]{1,0:T(8,128)(2,1)S(1)}, bf16[272,128]{1,0:T(8,128)(2,1)S(1)}, u32[]{:S(2)}, u32[]{:S(2)}) collective-permute-start(bf16[272,128]{1,0:T(8,128)(2,1)S(1)} %get-tuple-element.43), channel_id=1, source_target_pairs={{0,1},{1,0},{2,3},{3,2},{4,5},{5,4},{6,7},{7,6},{8,9},{9,8},{10,11... | collective-permute-start | bytes 208904 | tf_op jit(solution)/shard_map/ppermute | solution.py:29
  12.9 5.7 %collective-permute-start.2 = (bf16[64,1024]{1,0:T(8,128)(2,1)S(1)}, bf16[64,1024]{1,0:T(8,128)(2,1)S(1)}, u32[]{:S(2)}, u32[]{:S(2)}) collective-permute-start(bf16[64,1024]{1,0:T(8,128)(2,1)S(1)} %inverse_join.2.near_ref), channel_id=1, source_target_pairs={{0,2},{1,3},{2,0},{3,1},{4,6},{5,7},{6,4},{7,5},{8,10},{9,11},{10,... | collective-permute-start | bytes 393224 | tf_op jit(solution)/shard_map/ppermute | solution.py:29
  15.8 4.3 %collective-permute-start.5 = (bf16[256,128]{1,0:T(8,128)(2,1)S(1)}, bf16[256,128]{1,0:T(8,128)(2,1)S(1)}, u32[]{:S(2)}, u32[]{:S(2)}) collective-permute-start(bf16[256,128]{1,0:T(8,128)(2,1)S(1)} %get-tuple-element.47), channel_id=1, source_target_pairs={{0,2},{1,3},{2,0},{3,1},{4,6},{5,7},{6,4},{7,5},{8,10},{9,11},{10,... | collective-permute-start | bytes 196616 | tf_op jit(solution)/shard_map/ppermute | solution.py:29
  19.2 6.1 %collective-permute-start.6 = (bf16[640,128]{1,0:T(8,128)(2,1)S(1)}, bf16[640,128]{1,0:T(8,128)(2,1)S(1)}, u32[]{:S(2)}, u32[]{:S(2)}) collective-permute-start(bf16[640,128]{1,0:T(8,128)(2,1)S(1)} %inverse_pick.3), channel_id=1, source_target_pairs={{0,1},{1,0},{2,3},{3,2},{4,5},{5,4},{6,7},{7,6},{8,9},{9,8},{10,11... | collective-permute-start | bytes 491528 | tf_op jit(solution)/shard_map/ppermute | solution.py:29
  20.1 5.2 %collective-permute-start.7 = (bf16[256,128]{1,0:T(8,128)(2,1)S(1)}, bf16[256,128]{1,0:T(8,128)(2,1)S(1)}, u32[]{:S(2)}, u32[]{:S(2)}) collective-permute-start(bf16[256,128]{1,0:T(8,128)(2,1)S(1)} %get-tuple-element.49.token_ref), channel_id=1, source_target_pairs={{0,4},{1,5},{2,6},{3,7},{4,0},{5,1},{6,2},{7,3},{8,12},{9,13},{10,... | collective-permute-start | bytes 196616 | tf_op jit(solution)/shard_map/ppermute | solution.py:29
  25.4 2.9 %copy-start.2 = (s32[2,1,4,64]{3,2,1,0:T(4,128)S(1)}, s32[2,1,4,64]{3,2,1,0:T(4,128)}, u32[]{:S(2)}) copy-start(s32[2,1,4,64]{3,2,1,0:T(4,128)} %spill_ref.3) | copy-start | bytes 6148
  25.4 2.9 %copy-start.4 = (bf16[2,1,64,768]{3,2,1,0:T(8,128)(2,1)S(1)}, bf16[2,1,64,768]{3,2,1,0:T(8,128)(2,1)}, u32[]{:S(2)}) copy-start(bf16[2,1,64,768]{3,2,1,0:T(8,128)(2,1)} %basis_ref.1) | copy-start | bytes 589828
  25.6 1.3 %collective-permute-start.8 = (bf16[320,128]{1,0:T(8,128)(2,1)S(1)}, bf16[320,128]{1,0:T(8,128)(2,1)S(1)}, u32[]{:S(2)}, u32[]{:S(2)}) collective-permute-start(bf16[320,128]{1,0:T(8,128)(2,1)S(1)} %get-tuple-element.54), channel_id=1, source_target_pairs={{0,8},{8,0},{16,24},{24,16},{1,9},{9,1},{17,25},{25,17},{2,10},{10... | collective-permute-start | bytes 245768 | tf_op jit(solution)/shard_map/ppermute | solution.py:29
  25.7 3.2 %collective-permute-start.9 = (bf16[128,128]{1,0:T(8,128)(2,1)S(1)}, bf16[128,128]{1,0:T(8,128)(2,1)S(1)}, u32[]{:S(2)}, u32[]{:S(2)}) collective-permute-start(bf16[128,128]{1,0:T(8,128)(2,1)S(1)} %get-tuple-element.60), channel_id=1, source_target_pairs={{0,8},{1,2},{2,1},{3,4},{4,3},{5,6},{6,5},{7,15},{8,0},{9,10},{10,... | collective-permute-start | bytes 98312 | tf_op jit(solution)/shard_map/ppermute | solution.py:45
  26.9 3.8 %copy-start = (bf16[2,1,1024,768]{3,2,1,0:T(8,128)(2,1)S(1)}, bf16[2,1,1024,768]{3,2,1,0:T(8,128)(2,1)}, u32[]{:S(2)}) copy-start(bf16[2,1,1024,768]{3,2,1,0:T(8,128)(2,1)} %operator_ref.3) | copy-start | bytes 9437188
  27.0 3.8 %collective-permute-start.10 = (bf16[192,128]{1,0:T(8,128)(2,1)S(1)}, bf16[192,128]{1,0:T(8,128)(2,1)S(1)}, u32[]{:S(2)}, u32[]{:S(2)}) collective-permute-start(bf16[192,128]{1,0:T(8,128)(2,1)S(1)} %get-tuple-element.56.token_ref), channel_id=1, source_target_pairs={{0,24},{8,16},{16,8},{24,0},{1,25},{9,17},{17,9},{25,1},{2,26},{10... | collective-permute-start | bytes 147464 | tf_op jit(solution)/shard_map/ppermute | solution.py:29
  28.9 6.3 %copy-start.1 = (f32[2,1,768,128]{3,2,1,0:T(8,128)S(1)}, f32[2,1,768,128]{3,2,1,0:T(8,128)}, u32[]{:S(2)}) copy-start(f32[2,1,768,128]{3,2,1,0:T(8,128)} %rhs_ref.1) | copy-start | bytes 2359300
  31.6 5.6 %collective-permute-start.13 = (bf16[128,128]{1,0:T(8,128)(2,1)S(1)}, bf16[128,128]{1,0:T(8,128)(2,1)S(1)}, u32[]{:S(2)}, u32[]{:S(2)}) collective-permute-start(bf16[128,128]{1,0:T(8,128)(2,1)S(1)} %get-tuple-element.70), channel_id=1, source_target_pairs={{0,1},{1,0},{2,3},{3,2},{4,5},{5,4},{6,7},{7,6},{8,9},{9,8},{10,11... | collective-permute-start | bytes 98312 | tf_op jit(solution)/shard_map/ppermute | solution.py:29
  33.5 3.7 %collective-permute-start.14 = (bf16[128,128]{1,0:T(8,128)(2,1)S(1)}, bf16[128,128]{1,0:T(8,128)(2,1)S(1)}, u32[]{:S(2)}, u32[]{:S(2)}) collective-permute-start(bf16[128,128]{1,0:T(8,128)(2,1)S(1)} %get-tuple-element.71), channel_id=1, source_target_pairs={{0,8},{1,2},{2,1},{3,4},{4,3},{5,6},{6,5},{7,15},{8,0},{9,10},{10,... | collective-permute-start | bytes 98312 | tf_op jit(solution)/shard_map/ppermute | solution.py:45
  33.5 2.7 %collective-permute-start.11 = (bf16[64,128]{1,0:T(8,128)(2,1)S(1)}, bf16[64,128]{1,0:T(8,128)(2,1)S(1)}, u32[]{:S(2)}, u32[]{:S(2)}) collective-permute-start(bf16[64,128]{1,0:T(8,128)(2,1)S(1)} %get-tuple-element.68), channel_id=1, source_target_pairs={{0,8},{8,0},{16,24},{24,16},{1,9},{9,1},{17,25},{25,17},{2,10},{10... | collective-permute-start | bytes 49160 | tf_op jit(solution)/shard_map/ppermute | solution.py:29
  34.1 3.2 %collective-permute-start.12 = (bf16[64,128]{1,0:T(8,128)(2,1)S(1)}, bf16[64,128]{1,0:T(8,128)(2,1)S(1)}, u32[]{:S(2)}, u32[]{:S(2)}) collective-permute-start(bf16[64,128]{1,0:T(8,128)(2,1)S(1)} %get-tuple-element.69), channel_id=1, source_target_pairs={{0,24},{1,25},{2,26},{3,27},{4,28},{5,29},{6,30},{7,31},{8,16},{9,... | collective-permute-start | bytes 49160 | tf_op jit(solution)/shard_map/ppermute | solution.py:45

commit v7 on v6

--- a/solution.py
+++ b/solution.py
@@ -501,21 +501,23 @@
     near = join(near, far, got)
     partner = [(0, size + 2 * q // 16 * 16, 2 * q % 16) for q in range(count_x)]
     far = swap(picked(near, got, partner, [got], halo_yp), "gy", gather_masks[-1])
-    for bit in range(1, steps_y):
+    last = 0
+    for bit in range(steps_y - 1, 0, -1):
         keep, send, halo_yo = call(
-            functools.partial(sum_kernel, bit - 1),
+            functools.partial(sum_kernel, last),
             [((size, width), F32), ((size, width), BF16), ((halo, width), BF16)],
             [keep, got, halo_yo],
             "coarse_sum",
         )
         got = swap(send, "gy", 1 << bit)
+        last = bit
     far_halo = other(halo_yo, "gy")
 
     near = picked(near, send, places, holders)
 
     half = count_x * listed // 2
     keep, send = call(
-        functools.partial(coarse_kernel, steps_y - 1),
+        functools.partial(coarse_kernel, last),
         [((half, width), F32), ((half + margin, width), BF16)],
         [near, far, keep, halo_xp, got],
         "coarse_solve",

time: 38.6 us -> 38.6 us (level)
  starting transfers between devices: 18.1 us -> 17.4 us
  waiting for transfers between devices: 11.4 us -> 12 us
    ppermute x12, starting transfers between devices: 16.4 us -> 15.8 us  [swap(): return lax.ppermute(value, axis, [(i, i ^ mask) for i in range(count)])]
    ppermute x12, waiting for transfers between devices: 10.5 us -> 11.1 us  [swap(): return lax.ppermute(value, axis, [(i, i ^ mask) for i in range(count)])]
where the time goes in v7:
time: 38.6 us; the launch traced here: 38.4 us
  starting transfers between devices  17.4 us (45%)
  waiting for transfers between devices  12 us (31%)
  Pallas kernels  8.14 us (21%)
  between operations  0.77 us (2%)
    ppermute x12, starting transfers between devices, swap(): return lax.ppermute(value, axis, [(i, i ^ mask) for i in range(count)])  15.8 us
    ppermute x12, waiting for transfers between devices, swap(): return lax.ppermute(value, axis, [(i, i ^ mask) for i in range(count)])  11.1 us
    pallas_call x16, Pallas kernels, call(): pl.pallas_call(kernel, out_shape=[jax.ShapeDtypeStruct(shape, dtype) for...  8.14 us
    ppermute x3, starting transfers between devices, other(): return lax.ppermute(value, ('gx', 'gy'), pairs)  1.63 us
    ppermute x3, waiting for transfers between devices, other(): return lax.ppermute(value, ('gx', 'gy'), pairs)  0.94 us
  transfers between devices with their start and end apart: 15, of which 8 were waited for; matrix products, arithmetic and copies ran while one was open for 0% of the time, Pallas kernels for 10%

profile of v7, /device:TPU:0, one launch (start us, length us, event | category | flops | bytes accessed | tf_op | source)
XLA Modules:
  0.0 38.4 jit_solution(5757104673871574536)
XLA Ops:
  0.7 2.0 %coarse_terms.1 = (f32[512,128]{1,0:T(8,128)S(1)}, bf16[528,128]{1,0:T(8,128)(2,1)S(1)}, bf16[2,768,128]{2,1,0:T(8,128)(2,1)S(1)}) custom-call(f32[2,1,768,128]{3,2,1,0:T(8,128)} %rhs_ref.1, bf16[2,1,64,768]{3,2,1,0:T(8,128)(2,1)} %basis_ref.1, s32[2,1,64]{2,1,0:T(1,128)} %ids_hbm.1), custom_call_target="tpu_custom_call" | custom-call | flops 1000000000 | bytes 1048576 | tf_op jit(solution)/shard_map/coarse_terms/pallas_call | solution.py:386
  2.7 0.5 %collective-permute-start = (bf16[528,128]{1,0:T(8,128)(2,1)S(1)}, bf16[528,128]{1,0:T(8,128)(2,1)S(1)}, u32[]{:S(2)}, u32[]{:S(2)}) collective-permute-start(bf16[528,128]{1,0:T(8,128)(2,1)S(1)} %get-tuple-element.39.sent_ref.rest_0_.rest_1_), channel_id=1, source_target_pairs={{0,8},{8,0},{16,24},{24,16},{1,9},{9,1},{17,25},{25,17},{2,10},{10... | collective-permute-start | bytes 405512 | tf_op jit(solution)/shard_map/ppermute | solution.py:29
  3.2 3.7 %collective-permute-start.1 = (bf16[32,1024]{1,0:T(8,128)(2,1)S(1)}, bf16[32,1024]{1,0:T(8,128)(2,1)S(1)}, u32[]{:S(2)}, u32[]{:S(2)}) collective-permute-start(bf16[32,1024]{1,0:T(8,128)(2,1)S(1)} %copy-done.5), channel_id=1, source_target_pairs={{0,4},{1,5},{2,6},{3,7},{4,0},{5,1},{6,2},{7,3},{8,12},{9,13},{10,... | collective-permute-start | bytes 196616 | tf_op jit(solution)/shard_map/ppermute | solution.py:29
  6.9 1.6 %collective-permute-start.3 = (bf16[288,128]{1,0:T(8,128)(2,1)S(1)}, bf16[288,128]{1,0:T(8,128)(2,1)S(1)}, u32[]{:S(2)}, u32[]{:S(2)}) collective-permute-start(bf16[288,128]{1,0:T(8,128)(2,1)S(1)} %get-tuple-element.40.token_ref), channel_id=1, source_target_pairs={{0,16},{8,24},{16,0},{24,8},{1,17},{9,25},{17,1},{25,9},{2,18},{10... | collective-permute-start | bytes 221192 | tf_op jit(solution)/shard_map/ppermute | solution.py:29
  8.5 1.0 %local_solve.1 = (f32[2,768,128]{2,1,0:T(8,128)S(1)}, bf16[2,256,128]{2,1,0:T(8,128)(2,1)S(1)}, bf16[64,128]{1,0:T(8,128)(2,1)S(1)}, bf16[64,128]{1,0:T(8,128)(2...) custom-call(bf16[2,1,1024,768]{3,2,1,0:T(8,128)(2,1)S(1)} %copy-done.3, ...), custom_call_target="tpu_custom_call" | custom-call | flops 1000000000 | bytes 1048576 | tf_op jit(solution)/shard_map/local_solve/pallas_call | solution.py:386
  9.5 1.8 %collective-permute-done.3.got_ref.rest_0_ = bf16[288,128]{1,0:T(8,128)(2,1)S(1)} collective-permute-done((bf16[288,128]{1,0:T(8,128)(2,1)S(1)}, bf16[288,128]{1,0:T(8,128)(2,1)S(1)}, u32[]{:S(2)}, u32[]{:S(2)}) %collective-permute-start.3) | collective-permute-done | bytes 73760 | tf_op jit(solution)/shard_map/ppermute | solution.py:29
  11.4 1.6 %collective-permute-start.4 = (bf16[272,128]{1,0:T(8,128)(2,1)S(1)}, bf16[272,128]{1,0:T(8,128)(2,1)S(1)}, u32[]{:S(2)}, u32[]{:S(2)}) collective-permute-start(bf16[272,128]{1,0:T(8,128)(2,1)S(1)} %get-tuple-element.43), channel_id=1, source_target_pairs={{0,1},{1,0},{2,3},{3,2},{4,5},{5,4},{6,7},{7,6},{8,9},{9,8},{10,11... | collective-permute-start | bytes 208904 | tf_op jit(solution)/shard_map/ppermute | solution.py:29
  12.9 1.6 %collective-permute-start.2 = (bf16[64,1024]{1,0:T(8,128)(2,1)S(1)}, bf16[64,1024]{1,0:T(8,128)(2,1)S(1)}, u32[]{:S(2)}, u32[]{:S(2)}) collective-permute-start(bf16[64,1024]{1,0:T(8,128)(2,1)S(1)} %inverse_join.2.near_ref), channel_id=1, source_target_pairs={{0,2},{1,3},{2,0},{3,1},{4,6},{5,7},{6,4},{7,5},{8,10},{9,11},{10,... | collective-permute-start | bytes 393224 | tf_op jit(solution)/shard_map/ppermute | solution.py:29
  14.6 1.2 %collective-permute-done.4.token_ref.got_ref.rest_0_ = bf16[272,128]{1,0:T(8,128)(2,1)S(1)} collective-permute-done((bf16[272,128]{1,0:T(8,128)(2,1)S(1)}, bf16[272,128]{1,0:T(8,128)(2,1)S(1)}, u32[]{:S(2)}, u32[]{:S(2)}) %collective-permute-start.4) | collective-permute-done | bytes 69664 | tf_op jit(solution)/shard_map/ppermute | solution.py:29
  15.8 1.3 %collective-permute-start.5 = (bf16[256,128]{1,0:T(8,128)(2,1)S(1)}, bf16[256,128]{1,0:T(8,128)(2,1)S(1)}, u32[]{:S(2)}, u32[]{:S(2)}) collective-permute-start(bf16[256,128]{1,0:T(8,128)(2,1)S(1)} %get-tuple-element.47), channel_id=1, source_target_pairs={{0,4},{1,5},{2,6},{3,7},{4,0},{5,1},{6,2},{7,3},{8,12},{9,13},{10,... | collective-permute-start | bytes 196616 | tf_op jit(solution)/shard_map/ppermute | solution.py:29
  17.1 1.6 %collective-permute-done.2.far_ref = bf16[64,1024]{1,0:T(8,128)(2,1)S(1)} collective-permute-done((bf16[64,1024]{1,0:T(8,128)(2,1)S(1)}, bf16[64,1024]{1,0:T(8,128)(2,1)S(1)}, u32[]{:S(2)}, u32[]{:S(2)}) %collective-permute-start.2) | collective-permute-done | bytes 131104 | tf_op jit(solution)/shard_map/ppermute | solution.py:29
  18.7 0.5 %inverse_pick.3 = bf16[640,128]{1,0:T(8,128)(2,1)S(1)} custom-call(bf16[128,1024]{1,0:T(8,128)(2,1)S(1)} %inverse_join.3.rows_ref, bf16[272,128]{1,0:T(8,128)(2,1)S(1)} %collective-permute-done.4.token_ref.got_ref.rest_0_, bf16[272,128]{1,0:T(8,128)(2,1)S(1)} %collective-permute-done.4.token_ref.got_ref.rest_0_, bf16[128,128]{1,0:T(8,128)(2,1)S(1)} %get-tuple-element.50.rest_1_), custom_call_target="tpu_custom_call" | custom-call | flops 1000000000 | bytes 1048576 | tf_op jit(solution)/shard_map/inverse_pick/pallas_call | solution.py:386
  19.2 0.1 collective-permute-start.6
  19.3 1.7 %collective-permute-done.5.got_ref = bf16[256,128]{1,0:T(8,128)(2,1)S(1)} collective-permute-done((bf16[256,128]{1,0:T(8,128)(2,1)S(1)}, bf16[256,128]{1,0:T(8,128)(2,1)S(1)}, u32[]{:S(2)}, u32[]{:S(2)}) %collective-permute-start.5) | collective-permute-done | bytes 65568 | tf_op jit(solution)/shard_map/ppermute | solution.py:29
  21.0 1.6 %collective-permute-start.7 = (bf16[256,128]{1,0:T(8,128)(2,1)S(1)}, bf16[256,128]{1,0:T(8,128)(2,1)S(1)}, u32[]{:S(2)}, u32[]{:S(2)}) collective-permute-start(bf16[256,128]{1,0:T(8,128)(2,1)S(1)} %get-tuple-element.49.token_ref), channel_id=1, source_target_pairs={{0,2},{1,3},{2,0},{3,1},{4,6},{5,7},{6,4},{7,5},{8,10},{9,11},{10,... | collective-permute-start | bytes 196616 | tf_op jit(solution)/shard_map/ppermute | solution.py:29
  22.7 0.5 %inverse_pick.2.near_ref = bf16[512,128]{1,0:T(8,128)(2,1)S(1)} custom-call(bf16[128,1024]{1,0:T(8,128)(2,1)S(1)} %inverse_join.3.rows_ref, bf16[256,128]{1,0:T(8,128)(2,1)S(1)} %get-tuple-element.49.token_ref, bf16[288,128]{1,0:T(8,128)(2,1)S(1)} %collective-permute-done.3.got_ref.rest_0_, bf16[528,128]{1,0:T(8,128)(2,1)S(1)} %get-tuple-element.39.sent_ref.rest_0_.rest_1_, ...), custom_call_target="tpu_custom_call" | custom-call | flops 1000000000 | bytes 1048576 | tf_op jit(solution)/shard_map/inverse_pick/pallas_call | solution.py:386
  23.2 2.2 %collective-permute-done.7.got_ref = bf16[256,128]{1,0:T(8,128)(2,1)S(1)} collective-permute-done((bf16[256,128]{1,0:T(8,128)(2,1)S(1)}, bf16[256,128]{1,0:T(8,128)(2,1)S(1)}, u32[]{:S(2)}, u32[]{:S(2)}) %collective-permute-start.7) | collective-permute-done | bytes 65568 | tf_op jit(solution)/shard_map/ppermute | solution.py:29
  25.4 0.2 coarse_solve.1
  25.6 0.1 collective-permute-start.8
  25.7 0.5 %collective-permute-start.9 = (bf16[128,128]{1,0:T(8,128)(2,1)S(1)}, bf16[128,128]{1,0:T(8,128)(2,1)S(1)}, u32[]{:S(2)}, u32[]{:S(2)}) collective-permute-start(bf16[128,128]{1,0:T(8,128)(2,1)S(1)} %get-tuple-element.60), channel_id=1, source_target_pairs={{0,8},{1,2},{2,1},{3,4},{4,3},{5,6},{6,5},{7,15},{8,0},{9,10},{10,... | collective-permute-start | bytes 98312 | tf_op jit(solution)/shard_map/ppermute | solution.py:45
  26.2 0.8 %collective-permute-done.8.got_ref.rest_0_ = bf16[320,128]{1,0:T(8,128)(2,1)S(1)} collective-permute-done((bf16[320,128]{1,0:T(8,128)(2,1)S(1)}, bf16[320,128]{1,0:T(8,128)(2,1)S(1)}, u32[]{:S(2)}, u32[]{:S(2)}) %collective-permute-start.8) | collective-permute-done | bytes 81952 | tf_op jit(solution)/shard_map/ppermute | solution.py:29
  27.0 1.3 %collective-permute-start.10 = (bf16[192,128]{1,0:T(8,128)(2,1)S(1)}, bf16[192,128]{1,0:T(8,128)(2,1)S(1)}, u32[]{:S(2)}, u32[]{:S(2)}) collective-permute-start(bf16[192,128]{1,0:T(8,128)(2,1)S(1)} %get-tuple-element.56.token_ref), channel_id=1, source_target_pairs={{0,24},{8,16},{16,8},{24,0},{1,25},{9,17},{17,9},{25,1},{2,26},{10... | collective-permute-start | bytes 147464 | tf_op jit(solution)/shard_map/ppermute | solution.py:29
  28.3 0.6 %local_spread.1 = (f32[2,768,128]{2,1,0:T(8,128)S(1)}, bf16[2,768,320]{2,1,0:T(8,128)(2,1)S(1)}) custom-call(f32[2,768,128]{2,1,0:T(8,128)S(1)} %get-tuple-element.41.token_ref.own_ref, s32[2,1,4,64]{3,2,1,0:T(4,128)S(1)} %copy-done.2, bf16[2,1,64,768]{3,2,1,0:T(8,128)(2,1)S(1)} %copy-done.4, bf16[192,128]{1,0:T(8,128)(2,1)S(1)} %get-tuple-element.56.token_ref, ...), custom_call_target="tpu_custom_call" | custom-call | flops 1000000000 | bytes 1048576 | tf_op jit(solution)/shard_map/local_spread/pallas_call | solution.py:386
  28.9 0.0 copy-start.1
  28.9 1.8 %collective-permute-done.10.rest_1_ = bf16[192,128]{1,0:T(8,128)(2,1)S(1)} collective-permute-done((bf16[192,128]{1,0:T(8,128)(2,1)S(1)}, bf16[192,128]{1,0:T(8,128)(2,1)S(1)}, u32[]{:S(2)}, u32[]{:S(2)}) %collective-permute-start.10) | collective-permute-done | bytes 49184 | tf_op jit(solution)/shard_map/ppermute | solution.py:29
  30.7 0.9 %correction.1 = (f32[2,768,128]{2,1,0:T(8,128)S(1)}, bf16[2,768,128]{2,1,0:T(8,128)(2,1)S(1)}, bf16[2,256,128]{2,1,0:T(8,128)(2,1)S(1)}, bf16[64,128]{1,0:T(8,12...) custom-call(f32[2,768,128]{2,1,0:T(8,128)S(1)} %get-tuple-element.57.local_ref,, ...), custom_call_target="tpu_custom_call" | custom-call | flops 1000000000 | bytes 1048576 | tf_op jit(solution)/shard_map/correction/pallas_call | solution.py:386
  31.7 1.9 %collective-permute-start.13 = (bf16[128,128]{1,0:T(8,128)(2,1)S(1)}, bf16[128,128]{1,0:T(8,128)(2,1)S(1)}, u32[]{:S(2)}, u32[]{:S(2)}) collective-permute-start(bf16[128,128]{1,0:T(8,128)(2,1)S(1)} %get-tuple-element.70), channel_id=1, source_target_pairs={{0,1},{1,0},{2,3},{3,2},{4,5},{5,4},{6,7},{7,6},{8,9},{9,8},{10,11... | collective-permute-start | bytes 98312 | tf_op jit(solution)/shard_map/ppermute | solution.py:29
  33.5 0.5 %collective-permute-start.11 = (bf16[64,128]{1,0:T(8,128)(2,1)S(1)}, bf16[64,128]{1,0:T(8,128)(2,1)S(1)}, u32[]{:S(2)}, u32[]{:S(2)}) collective-permute-start(bf16[64,128]{1,0:T(8,128)(2,1)S(1)} %get-tuple-element.68), channel_id=1, source_target_pairs={{0,8},{8,0},{16,24},{24,16},{1,9},{9,1},{17,25},{25,17},{2,10},{10... | collective-permute-start | bytes 49160 | tf_op jit(solution)/shard_map/ppermute | solution.py:29
  34.0 1.1 %collective-permute-start.12 = (bf16[64,128]{1,0:T(8,128)(2,1)S(1)}, bf16[64,128]{1,0:T(8,128)(2,1)S(1)}, u32[]{:S(2)}, u32[]{:S(2)}) collective-permute-start(bf16[64,128]{1,0:T(8,128)(2,1)S(1)} %get-tuple-element.69), channel_id=1, source_target_pairs={{0,24},{1,25},{2,26},{3,27},{4,28},{5,29},{6,30},{7,31},{8,16},{9,... | collective-permute-start | bytes 49160 | tf_op jit(solution)/shard_map/ppermute | solution.py:45
  35.2 1.1 %image_own.1 = (f32[2,768,128]{2,1,0:T(8,128)S(1)}, bf16[2,768,256]{2,1,0:T(8,128)(2,1)S(1)}, f32[2,1,768,128]{3,2,1,0:T(8,128)}) custom-call(bf16[2,1,1024,768]{3,2,1,0:T(8,128)(2,1)S(1)} %copy-done, bf16[2,768,128]{2,1,0:T(8,128)(2,1)S(1)} %get-tuple-element.62.low_ref, f32[2,1,768,128]{3,2,1,0:T(8,128)S(1)} %copy-done.1, ...), custom_call_target="tpu_custom_call" | custom-call | flops 1 | bytes 1048576 | tf_op jit(solution)/shard_map/image_own/pallas_call | solution.py:386
  36.3 0.9 %collective-permute-done.12.xo_ref = bf16[64,128]{1,0:T(8,128)(2,1)S(1)} collective-permute-done((bf16[64,128]{1,0:T(8,128)(2,1)S(1)}, bf16[64,128]{1,0:T(8,128)(2,1)S(1)}, u32[]{:S(2)}, u32[]{:S(2)}) %collective-permute-start.12) | collective-permute-done | bytes 16416 | tf_op jit(solution)/shard_map/ppermute | solution.py:45
  37.2 1.2 %residual.1 = f32[2,1,768,128]{3,2,1,0:T(8,128)} custom-call(f32[2,768,128]{2,1,0:T(8,128)S(1)} %get-tuple-element.65.part_ref, bf16[2,256,128]{2,1,0:T(8,128)(2,1)S(1)} %get-tuple-element.66.image_ref, bf16[2,768,256]{2,1,0:T(8,128)(2,1)S(1)} %get-tuple-element.67.pick_ref, bf16[64,128]{1,0:T(8,128)(2,1)S(1)} %collective-permute-done.11.xp_ref, ...), custom_call_target="tpu_custom_call" | custom-call | flops 1000000000 | bytes 1048576 | tf_op jit(solution)/shard_map/residual/pallas_call | solution.py:386
  (26 shorter events, 0.2 us)
Async XLA Ops:
  0.6 2.6 %copy-start.5 = (bf16[32,1024]{1,0:T(8,128)(2,1)S(1)}, bf16[32,1024]{1,0:T(8,128)(2,1)}, u32[]{:S(2)}) copy-start(bf16[32,1024]{1,0:T(8,128)(2,1)} %near_ref.1) | copy-start | bytes 196612
  0.6 7.9 %copy-start.3 = (bf16[2,1,1024,768]{3,2,1,0:T(8,128)(2,1)S(1)}, bf16[2,1,1024,768]{3,2,1,0:T(8,128)(2,1)}, u32[]{:S(2)}) copy-start(bf16[2,1,1024,768]{3,2,1,0:T(8,128)(2,1)} %inverse_ref.1) | copy-start | bytes 9437188
  2.7 4.2 %collective-permute-start = (bf16[528,128]{1,0:T(8,128)(2,1)S(1)}, bf16[528,128]{1,0:T(8,128)(2,1)S(1)}, u32[]{:S(2)}, u32[]{:S(2)}) collective-permute-start(bf16[528,128]{1,0:T(8,128)(2,1)S(1)} %get-tuple-element.39.sent_ref.rest_0_.rest_1_), channel_id=1, source_target_pairs={{0,8},{8,0},{16,24},{24,16},{1,9},{9,1},{17,25},{25,17},{2,10},{10... | collective-permute-start | bytes 405512 | tf_op jit(solution)/shard_map/ppermute | solution.py:29
  3.2 9.7 %collective-permute-start.1 = (bf16[32,1024]{1,0:T(8,128)(2,1)S(1)}, bf16[32,1024]{1,0:T(8,128)(2,1)S(1)}, u32[]{:S(2)}, u32[]{:S(2)}) collective-permute-start(bf16[32,1024]{1,0:T(8,128)(2,1)S(1)} %copy-done.5), channel_id=1, source_target_pairs={{0,4},{1,5},{2,6},{3,7},{4,0},{5,1},{6,2},{7,3},{8,12},{9,13},{10,... | collective-permute-start | bytes 196616 | tf_op jit(solution)/shard_map/ppermute | solution.py:29
  6.9 4.4 %collective-permute-start.3 = (bf16[288,128]{1,0:T(8,128)(2,1)S(1)}, bf16[288,128]{1,0:T(8,128)(2,1)S(1)}, u32[]{:S(2)}, u32[]{:S(2)}) collective-permute-start(bf16[288,128]{1,0:T(8,128)(2,1)S(1)} %get-tuple-element.40.token_ref), channel_id=1, source_target_pairs={{0,16},{8,24},{16,0},{24,8},{1,17},{9,25},{17,1},{25,9},{2,18},{10... | collective-permute-start | bytes 221192 | tf_op jit(solution)/shard_map/ppermute | solution.py:29
  11.4 4.4 %collective-permute-start.4 = (bf16[272,128]{1,0:T(8,128)(2,1)S(1)}, bf16[272,128]{1,0:T(8,128)(2,1)S(1)}, u32[]{:S(2)}, u32[]{:S(2)}) collective-permute-start(bf16[272,128]{1,0:T(8,128)(2,1)S(1)} %get-tuple-element.43), channel_id=1, source_target_pairs={{0,1},{1,0},{2,3},{3,2},{4,5},{5,4},{6,7},{7,6},{8,9},{9,8},{10,11... | collective-permute-start | bytes 208904 | tf_op jit(solution)/shard_map/ppermute | solution.py:29
  12.9 5.7 %collective-permute-start.2 = (bf16[64,1024]{1,0:T(8,128)(2,1)S(1)}, bf16[64,1024]{1,0:T(8,128)(2,1)S(1)}, u32[]{:S(2)}, u32[]{:S(2)}) collective-permute-start(bf16[64,1024]{1,0:T(8,128)(2,1)S(1)} %inverse_join.2.near_ref), channel_id=1, source_target_pairs={{0,2},{1,3},{2,0},{3,1},{4,6},{5,7},{6,4},{7,5},{8,10},{9,11},{10,... | collective-permute-start | bytes 393224 | tf_op jit(solution)/shard_map/ppermute | solution.py:29
  15.8 5.2 %collective-permute-start.5 = (bf16[256,128]{1,0:T(8,128)(2,1)S(1)}, bf16[256,128]{1,0:T(8,128)(2,1)S(1)}, u32[]{:S(2)}, u32[]{:S(2)}) collective-permute-start(bf16[256,128]{1,0:T(8,128)(2,1)S(1)} %get-tuple-element.47), channel_id=1, source_target_pairs={{0,4},{1,5},{2,6},{3,7},{4,0},{5,1},{6,2},{7,3},{8,12},{9,13},{10,... | collective-permute-start | bytes 196616 | tf_op jit(solution)/shard_map/ppermute | solution.py:29
  19.2 6.2 %collective-permute-start.6 = (bf16[640,128]{1,0:T(8,128)(2,1)S(1)}, bf16[640,128]{1,0:T(8,128)(2,1)S(1)}, u32[]{:S(2)}, u32[]{:S(2)}) collective-permute-start(bf16[640,128]{1,0:T(8,128)(2,1)S(1)} %inverse_pick.3), channel_id=1, source_target_pairs={{0,1},{1,0},{2,3},{3,2},{4,5},{5,4},{6,7},{7,6},{8,9},{9,8},{10,11... | collective-permute-start | bytes 491528 | tf_op jit(solution)/shard_map/ppermute | solution.py:29
  21.0 4.3 %collective-permute-start.7 = (bf16[256,128]{1,0:T(8,128)(2,1)S(1)}, bf16[256,128]{1,0:T(8,128)(2,1)S(1)}, u32[]{:S(2)}, u32[]{:S(2)}) collective-permute-start(bf16[256,128]{1,0:T(8,128)(2,1)S(1)} %get-tuple-element.49.token_ref), channel_id=1, source_target_pairs={{0,2},{1,3},{2,0},{3,1},{4,6},{5,7},{6,4},{7,5},{8,10},{9,11},{10,... | collective-permute-start | bytes 196616 | tf_op jit(solution)/shard_map/ppermute | solution.py:29
  25.4 3.0 %copy-start.2 = (s32[2,1,4,64]{3,2,1,0:T(4,128)S(1)}, s32[2,1,4,64]{3,2,1,0:T(4,128)}, u32[]{:S(2)}) copy-start(s32[2,1,4,64]{3,2,1,0:T(4,128)} %spill_ref.3) | copy-start | bytes 6148
  25.4 3.0 %copy-start.4 = (bf16[2,1,64,768]{3,2,1,0:T(8,128)(2,1)S(1)}, bf16[2,1,64,768]{3,2,1,0:T(8,128)(2,1)}, u32[]{:S(2)}) copy-start(bf16[2,1,64,768]{3,2,1,0:T(8,128)(2,1)} %basis_ref.1) | copy-start | bytes 589828
  25.6 1.3 %collective-permute-start.8 = (bf16[320,128]{1,0:T(8,128)(2,1)S(1)}, bf16[320,128]{1,0:T(8,128)(2,1)S(1)}, u32[]{:S(2)}, u32[]{:S(2)}) collective-permute-start(bf16[320,128]{1,0:T(8,128)(2,1)S(1)} %get-tuple-element.54), channel_id=1, source_target_pairs={{0,8},{8,0},{16,24},{24,16},{1,9},{9,1},{17,25},{25,17},{2,10},{10... | collective-permute-start | bytes 245768 | tf_op jit(solution)/shard_map/ppermute | solution.py:29
  25.7 3.2 %collective-permute-start.9 = (bf16[128,128]{1,0:T(8,128)(2,1)S(1)}, bf16[128,128]{1,0:T(8,128)(2,1)S(1)}, u32[]{:S(2)}, u32[]{:S(2)}) collective-permute-start(bf16[128,128]{1,0:T(8,128)(2,1)S(1)} %get-tuple-element.60), channel_id=1, source_target_pairs={{0,8},{1,2},{2,1},{3,4},{4,3},{5,6},{6,5},{7,15},{8,0},{9,10},{10,... | collective-permute-start | bytes 98312 | tf_op jit(solution)/shard_map/ppermute | solution.py:45
  27.0 3.8 %copy-start = (bf16[2,1,1024,768]{3,2,1,0:T(8,128)(2,1)S(1)}, bf16[2,1,1024,768]{3,2,1,0:T(8,128)(2,1)}, u32[]{:S(2)}) copy-start(bf16[2,1,1024,768]{3,2,1,0:T(8,128)(2,1)} %operator_ref.3) | copy-start | bytes 9437188
  27.0 3.8 %collective-permute-start.10 = (bf16[192,128]{1,0:T(8,128)(2,1)S(1)}, bf16[192,128]{1,0:T(8,128)(2,1)S(1)}, u32[]{:S(2)}, u32[]{:S(2)}) collective-permute-start(bf16[192,128]{1,0:T(8,128)(2,1)S(1)} %get-tuple-element.56.token_ref), channel_id=1, source_target_pairs={{0,24},{8,16},{16,8},{24,0},{1,25},{9,17},{17,9},{25,1},{2,26},{10... | collective-permute-start | bytes 147464 | tf_op jit(solution)/shard_map/ppermute | solution.py:29
  28.9 6.3 %copy-start.1 = (f32[2,1,768,128]{3,2,1,0:T(8,128)S(1)}, f32[2,1,768,128]{3,2,1,0:T(8,128)}, u32[]{:S(2)}) copy-start(f32[2,1,768,128]{3,2,1,0:T(8,128)} %rhs_ref.1) | copy-start | bytes 2359300
  31.7 5.6 %collective-permute-start.13 = (bf16[128,128]{1,0:T(8,128)(2,1)S(1)}, bf16[128,128]{1,0:T(8,128)(2,1)S(1)}, u32[]{:S(2)}, u32[]{:S(2)}) collective-permute-start(bf16[128,128]{1,0:T(8,128)(2,1)S(1)} %get-tuple-element.70), channel_id=1, source_target_pairs={{0,1},{1,0},{2,3},{3,2},{4,5},{5,4},{6,7},{7,6},{8,9},{9,8},{10,11... | collective-permute-start | bytes 98312 | tf_op jit(solution)/shard_map/ppermute | solution.py:29
  33.5 3.7 %collective-permute-start.14 = (bf16[128,128]{1,0:T(8,128)(2,1)S(1)}, bf16[128,128]{1,0:T(8,128)(2,1)S(1)}, u32[]{:S(2)}, u32[]{:S(2)}) collective-permute-start(bf16[128,128]{1,0:T(8,128)(2,1)S(1)} %get-tuple-element.71), channel_id=1, source_target_pairs={{0,8},{1,2},{2,1},{3,4},{4,3},{5,6},{6,5},{7,15},{8,0},{9,10},{10,... | collective-permute-start | bytes 98312 | tf_op jit(solution)/shard_map/ppermute | solution.py:45
  33.5 2.7 %collective-permute-start.11 = (bf16[64,128]{1,0:T(8,128)(2,1)S(1)}, bf16[64,128]{1,0:T(8,128)(2,1)S(1)}, u32[]{:S(2)}, u32[]{:S(2)}) collective-permute-start(bf16[64,128]{1,0:T(8,128)(2,1)S(1)} %get-tuple-element.68), channel_id=1, source_target_pairs={{0,8},{8,0},{16,24},{24,16},{1,9},{9,1},{17,25},{25,17},{2,10},{10... | collective-permute-start | bytes 49160 | tf_op jit(solution)/shard_map/ppermute | solution.py:29
  34.0 3.2 %collective-permute-start.12 = (bf16[64,128]{1,0:T(8,128)(2,1)S(1)}, bf16[64,128]{1,0:T(8,128)(2,1)S(1)}, u32[]{:S(2)}, u32[]{:S(2)}) collective-permute-start(bf16[64,128]{1,0:T(8,128)(2,1)S(1)} %get-tuple-element.69), channel_id=1, source_target_pairs={{0,24},{1,25},{2,26},{3,27},{4,28},{5,29},{6,30},{7,31},{8,16},{9,... | collective-permute-start | bytes 49160 | tf_op jit(solution)/shard_map/ppermute | solution.py:45
